TPU v7x, 32 devices: a whole 2x2x4 slice. The times are simulated.
32 devices in a mesh: dp: 8 (over z, x), tensor: 4 (over y, core).
Axes of the slice: x: 2, y: 2, z: 4, core: 2. Of those that a mesh axis runs over, the one named last changes fastest.
Arguments:
- tokens: bfloat16 [32768, 768], P(('dp', 'tensor')), may hold values from -6 to 6
- qkv_weight: bfloat16 [3, 768, 768], replicated, may hold values from -0.21875 to 0.21875
- out_weight: bfloat16 [768, 768], replicated, may hold values from -0.625 to 0.625
- in_weight: bfloat16 [768, 3072], P(None, 'tensor'), may hold values from -0.21875 to 0.21875
- back_weight: bfloat16 [3072, 768], P('tensor'), may hold values from -0.109375 to 0.109375
- rel_embed: bfloat16 [512, 768], replicated, may hold values from -6 to 6
- gain_one: float32 [768], replicated, may hold values from 0.5 to 1.5
- shift_one: float32 [768], replicated, may hold values from -1 to 1
- gain_two: float32 [768], replicated, may hold values from 0.5 to 1.5
- shift_two: float32 [768], replicated, may hold values from -1 to 1
- adapt_down: bfloat16 [5, 12, 768], replicated, may hold values from -0.21875 to 0.21875
- adapt_up: bfloat16 [5, 12, 768], replicated, may hold values from -1.75 to 1.75
- hidden_up: bfloat16 [12, 3072], P(None, 'tensor'), may hold values from -1.75 to 1.75
- hidden_down: bfloat16 [12, 3072], P(None, 'tensor'), may hold values from -0.109375 to 0.109375
- adapt_scale: float32 [6, 12], replicated, may hold values from -3 to 3
- seq_lengths: int32 [32, 4], P(('dp', 'tensor')), may hold values from 65 to 512, as said below
- seq_counts: int32 [32, 3], P(('dp', 'tensor')), may hold values from 0 to 2, as said below
- rel_bucket: int32 [1023], replicated, may hold values from 1 to 511, as said below
- out_grad: bfloat16 [32768, 768], P(('dp', 'tensor')), may hold values from -6 to 6
Outputs:
- mixed: bfloat16 [32768, 768], P(('dp', 'tensor'))
- in_grad: float32 [32768, 768], P(('dp', 'tensor'))
- down_grad: float32 [5, 12, 768], replicated
- up_grad: float32 [5, 12, 768], replicated
- hidden_up_grad: float32 [12, 3072], P(None, 'tensor')
- hidden_down_grad: float32 [12, 3072], P(None, 'tensor')
- scale_grad: float32 [6, 12], replicated
Inputs may be any that keep to these rules, and one draw needn't show every extreme that they name: `seq_lengths`: column s of row g is the length of slot s of row group g; a slot of 128, 256 or 512 rows has a length from half its rows plus one to its rows; in every draw some row group has all its slots full. `seq_counts`: column b of row g counts the used slots of bucket b (2 slots of 128 rows, 1 of 256, 1 of 512) in row group g; the used slots are the first of their bucket in row order; column 0 is 1 or more; in every draw some row group uses all its slots. `rel_bucket`: entry 511 + d is the bucket of relative position d: 256 + sign(d) m(|d|), where m never decreases, m(0) = 0 and m(|d|) = |d| for |d| up to 64.
All inputs are finite; a program needn't handle non-finite values.
Results may differ from a plain program's by a relative error of at most 0.018.
Values may be sent and summed in bfloat16 or wider, within the bound.
A program may use at most 256 MiB of HBM per device.

v0:
```python
from functools import partial

import jax
import jax.numpy as jnp
from jax import lax
from jax.sharding import PartitionSpec as P

D = 768
H = 12
DH = 64
SPAN = 256
LEN1 = 128
LEN3 = 512


norm_epsilon = 1e-07
masked_score = -1e30
topmost_precision = lax.Precision.HIGHEST


def row_layout(row_count, lengths, counts):
    row_index = jnp.arange(row_count, dtype=jnp.int32)
    group_id = row_index // (2 * LEN3)
    within_set = row_index % (2 * LEN3)
    second = within_set >= LEN3
    inner_row = within_set % LEN3
    first_slot = jnp.minimum(inner_row // LEN1, 2)
    slot_kind = jnp.where(second, 3, first_slot)
    position = inner_row - jnp.where(second, 0, first_slot * LEN1)
    slot_id = group_id * 4 + slot_kind
    bucket = jnp.maximum(slot_kind - 1, 0)
    bucket_rank = jnp.where(slot_kind < 2, 2 * group_id + slot_kind, group_id)
    used_slots = jnp.sum(
        jnp.where(bucket[:, None] == jnp.arange(3, dtype=jnp.int32)[None, :], counts[None, :], 0),
        axis=1,
    )
    slot_length = jnp.sum(
        jnp.where(
            slot_id[:, None] == jnp.arange(lengths.shape[0], dtype=jnp.int32)[None, :],
            lengths[None, :],
            0,
        ),
        axis=1,
    )
    is_live = (bucket_rank < used_slots) & (position < slot_length)
    return (slot_id, position, is_live)


def adapter_forward(inputs, weight, downward, upward, scaling):
    coefficient = jnp.dot(inputs, downward.T, preferred_element_type=jnp.float32)
    output = jnp.dot(inputs, weight, preferred_element_type=jnp.float32)
    output = output + jnp.dot(
        coefficient * scaling, upward.astype(jnp.float32), precision=topmost_precision
    )
    return (output, coefficient)


def adapter_grads(grad_out, inputs, upward, scaling, coefficient):
    up_grad = jnp.dot(
        (coefficient * scaling).T, grad_out.astype(jnp.float32), precision=topmost_precision
    )
    slope = jnp.dot(grad_out, upward.T, preferred_element_type=jnp.float32)
    scale_grad = jnp.sum(coefficient * slope, axis=0)
    through = slope * scaling
    down_grad = jnp.dot(through.T, inputs.astype(jnp.float32), precision=topmost_precision)
    return (down_grad, up_grad, scale_grad, through)


def input_grad(grad_out, weight, downward, through):
    return jnp.dot(grad_out, weight.T, preferred_element_type=jnp.float32) + jnp.dot(
        through, downward.astype(jnp.float32), precision=topmost_precision
    )


def norm_forward(values, norm_gain, norm_shift):
    centered = values - jnp.mean(values, axis=1, keepdims=True)
    inverse = lax.rsqrt(jnp.mean(centered * centered, axis=1, keepdims=True) + norm_epsilon)
    normal = centered * inverse
    return (normal * norm_gain + norm_shift, normal, inverse)


def norm_backward(grad_out, normal, inverse, norm_gain):
    scaled = grad_out * norm_gain
    return inverse * (
        scaled
        - jnp.mean(scaled, axis=1, keepdims=True)
        - normal * jnp.mean(scaled * normal, axis=1, keepdims=True)
    )


def take_pair(source, start_row, start_col):
    return lax.dynamic_slice(source, (start_row, start_col), (LEN3, 2 * DH)).reshape(LEN3, 2, DH)


def rel_shift(offset_table):
    heads = offset_table.shape[0]
    flat = offset_table.reshape(heads, LEN3 * 2 * LEN3)
    window = flat[:, LEN3 - 1 : LEN3 - 1 + LEN3 * (2 * LEN3 - 1)]
    return window.reshape(heads, LEN3, 2 * LEN3 - 1)[:, :, :LEN3]


def pair_scores(query_per_head, head_key, offset_key_rows, offset_query_rows, allowed):
    content = jnp.einsum(
        "ihd,jhd->hij", query_per_head, head_key, preferred_element_type=jnp.float32
    )
    target_table = jnp.einsum(
        "ihd,khd->hik", query_per_head, offset_key_rows, preferred_element_type=jnp.float32
    )
    source_table = jnp.einsum(
        "jhd,khd->hjk", head_key, offset_query_rows, preferred_element_type=jnp.float32
    )
    relative = rel_shift(target_table) + jnp.swapaxes(rel_shift(source_table), 1, 2)
    return jnp.where(allowed[None], (content + relative) * (3.0 * DH) ** (-0.5), masked_score)


def share(downward, upward, scaling):
    return lax.psum((downward, upward, scaling), ("dp", "tensor"))


def on_device(
    tokens,
    qkv_weight,
    out_weight,
    in_weight,
    back_weight,
    rel_embed,
    gain_one,
    shift_one,
    gain_two,
    shift_two,
    adapt_down,
    adapt_up,
    hidden_up,
    hidden_down,
    adapt_scale,
    seq_lengths,
    seq_counts,
    rel_bucket,
    out_grad,
):
    row_count = tokens.shape[0]
    slot_id, position, is_live = row_layout(row_count, seq_lengths[0], seq_counts[0])
    live_rows = is_live.astype(jnp.float32)[:, None]
    query_full, query_coeff = adapter_forward(
        tokens, qkv_weight[0], adapt_down[0], adapt_up[0], adapt_scale[0]
    )
    key_full, key_coeff = adapter_forward(
        tokens, qkv_weight[1], adapt_down[1], adapt_up[1], adapt_scale[1]
    )
    value_full, value_coeff = adapter_forward(
        tokens, qkv_weight[2], adapt_down[2], adapt_up[2], adapt_scale[2]
    )
    rel_key_full, rel_key_coeff = adapter_forward(
        rel_embed, qkv_weight[1], adapt_down[1], adapt_up[1], adapt_scale[1]
    )
    rel_query_full, rel_query_coeff = adapter_forward(
        rel_embed, qkv_weight[0], adapt_down[0], adapt_up[0], adapt_scale[0]
    )
    queries = query_full.astype(jnp.bfloat16)
    every_key_rows = key_full.astype(jnp.bfloat16)
    values_all = value_full.astype(jnp.bfloat16)
    pos_key = rel_key_full.astype(jnp.bfloat16)
    pos_query = rel_query_full.astype(jnp.bfloat16)
    offset_index = jnp.clip(2 * LEN3 - 2 - jnp.arange(2 * LEN3, dtype=jnp.int32), 0, 2 * LEN3 - 2)
    offset_bucket = rel_bucket[offset_index]
    key_by_offset = pos_key[offset_bucket]
    query_by_offset = pos_query[offset_bucket]
    pairs = H // 2
    pieces = row_count // LEN3 * pairs

    def pair_inputs(number):
        start_row = number // pairs * LEN3
        start_col = number % pairs * (2 * DH)
        offset_key_rows = lax.dynamic_slice_in_dim(key_by_offset, start_col, 2 * DH, 1).reshape(
            2 * LEN3, 2, DH
        )
        offset_query_rows = lax.dynamic_slice_in_dim(query_by_offset, start_col, 2 * DH, 1).reshape(
            2 * LEN3, 2, DH
        )
        block_slot = lax.dynamic_slice_in_dim(slot_id, start_row, LEN3)
        block_live = lax.dynamic_slice_in_dim(is_live, start_row, LEN3)
        allowed = (block_slot[:, None] == block_slot[None, :]) & block_live[None, :]
        query_per_head = take_pair(queries, start_row, start_col)
        head_key = take_pair(every_key_rows, start_row, start_col)
        head_value = take_pair(values_all, start_row, start_col)
        return (
            query_per_head,
            head_key,
            head_value,
            offset_key_rows,
            offset_query_rows,
            allowed,
            start_row,
            start_col,
        )

    def forward_piece(number, carried):
        context_all, lse_all = carried
        (
            query_per_head,
            head_key,
            head_value,
            offset_key_rows,
            offset_query_rows,
            allowed,
            start_row,
            start_col,
        ) = pair_inputs(number)
        scores = pair_scores(query_per_head, head_key, offset_key_rows, offset_query_rows, allowed)
        row_max = jnp.max(scores, axis=2, keepdims=True)
        weights = jnp.exp(scores - row_max)
        row_total = jnp.sum(weights, axis=2, keepdims=True)
        prob_low = (weights / row_total).astype(jnp.bfloat16)
        context = jnp.einsum(
            "hij,jhd->ihd", prob_low, head_value, preferred_element_type=jnp.float32
        ).reshape(LEN3, 2 * DH)
        context_all = lax.dynamic_update_slice(context_all, context, (start_row, start_col))
        lse_all = lax.dynamic_update_slice(
            lse_all, (row_max + jnp.log(row_total))[:, :, 0], (start_col // DH, start_row)
        )
        return (context_all, lse_all)

    context_all, lse_all = lax.fori_loop(
        0,
        pieces,
        forward_piece,
        (jnp.zeros((row_count, D), jnp.float32), jnp.zeros((H, row_count), jnp.float32)),
    )
    context_low = context_all.astype(jnp.bfloat16)
    attended, out_coeff = adapter_forward(
        context_low, out_weight, adapt_down[3], adapt_up[3], adapt_scale[3]
    )
    normed, normal_one, inverse_one = norm_forward(
        tokens.astype(jnp.float32) + attended, gain_one, shift_one
    )
    normed_low = normed.astype(jnp.bfloat16)
    ffn_in_weight, ffn_out_weight, ffn_up_factor, ffn_down_factor = (
        in_weight,
        back_weight,
        hidden_up,
        hidden_down,
    )
    ffn_rows = lax.all_gather(normed_low, "tensor", axis=0, tiled=True)
    hidden, in_coeff = adapter_forward(
        ffn_rows, ffn_in_weight, adapt_down[4], ffn_up_factor, adapt_scale[4]
    )
    active = jax.nn.gelu(hidden, approximate=False).astype(jnp.bfloat16)
    back_coeff = jnp.dot(active, ffn_down_factor.T, preferred_element_type=jnp.float32)
    active_rows = active
    coeff_rows = back_coeff
    mlp_out = lax.psum_scatter(
        (
            jnp.dot(active_rows, back_weight, preferred_element_type=jnp.float32)
            + jnp.dot(
                coeff_rows * adapt_scale[5],
                adapt_up[4].astype(jnp.float32),
                precision=topmost_precision,
            )
        ).astype(jnp.bfloat16),
        "tensor",
        scatter_dimension=0,
        tiled=True,
    ).astype(jnp.float32)
    result, normal_two, inverse_two = norm_forward(normed + mlp_out, gain_two, shift_two)
    mixed = (result * live_rows).astype(jnp.bfloat16)
    grad_sum_two = norm_backward(
        out_grad.astype(jnp.float32) * live_rows, normal_two, inverse_two, gain_two
    )
    grad_mlp = grad_sum_two.astype(jnp.bfloat16)
    grad_rows = lax.all_gather(grad_mlp, "tensor", axis=0, tiled=True)
    ffn_rows = lax.all_gather(normed_low, "tensor", axis=0, tiled=True)
    hidden, in_coeff = adapter_forward(
        ffn_rows, in_weight, adapt_down[4], hidden_up, adapt_scale[4]
    )
    active = jax.nn.gelu(hidden, approximate=False).astype(jnp.bfloat16)
    back_coeff = jnp.dot(active, hidden_down.T, preferred_element_type=jnp.float32)
    hid_down_grad, up_ffn_grad, scale_back_grad, through_back = adapter_grads(
        grad_rows, active, adapt_up[4], adapt_scale[5], back_coeff
    )
    grad_active = input_grad(grad_rows, ffn_out_weight, ffn_down_factor, through_back)
    unused, gelu_back = jax.vjp(partial(jax.nn.gelu, approximate=False), hidden)
    grad_hidden = gelu_back(grad_active)[0].astype(jnp.bfloat16)
    down_ffn_grad, hid_up_grad, scale_in_grad, through_in = adapter_grads(
        grad_hidden, ffn_rows, ffn_up_factor, adapt_scale[4], in_coeff
    )
    grad_from_ffn = lax.psum_scatter(
        input_grad(grad_hidden, in_weight, adapt_down[4], through_in).astype(jnp.bfloat16),
        "tensor",
        scatter_dimension=0,
        tiled=True,
    ).astype(jnp.float32)
    ffn_scale_grad = jnp.stack([scale_in_grad, scale_back_grad])
    hid_up_grad, hid_down_grad = lax.psum((hid_up_grad, hid_down_grad), "dp")
    down_ffn_grad, up_ffn_grad, ffn_scale_grad = share(down_ffn_grad, up_ffn_grad, ffn_scale_grad)
    grad_sum_one = norm_backward(grad_sum_two + grad_from_ffn, normal_one, inverse_one, gain_one)
    grad_attended = grad_sum_one.astype(jnp.bfloat16)
    out_down_grad, out_up_grad, out_scale_grad, through_out = adapter_grads(
        grad_attended, context_low, adapt_up[3], adapt_scale[3], out_coeff
    )
    context_grad = input_grad(grad_attended, out_weight, adapt_down[3], through_out).astype(
        jnp.bfloat16
    )
    out_down_grad, out_up_grad, out_scale_grad = share(out_down_grad, out_up_grad, out_scale_grad)
    unused, shift_back = jax.vjp(rel_shift, jnp.zeros((2, LEN3, 2 * LEN3), jnp.float32))

    def backward_piece(number, carried):
        grad_query, grad_key, grad_value, grad_rel_key, grad_rel_query = carried
        (
            query_per_head,
            head_key,
            head_value,
            offset_key_rows,
            offset_query_rows,
            allowed,
            start_row,
            start_col,
        ) = pair_inputs(number)
        scores = pair_scores(query_per_head, head_key, offset_key_rows, offset_query_rows, allowed)
        row_lse = lax.dynamic_slice(lse_all, (start_col // DH, start_row), (2, LEN3))
        prob_full = jnp.exp(scores - row_lse[:, :, None])
        grad_pair = take_pair(context_grad, start_row, start_col)
        grad_prob = jnp.einsum(
            "ihd,jhd->hij", grad_pair, head_value, preferred_element_type=jnp.float32
        )
        grad_score = prob_full * (grad_prob - jnp.sum(prob_full * grad_prob, axis=2, keepdims=True))
        grad_raw = jnp.where(allowed[None], grad_score * (3.0 * DH) ** (-0.5), 0.0).astype(
            jnp.bfloat16
        )
        target_grad = shift_back(grad_raw.astype(jnp.float32))[0].astype(jnp.bfloat16)
        source_grad = shift_back(jnp.swapaxes(grad_raw, 1, 2).astype(jnp.float32))[0].astype(
            jnp.bfloat16
        )
        prob_low = prob_full.astype(jnp.bfloat16)
        new_query = jnp.einsum(
            "hij,jhd->ihd", grad_raw, head_key, preferred_element_type=jnp.float32
        ) + jnp.einsum(
            "hik,khd->ihd", target_grad, offset_key_rows, preferred_element_type=jnp.float32
        )
        new_key = jnp.einsum(
            "hij,ihd->jhd", grad_raw, query_per_head, preferred_element_type=jnp.float32
        ) + jnp.einsum(
            "hjk,khd->jhd", source_grad, offset_query_rows, preferred_element_type=jnp.float32
        )
        new_value = jnp.einsum(
            "hij,ihd->jhd", prob_low, grad_pair, preferred_element_type=jnp.float32
        )
        add_key = jnp.einsum(
            "hik,ihd->khd", target_grad, query_per_head, preferred_element_type=jnp.float32
        ).reshape(2 * LEN3, 2 * DH)
        add_query = jnp.einsum(
            "hjk,jhd->khd", source_grad, head_key, preferred_element_type=jnp.float32
        ).reshape(2 * LEN3, 2 * DH)
        grad_query = lax.dynamic_update_slice(
            grad_query, new_query.reshape(LEN3, 2 * DH), (start_row, start_col)
        )
        grad_key = lax.dynamic_update_slice(
            grad_key, new_key.reshape(LEN3, 2 * DH), (start_row, start_col)
        )
        grad_value = lax.dynamic_update_slice(
            grad_value, new_value.reshape(LEN3, 2 * DH), (start_row, start_col)
        )
        old_key = lax.dynamic_slice(grad_rel_key, (0, start_col), (2 * LEN3, 2 * DH))
        old_query = lax.dynamic_slice(grad_rel_query, (0, start_col), (2 * LEN3, 2 * DH))
        grad_rel_key = lax.dynamic_update_slice(grad_rel_key, old_key + add_key, (0, start_col))
        grad_rel_query = lax.dynamic_update_slice(
            grad_rel_query, old_query + add_query, (0, start_col)
        )
        return (grad_query, grad_key, grad_value, grad_rel_key, grad_rel_query)

    zero_rows = jnp.zeros((row_count, D), jnp.float32)
    zero_offsets = jnp.zeros((2 * LEN3, D), jnp.float32)
    grad_query, grad_key, grad_value, offset_key_grad, offset_query_grad = lax.fori_loop(
        0, pieces, backward_piece, (zero_rows, zero_rows, zero_rows, zero_offsets, zero_offsets)
    )
    offset_live = jnp.arange(2 * LEN3, dtype=jnp.int32) < 2 * LEN3 - 1
    fold_table = (
        (offset_bucket[None, :] == jnp.arange(2 * SPAN, dtype=jnp.int32)[:, None])
        & offset_live[None, :]
    ).astype(jnp.float32)
    grad_rel_key = jnp.dot(fold_table, offset_key_grad, precision=topmost_precision)
    grad_rel_query = jnp.dot(fold_table, offset_query_grad, precision=topmost_precision)
    grad_query = grad_query.astype(jnp.bfloat16)
    grad_key = grad_key.astype(jnp.bfloat16)
    grad_value = grad_value.astype(jnp.bfloat16)
    grad_rel_key = grad_rel_key.astype(jnp.bfloat16)
    grad_rel_query = grad_rel_query.astype(jnp.bfloat16)
    query_parts = adapter_grads(grad_query, tokens, adapt_up[0], adapt_scale[0], query_coeff)
    key_parts = adapter_grads(grad_key, tokens, adapt_up[1], adapt_scale[1], key_coeff)
    value_parts = adapter_grads(grad_value, tokens, adapt_up[2], adapt_scale[2], value_coeff)
    rel_query_parts = adapter_grads(
        grad_rel_query, rel_embed, adapt_up[0], adapt_scale[0], rel_query_coeff
    )
    rel_key_parts = adapter_grads(
        grad_rel_key, rel_embed, adapt_up[1], adapt_scale[1], rel_key_coeff
    )
    grad_tokens = grad_sum_one + input_grad(
        grad_query, qkv_weight[0], adapt_down[0], query_parts[3]
    )
    grad_tokens = grad_tokens + input_grad(grad_key, qkv_weight[1], adapt_down[1], key_parts[3])
    grad_tokens = grad_tokens + input_grad(grad_value, qkv_weight[2], adapt_down[2], value_parts[3])
    attention_down_factor = jnp.stack(
        [query_parts[0] + rel_query_parts[0], key_parts[0] + rel_key_parts[0], value_parts[0]]
    )
    qkv_up = jnp.stack(
        [query_parts[1] + rel_query_parts[1], key_parts[1] + rel_key_parts[1], value_parts[1]]
    )
    qkv_scale = jnp.stack(
        [query_parts[2] + rel_query_parts[2], key_parts[2] + rel_key_parts[2], value_parts[2]]
    )
    attention_down_factor, qkv_up, qkv_scale = share(attention_down_factor, qkv_up, qkv_scale)
    down_grad = jnp.concatenate(
        [attention_down_factor, out_down_grad[None], down_ffn_grad[None]], axis=0
    )
    up_grad = jnp.concatenate([qkv_up, out_up_grad[None], up_ffn_grad[None]], axis=0)
    scale_grad = jnp.concatenate([qkv_scale, out_scale_grad[None], ffn_scale_grad], axis=0)
    return (mixed, grad_tokens, down_grad, up_grad, hid_up_grad, hid_down_grad, scale_grad)


def solution(mesh):
    return jax.shard_map(
        on_device,
        mesh=mesh,
        in_specs=(
            P(("dp", "tensor"), None),
            P(),
            P(),
            P(None, "tensor"),
            P("tensor", None),
            P(),
            P(),
            P(),
            P(),
            P(),
            P(),
            P(),
            P(None, "tensor"),
            P(None, "tensor"),
            P(),
            P(("dp", "tensor"), None),
            P(("dp", "tensor"), None),
            P(),
            P(("dp", "tensor"), None),
        ),
        out_specs=(
            P(("dp", "tensor"), None),
            P(("dp", "tensor"), None),
            P(),
            P(),
            P(None, "tensor"),
            P(None, "tensor"),
            P(),
        ),
        check_vma=False,
    )
```

profile of v0, /device:TPU:0, one launch (start us, length us, event | category | flops | bytes accessed | tf_op | source)
XLA Modules:
  0.0 2696.3 jit_solution(14119873286051127963)
XLA Ops:
  74.7 675.3 %while.42 = (s32[]{:T(128)}, bf16[1024,768]{0,1:T(8,128)(2,1)}, f32[12,1024]{1,0:T(8,128)}, bf16[1024,768]{0,1:T(8,128)(2,1)}, s32[1024]{0:T(1024)S(1)}, /*index...) while((s32[]{:T(128)}, bf16[1024,768]{0,1:T(8,128)(2,1)}, ...), condition=%wide.region_5.6_spmd, body=%wide.region_2.5_spmd.sunk | while | flops 408419328 | bytes 84164744 | solution.py:223
  90.5 9.5 reshape.643
  109.6 9.5 reshape.642
  147.8 9.5 reshape.643
  166.9 9.5 reshape.642
  205.0 9.5 reshape.643
  224.1 9.5 reshape.642
  262.3 9.5 reshape.643
  281.4 9.5 reshape.642
  319.6 9.5 reshape.643
  338.7 9.5 reshape.642
  375.7 9.5 reshape.643
  394.8 9.5 reshape.642
  430.6 9.5 reshape.643
  449.8 9.5 reshape.642
  486.7 9.5 reshape.643
  505.8 9.5 reshape.642
  542.8 9.5 reshape.643
  561.9 9.5 reshape.642
  598.9 9.5 reshape.643
  618.0 9.5 reshape.642
  655.0 9.5 reshape.643
  674.1 9.5 reshape.642
  710.5 9.5 reshape.643
  729.6 9.5 reshape.642
  761.2 49.2 %all-gather.3.cloned.1.call-done = bf16[4096,768]{0,1:T(8,128)(2,1)} async-done(((bf16[1024,768]{0,1:T(8,128)(2,1)}), bf16[4096,768]{0,1:T(8,128)(2,1)}) %all-gather.3.cloned.1.call-update) | async-done | bytes 6291472 | tf_op jit(solution)/shard_map/all_gather | solution.py:243
  820.4 37.5 %multiply_convert_fusion = (bf16[4096,768]{1,0:T(8,128)(2,1)S(1)}, f32[4096,768]{1,0:T(8,128)}, f32[4096,768]{1,0:T(8,128)}) fusion(f32[4096,768]{1,0:T(8,128)S(1)} %fusion.279, bf16[12,768]{1,0:T(8,128)(2,1)S(1)} %copy-done.78, f32[4096,12]{0,1:T(8,128)S(1)} %fusion.171, f32[12]{0:T(128)S(1)} %copy-done.90), kind=kOutput, calls=%fused_computation.66 | convolution fusion | flops 660652032 | bytes 44255280 | tf_op jit(solution)/shard_map/dot_general | solution.py:52
  865.6 8.1 add_convert_fusion.2
  875.7 56.6 %reduce-scatter.3.cloned.1.call-done = bf16[1024,768]{0,1:T(8,128)(2,1)} async-done(((bf16[4096,768]{0,1:T(8,128)(2,1)}), bf16[1024,768]{0,1:T(8,128)(2,1)}) %reduce-scatter.3.cloned.1.call-update) | async-done | bytes 1572880 | tf_op jit(solution)/shard_map/reduce_scatter | solution.py:251
  939.4 46.5 %all-gather.5.cloned.1.call-done = bf16[4096,768]{0,1:T(8,128)(2,1)} async-done(((bf16[1024,768]{0,1:T(8,128)(2,1)}), bf16[4096,768]{0,1:T(8,128)(2,1)}) %all-gather.5.cloned.1.call-update) | async-done | bytes 6291472 | tf_op jit(solution)/shard_map/all_gather | solution.py:270
  990.5 8.2 fusion.282
  998.8 19.2 add_convert_fusion.1
  1027.9 8.9 add_convert_fusion
  1047.8 7.8 convolution_bitcast_fusion.8
  1061.3 34.0 %reduce-scatter.5.cloned.1.call-done = bf16[1024,768]{0,1:T(8,128)(2,1)} async-done(((bf16[4096,768]{0,1:T(8,128)(2,1)}), bf16[1024,768]{0,1:T(8,128)(2,1)}) %reduce-scatter.5.cloned.1.call-update) | async-done | bytes 1572880 | tf_op jit(solution)/shard_map/reduce_scatter | solution.py:286
  1118.3 1211.1 %while.43 = (s32[]{:T(128)}, bf16[1024,768]{0,1:T(8,128)(2,1)S(1)}, bf16[1024,768]{0,1:T(8,128)(2,1)}, bf16[1024,768]{0,1:T(8,128)(2,1)}, f32[1024,768]{0,1:T(8,...) while((s32[]{:T(128)}, bf16[1024,768]{0,1:T(8,128)(2,1)S(1)}, ...), condition=%wide.region_18.19_spmd, body=%wide.region_16.18_spmd.sunk | while | flops 1490031104 | bytes 188183136 | solution.py:372
  1136.0 9.5 reshape.644
  1158.8 9.6 reshape.645
  1237.7 9.5 reshape.644
  1260.7 9.6 reshape.645
  1339.4 9.5 reshape.644
  1362.2 9.6 reshape.645
  1441.0 9.5 reshape.644
  1463.8 9.6 reshape.645
  1542.5 9.5 reshape.644
  1565.5 9.6 reshape.645
  1644.2 9.5 reshape.644
  1667.0 9.6 reshape.645
  1742.0 9.5 reshape.644
  1764.8 9.6 reshape.645
  1841.8 9.5 reshape.644
  1864.8 9.6 reshape.645
  1941.7 9.5 reshape.644
  1964.5 9.6 reshape.645
  2041.4 9.5 reshape.644
  2064.2 9.6 reshape.645
  2141.1 9.5 reshape.644
  2164.1 9.6 reshape.645
  2241.0 9.5 reshape.644
  2263.7 9.6 reshape.645
  2377.5 11.8 add_add_fusion
  2392.8 86.0 %all-reduce.11.cloned.1.call-done = (f32[1,12,768]{2,1,0:T(8,128)}, f32[1,12,768]{2,1,0:T(8,128)}, f32[1,12,768]{2,1,0:T(8,128)}, f32[1,12,768]{2,1,0:T(8,128)},...) async-done(((f32[1,12,768]{2,1,0:T(8,128)}, f32[1,12,768]{2,1,0:T(8,128)}, f32[1,12,768]{2,1,0:T(8,128)}, f32[1,12,768]{2,1,0:T(8,128)}, f32[2,12]{1,0:T(2,128)}, ...) | async-done | bytes 147760 | tf_op jit(solution)/shard_map/psum | solution.py:117
  2480.2 131.7 %all-reduce.13.cloned.1.call-done = (f32[3,12,768]{2,1,0:T(8,128)}, f32[3,12,768]{2,1,0:T(8,128)}) async-done(((f32[3,12,768]{2,1,0:T(8,128)}, f32[3,12,768]{2,1,0:T(8,128)}), (f32[3,12,768]{2,1,0:T(8,128)}, f32[3,12,768]{2,1,0:T(8,128)})) %all-reduce.13.cloned.1.call-update) | async-done | bytes 221200 | tf_op jit(solution)/shard_map/psum | solution.py:117
  2615.2 71.1 %all-reduce.15.cloned.1.call-done = (f32[12,768]{1,0:T(8,128)}, f32[12,768]{1,0:T(8,128)}) async-done(((f32[12,768]{1,0:T(8,128)}, f32[12,768]{1,0:T(8,128)}), (f32[12,768]{1,0:T(8,128)}, f32[12,768]{1,0:T(8,128)})) %all-reduce.15.cloned.1.call-update) | async-done | bytes 73744 | tf_op jit(solution)/shard_map/psum | solution.py:293
  (1474 shorter events, 1629.4 us)
Async XLA Ops:
  7.2 853.3 %copy-start = (bf16[768,768]{1,0:T(8,128)(2,1)S(1)}, bf16[768,768]{1,0:T(8,128)(2,1)}, u32[]{:S(2)}) copy-start(bf16[768,768]{1,0:T(8,128)(2,1)} %param.27) | copy-start | bytes 3538948
  7.2 803.2 %all-gather.3.cloned.1.call-start = ((), (), s32[]{:S(2)}) async-start(), calls=%async_computation.2 | async-start | bytes 7864320 | tf_op jit(solution)/shard_map/all_gather | solution.py:243
  9.3 33.2 %copy-start.51 = (f32[512,12]{0,1:T(8,128)}, f32[512,12]{0,1:T(8,128)S(1)}, u32[]{:S(2)}) copy-start(f32[512,12]{0,1:T(8,128)S(1)} %fusion.197) | copy-start | bytes 73732
  36.2 26.9 copy-start.76
  36.2 32.0 %copy-start.74 = (f32[12]{0:T(128)}, f32[12]{0:T(128)S(1)}, u32[]{:S(2)}) copy-start(f32[12]{0:T(128)S(1)} %get-tuple-element.881) | copy-start | bytes 148
  757.8 344.0 %copy-start.55 = (f32[1024]{0:T(1024)}, f32[1024]{0:T(1024)S(1)}, u32[]{:S(2)}) copy-start(f32[1024]{0:T(1024)S(1)} %broadcast_multiply_fusion.5) | copy-start | bytes 12292
  759.4 342.3 %copy-start.57 = (f32[1024]{0:T(1024)}, f32[1024]{0:T(1024)S(1)}, u32[]{:S(2)}) copy-start(f32[1024]{0:T(1024)S(1)} %add_rsqrt_fusion.1) | copy-start | bytes 12292
  761.2 53.1 %copy-start.106 = (bf16[768,768]{1,0:T(8,128)(2,1)S(1)}, bf16[768,768]{1,0:T(8,128)(2,1)}, u32[]{:S(2)}) copy-start(bf16[768,768]{1,0:T(8,128)(2,1)} %param.26) | copy-start | bytes 3538948
  761.2 171.1 %reduce-scatter.3.cloned.1.call-start = ((), (), s32[]{:S(2)}) async-start(), calls=%async_computation.3 | async-start | bytes 7864320 | tf_op jit(solution)/shard_map/reduce_scatter | solution.py:251
  815.0 202.9 %copy-start.39 = (f32[4096,12]{0,1:T(8,128)}, f32[4096,12]{0,1:T(8,128)S(1)}, u32[]{:S(2)}) copy-start(f32[4096,12]{0,1:T(8,128)S(1)} %fusion.171) | copy-start | bytes 589828
  820.4 37.5 %copy-start.80 = (bf16[12,768]{1,0:T(8,128)(2,1)S(1)}, bf16[12,768]{1,0:T(8,128)(2,1)}, u32[]{:S(2)}) copy-start(bf16[12,768]{1,0:T(8,128)(2,1)} %param.36) | copy-start | bytes 55300
  873.8 112.1 %all-gather.5.cloned.1.call-start = ((), (), s32[]{:S(2)}) async-start(), calls=%async_computation.4 | async-start | bytes 7864320 | tf_op jit(solution)/shard_map/all_gather | solution.py:270
  875.7 61.4 %copy-start.26 = (bf16[1024,768]{0,1:T(8,128)(2,1)}, bf16[1024,768]{0,1:T(8,128)(2,1)S(1)}, u32[]{:S(2)}) copy-start(bf16[1024,768]{0,1:T(8,128)(2,1)S(1)} %copy.102) | copy-start | bytes 4718596
  939.4 156.0 %reduce-scatter.5.cloned.1.call-start = ((), (), s32[]{:S(2)}) async-start(), calls=%async_computation.5 | async-start | bytes 7864320 | tf_op jit(solution)/shard_map/reduce_scatter | solution.py:286
  998.8 19.2 copy-start.79
  1036.8 1442.1 %all-reduce.11.cloned.1.call-start = ((), (), s32[]{:S(2)}) async-start(), calls=%async_computation.6 | async-start | bytes 400384 | tf_op jit(solution)/shard_map/psum | solution.py:117
  1055.6 39.8 %copy-start.61 = (f32[1024]{0:T(1024)S(1)}, f32[1024]{0:T(1024)}, u32[]{:S(2)}) copy-start(f32[1024]{0:T(1024)} %copy-done.60) | copy-start | bytes 12292
  1055.6 39.8 %copy-start.67 = (f32[768]{0:T(1024)S(1)}, f32[768]{0:T(1024)}, u32[]{:S(2)}) copy-start(f32[768]{0:T(1024)} %param.29) | copy-start | bytes 9220
  1055.6 39.7 %copy-start.69 = (f32[768]{0:T(1024)S(1)}, f32[768]{0:T(1024)}, u32[]{:S(2)}) copy-start(f32[768]{0:T(1024)} %param.31) | copy-start | bytes 9220
  1055.6 39.7 %copy-start.71 = (f32[1024]{0:T(1024)S(1)}, f32[1024]{0:T(1024)}, u32[]{:S(2)}) copy-start(f32[1024]{0:T(1024)} %copy-done.70) | copy-start | bytes 12292
  1055.7 39.7 %copy-start.73 = (f32[1024]{0:T(1024)S(1)}, f32[1024]{0:T(1024)}, u32[]{:S(2)}) copy-start(f32[1024]{0:T(1024)} %copy-done.72) | copy-start | bytes 12292
  1055.7 39.7 %copy-start.96 = (f32[768]{0:T(1024)S(1)}, f32[768]{0:T(1024)}, u32[]{:S(2)}) copy-start(f32[768]{0:T(1024)} %param.32) | copy-start | bytes 9220
  1118.3 1211.2 %copy-start.75 = (f32[12]{0:T(128)S(1)}, f32[12]{0:T(128)}, u32[]{:S(2)}) copy-start(f32[12]{0:T(128)} %copy-done.74) | copy-start | bytes 148
  1120.8 56.8 %copy-start.38 = (bf16[512,128]{0,1:T(8,128)(2,1)}, bf16[512,128]{0,1:T(8,128)(2,1)S(1)}, u32[]{:S(2)}) copy-start(bf16[512,128]{0,1:T(8,128)(2,1)S(1)} %dynamic_slice.233) | copy-start | bytes 393220 | tf_op jit(solution)/shard_map/while
  1124.0 53.6 %copy-start.25 = (pred[512,512]{0,1:T(8,128)(4,1)}, pred[512,512]{0,1:T(8,128)(4,1)S(1)}, u32[]{:S(2)}) copy-start(pred[512,512]{0,1:T(8,128)(4,1)S(1)} %compare_and_fusion.5) | copy-start | bytes 786436 | tf_op jit(solution)/shard_map/while
  1125.0 23.9 copy-start.21
  1222.3 57.0 %copy-start.38 = (bf16[512,128]{0,1:T(8,128)(2,1)}, bf16[512,128]{0,1:T(8,128)(2,1)S(1)}, u32[]{:S(2)}) copy-start(bf16[512,128]{0,1:T(8,128)(2,1)S(1)} %dynamic_slice.233) | copy-start | bytes 393220 | tf_op jit(solution)/shard_map/while
  1225.5 53.8 %copy-start.25 = (pred[512,512]{0,1:T(8,128)(4,1)}, pred[512,512]{0,1:T(8,128)(4,1)S(1)}, u32[]{:S(2)}) copy-start(pred[512,512]{0,1:T(8,128)(4,1)S(1)} %compare_and_fusion.5) | copy-start | bytes 786436 | tf_op jit(solution)/shard_map/while
  1226.6 23.9 copy-start.21
  1321.9 17.5 copy-start.13
  1323.9 57.0 %copy-start.38 = (bf16[512,128]{0,1:T(8,128)(2,1)}, bf16[512,128]{0,1:T(8,128)(2,1)S(1)}, u32[]{:S(2)}) copy-start(bf16[512,128]{0,1:T(8,128)(2,1)S(1)} %dynamic_slice.233) | copy-start | bytes 393220 | tf_op jit(solution)/shard_map/while
  1327.1 53.8 %copy-start.25 = (pred[512,512]{0,1:T(8,128)(4,1)}, pred[512,512]{0,1:T(8,128)(4,1)S(1)}, u32[]{:S(2)}) copy-start(pred[512,512]{0,1:T(8,128)(4,1)S(1)} %compare_and_fusion.5) | copy-start | bytes 786436 | tf_op jit(solution)/shard_map/while
  1328.2 24.1 copy-start.21
  1425.7 56.8 %copy-start.38 = (bf16[512,128]{0,1:T(8,128)(2,1)}, bf16[512,128]{0,1:T(8,128)(2,1)S(1)}, u32[]{:S(2)}) copy-start(bf16[512,128]{0,1:T(8,128)(2,1)S(1)} %dynamic_slice.233) | copy-start | bytes 393220 | tf_op jit(solution)/shard_map/while
  1428.9 53.6 %copy-start.25 = (pred[512,512]{0,1:T(8,128)(4,1)}, pred[512,512]{0,1:T(8,128)(4,1)S(1)}, u32[]{:S(2)}) copy-start(pred[512,512]{0,1:T(8,128)(4,1)S(1)} %compare_and_fusion.5) | copy-start | bytes 786436 | tf_op jit(solution)/shard_map/while
  1430.0 23.9 copy-start.21
  1527.2 57.0 %copy-start.38 = (bf16[512,128]{0,1:T(8,128)(2,1)}, bf16[512,128]{0,1:T(8,128)(2,1)S(1)}, u32[]{:S(2)}) copy-start(bf16[512,128]{0,1:T(8,128)(2,1)S(1)} %dynamic_slice.233) | copy-start | bytes 393220 | tf_op jit(solution)/shard_map/while
  1530.4 53.8 %copy-start.25 = (pred[512,512]{0,1:T(8,128)(4,1)}, pred[512,512]{0,1:T(8,128)(4,1)S(1)}, u32[]{:S(2)}) copy-start(pred[512,512]{0,1:T(8,128)(4,1)S(1)} %compare_and_fusion.5) | copy-start | bytes 786436 | tf_op jit(solution)/shard_map/while
  1531.5 23.9 copy-start.21
  1628.7 57.0 %copy-start.38 = (bf16[512,128]{0,1:T(8,128)(2,1)}, bf16[512,128]{0,1:T(8,128)(2,1)S(1)}, u32[]{:S(2)}) copy-start(bf16[512,128]{0,1:T(8,128)(2,1)S(1)} %dynamic_slice.233) | copy-start | bytes 393220 | tf_op jit(solution)/shard_map/while
  1631.9 53.8 %copy-start.25 = (pred[512,512]{0,1:T(8,128)(4,1)}, pred[512,512]{0,1:T(8,128)(4,1)S(1)}, u32[]{:S(2)}) copy-start(pred[512,512]{0,1:T(8,128)(4,1)S(1)} %compare_and_fusion.5) | copy-start | bytes 786436 | tf_op jit(solution)/shard_map/while
  1633.0 24.1 copy-start.21
  1726.7 56.8 %copy-start.38 = (bf16[512,128]{0,1:T(8,128)(2,1)}, bf16[512,128]{0,1:T(8,128)(2,1)S(1)}, u32[]{:S(2)}) copy-start(bf16[512,128]{0,1:T(8,128)(2,1)S(1)} %dynamic_slice.233) | copy-start | bytes 393220 | tf_op jit(solution)/shard_map/while
  1729.9 53.6 %copy-start.25 = (pred[512,512]{0,1:T(8,128)(4,1)}, pred[512,512]{0,1:T(8,128)(4,1)S(1)}, u32[]{:S(2)}) copy-start(pred[512,512]{0,1:T(8,128)(4,1)S(1)} %compare_and_fusion.5) | copy-start | bytes 786436 | tf_op jit(solution)/shard_map/while
  1731.0 23.9 copy-start.21
  1826.5 57.0 %copy-start.38 = (bf16[512,128]{0,1:T(8,128)(2,1)}, bf16[512,128]{0,1:T(8,128)(2,1)S(1)}, u32[]{:S(2)}) copy-start(bf16[512,128]{0,1:T(8,128)(2,1)S(1)} %dynamic_slice.233) | copy-start | bytes 393220 | tf_op jit(solution)/shard_map/while
  1829.7 53.8 %copy-start.25 = (pred[512,512]{0,1:T(8,128)(4,1)}, pred[512,512]{0,1:T(8,128)(4,1)S(1)}, u32[]{:S(2)}) copy-start(pred[512,512]{0,1:T(8,128)(4,1)S(1)} %compare_and_fusion.5) | copy-start | bytes 786436 | tf_op jit(solution)/shard_map/while
  1830.8 23.9 copy-start.21
  1924.2 17.5 copy-start.13
  1926.2 57.0 %copy-start.38 = (bf16[512,128]{0,1:T(8,128)(2,1)}, bf16[512,128]{0,1:T(8,128)(2,1)S(1)}, u32[]{:S(2)}) copy-start(bf16[512,128]{0,1:T(8,128)(2,1)S(1)} %dynamic_slice.233) | copy-start | bytes 393220 | tf_op jit(solution)/shard_map/while
  1929.4 53.8 %copy-start.25 = (pred[512,512]{0,1:T(8,128)(4,1)}, pred[512,512]{0,1:T(8,128)(4,1)S(1)}, u32[]{:S(2)}) copy-start(pred[512,512]{0,1:T(8,128)(4,1)S(1)} %compare_and_fusion.5) | copy-start | bytes 786436 | tf_op jit(solution)/shard_map/while
  1930.5 24.1 copy-start.21
  2026.1 56.8 %copy-start.38 = (bf16[512,128]{0,1:T(8,128)(2,1)}, bf16[512,128]{0,1:T(8,128)(2,1)S(1)}, u32[]{:S(2)}) copy-start(bf16[512,128]{0,1:T(8,128)(2,1)S(1)} %dynamic_slice.233) | copy-start | bytes 393220 | tf_op jit(solution)/shard_map/while
  2029.3 53.6 %copy-start.25 = (pred[512,512]{0,1:T(8,128)(4,1)}, pred[512,512]{0,1:T(8,128)(4,1)S(1)}, u32[]{:S(2)}) copy-start(pred[512,512]{0,1:T(8,128)(4,1)S(1)} %compare_and_fusion.5) | copy-start | bytes 786436 | tf_op jit(solution)/shard_map/while
  2030.4 23.9 copy-start.21
  2125.8 57.0 %copy-start.38 = (bf16[512,128]{0,1:T(8,128)(2,1)}, bf16[512,128]{0,1:T(8,128)(2,1)S(1)}, u32[]{:S(2)}) copy-start(bf16[512,128]{0,1:T(8,128)(2,1)S(1)} %dynamic_slice.233) | copy-start | bytes 393220 | tf_op jit(solution)/shard_map/while
  2129.0 53.8 %copy-start.25 = (pred[512,512]{0,1:T(8,128)(4,1)}, pred[512,512]{0,1:T(8,128)(4,1)S(1)}, u32[]{:S(2)}) copy-start(pred[512,512]{0,1:T(8,128)(4,1)S(1)} %compare_and_fusion.5) | copy-start | bytes 786436 | tf_op jit(solution)/shard_map/while
  2130.0 23.9 copy-start.21
  2225.5 57.0 %copy-start.38 = (bf16[512,128]{0,1:T(8,128)(2,1)}, bf16[512,128]{0,1:T(8,128)(2,1)S(1)}, u32[]{:S(2)}) copy-start(bf16[512,128]{0,1:T(8,128)(2,1)S(1)} %dynamic_slice.233) | copy-start | bytes 393220 | tf_op jit(solution)/shard_map/while
  2228.7 53.8 %copy-start.25 = (pred[512,512]{0,1:T(8,128)(4,1)}, pred[512,512]{0,1:T(8,128)(4,1)S(1)}, u32[]{:S(2)}) copy-start(pred[512,512]{0,1:T(8,128)(4,1)S(1)} %compare_and_fusion.5) | copy-start | bytes 786436 | tf_op jit(solution)/shard_map/while
  2229.7 24.1 copy-start.21
  2352.5 259.4 %all-reduce.13.cloned.1.call-start = ((), (), s32[]{:S(2)}) async-start(), calls=%async_computation.7 | async-start | bytes 589824 | tf_op jit(solution)/shard_map/psum | solution.py:117
  2353.2 333.1 %all-reduce.15.cloned.1.call-start = ((), (), s32[]{:S(2)}) async-start(), calls=%async_computation.8 | async-start | bytes 196608 | tf_op jit(solution)/shard_map/psum | solution.py:293
  2377.5 311.7 %copy-start.1 = (bf16[768,768]{1,0:T(8,128)(2,1)S(1)}, bf16[768,768]{1,0:T(8,128)(2,1)}, u32[]{:S(2)}) copy-start(bf16[768,768]{1,0:T(8,128)(2,1)} %param.27) | copy-start | bytes 3538948
  (257 other events, 1211.7 us)
Sparse Core Ops, SparseCore 0:
  761.3 49.0 all-gather.2
  873.9 58.3 reduce-scatter.2
  939.5 46.3 all-gather.4
  1036.9 58.3 reduce-scatter.4
  2352.6 126.2 all-reduce.10
  2484.7 127.0 all-reduce.12
  2615.7 70.5 all-reduce.14
where the time goes:
time: 2710 us; the launch traced here: 2700 us
  local copies, waits for them, and re-layouts  1610 us (59%)
  matrix products  509 us (19%)
  waiting for transfers between devices  475 us (18%)
  other arithmetic  73.1 us (3%)
    reshape x72, local copies, waits for them, and re-layouts, rel_shift(): return window.reshape(heads, LEN3, 2 * LEN3 - 1)[:, :, :LEN3]  508 us
    while x492, local copies, waits for them, and re-layouts  336 us
    slice x48, local copies, waits for them, and re-layouts, rel_shift(): window = flat[:, LEN3 - 1:LEN3 - 1 + LEN3 * (2 * LEN3 - 1)]  279 us
    psum x2, waiting for transfers between devices, share(): return lax.psum((downward, upward, scaling), ('dp', 'tensor'))  218 us
    dynamic_slice x96, local copies, waits for them, and re-layouts, take_pair(): lax.dynamic_slice(source, (start_row, start_col), (LEN3, 2 * DH))  87 us
    psum x1, waiting for transfers between devices, on_device(): hid_up_grad, hid_down_grad = lax.psum((hid_up_grad, hid_down_grad), 'dp')  71.1 us
    pad x24, local copies, waits for them, and re-layouts, rel_shift(): window = flat[:, LEN3 - 1:LEN3 - 1 + LEN3 * (2 * LEN3 - 1)]  70.8 us
    dot_general x24, matrix products, pair_scores(): jnp.einsum('ihd,jhd->hij', query_per_head, head_key, preferred_element_ty...  66.1 us
  transfers between devices with their start and end apart: 7, of which 7 were waited for; matrix products, arithmetic and copies ran while one was open for 3% of the time, Pallas kernels for 0%

commit v1 on v0

v1 whole, which is shorter than its diff:
```python
import jax
import jax.numpy as jnp
from jax import lax
from jax.experimental import pallas as pl
from jax.experimental.pallas import tpu as pltpu
from jax.sharding import PartitionSpec as P

D = 768
H = 12
DH = 64
PAIR = 2 * DH
SPAN = 256
RANK = 12
PAD = 16
ROWS = 1024
LEN1 = 128
LEN3 = 512
OFFSETS = 2 * LEN3
TILE = 128
BLOCK = 256
SLOTS = ((0, 128), (128, 128), (256, 256), (512, 512))
PACKED = 2 * D + 2 * PAD
norm_epsilon = 1e-07
masked_score = -1e30
bf16 = jnp.bfloat16
f32 = jnp.float32
MEMORY = 60 * 1024 * 1024


def dot_nn(a, b):
    return jnp.dot(a, b, preferred_element_type=f32)


def dot_nt(a, b):
    return lax.dot_general(a, b, (((1,), (1,)), ((), ())), preferred_element_type=f32)


def dot_tn(a, b):
    return lax.dot_general(a, b, (((0,), (0,)), ((), ())), preferred_element_type=f32)


def two_parts(wide):
    high = wide.astype(bf16)
    rest = (wide - high.astype(f32)).astype(bf16)
    return jnp.concatenate([high, rest], axis=0)


def add_parts(stacked):
    return stacked[:PAD] + stacked[PAD:]


def merged(weight, down, up, scale):
    twice = jnp.concatenate([up, up], axis=0)
    extra = dot_tn(two_parts(down.astype(f32) * scale), twice)
    return (weight.astype(f32) + extra).astype(bf16)


def live_counts(lengths_ref, counts_ref):
    ranks = ((0, 0), (0, 1), (1, 0), (2, 0))
    return [
        jnp.where(rank < counts_ref[0, bucket], lengths_ref[0, slot], 0)
        for slot, (bucket, rank) in enumerate(ranks)
    ]


def pack_kernel(in_ref, back_ref, factor_ref, scale_ref, packed_ref):
    packed_ref[:D] = merged(in_ref[...], factor_ref[4], factor_ref[10], scale_ref[:, 4:5])
    packed_ref[D : 2 * D] = merged(back_ref[...], factor_ref[11], factor_ref[9], scale_ref[:, 5:6])
    packed_ref[2 * D : 2 * D + PAD] = factor_ref[10]
    packed_ref[2 * D + PAD :] = factor_ref[11]


def pack_weights(in_weight, back_weight, factors, scales):
    return pl.pallas_call(
        pack_kernel,
        out_shape=jax.ShapeDtypeStruct((PACKED, D), bf16),
        compiler_params=pltpu.CompilerParams(vmem_limit_bytes=MEMORY),
        name="pack_weights",
    )(in_weight, back_weight, factors, scales)


def project_kernel(
    tokens_ref,
    qkv_ref,
    out_ref,
    rel_ref,
    index_ref,
    factor_ref,
    scale_ref,
    q_ref,
    k_ref,
    v_ref,
    ek_ref,
    eq_ref,
    fq_ref,
    merged_ref,
    coeff_ref,
    rel_coeff_ref,
    pos_scr,
):
    step = pl.program_id(0)

    @pl.when(step == 0)
    def _():
        for member in range(3):
            merged_ref[member] = merged(
                qkv_ref[member],
                factor_ref[member],
                factor_ref[5 + member],
                scale_ref[:, member : member + 1],
            )
        merged_ref[3] = merged(out_ref[...], factor_ref[3], factor_ref[8], scale_ref[:, 3:4])
        rel = rel_ref[...]
        for member in range(2):
            pos_scr[member] = dot_nn(rel, merged_ref[member]).astype(bf16)
            rel_coeff_ref[member] = dot_nt(factor_ref[member], rel)

    tokens = tokens_ref[...]
    for member, ref in enumerate((q_ref, k_ref, v_ref)):
        ref[...] = dot_nn(tokens, merged_ref[member]).astype(bf16)
        coeff_ref[member] = dot_nt(factor_ref[member], tokens)
    bucket = lax.broadcasted_iota(jnp.int32, (2 * SPAN, BLOCK), 0)
    for ref, row, member in ((ek_ref, 0, 1), (eq_ref, 0, 0), (fq_ref, 1, 0)):
        chosen = jnp.where(bucket == index_ref[row : row + 1, :], 1.0, 0.0).astype(bf16)
        ref[...] = dot_tn(chosen, pos_scr[member]).astype(bf16)


def whole(*shape):
    return pl.BlockSpec(shape, lambda *at: (0,) * len(shape))


def project(tokens, qkv_weight, out_weight, rel_embed, index_rows, factors, scales):
    tile = pl.BlockSpec((BLOCK, D), lambda i: (i, 0))
    rows = jax.ShapeDtypeStruct((ROWS, D), bf16)
    return pl.pallas_call(
        project_kernel,
        grid=(ROWS // BLOCK,),
        in_specs=[
            tile,
            whole(3, D, D),
            whole(D, D),
            whole(2 * SPAN, D),
            pl.BlockSpec((2, BLOCK), lambda i: (0, i)),
            whole(12, PAD, D),
            whole(PAD, 128),
        ],
        out_specs=[tile] * 6
        + [
            whole(4, D, D),
            pl.BlockSpec((3, PAD, BLOCK), lambda i: (0, 0, i)),
            whole(2, PAD, 2 * SPAN),
        ],
        out_shape=[rows] * 6
        + [
            jax.ShapeDtypeStruct((4, D, D), bf16),
            jax.ShapeDtypeStruct((3, PAD, ROWS), f32),
            jax.ShapeDtypeStruct((2, PAD, 2 * SPAN), f32),
        ],
        scratch_shapes=[pltpu.VMEM((2, 2 * SPAN, D), bf16)],
        compiler_params=pltpu.CompilerParams(vmem_limit_bytes=MEMORY),
        name="project",
    )(tokens, qkv_weight, out_weight, rel_embed, index_rows, factors, scales)


def unit_matrix(flipped):
    row = lax.broadcasted_iota(jnp.int32, (TILE, TILE), 0)
    col = lax.broadcasted_iota(jnp.int32, (TILE, TILE), 1)
    return jnp.where(row == (TILE - 1 - col if flipped else col), 1.0, 0.0).astype(bf16)


def head_lanes(member):
    lane = lax.broadcasted_iota(jnp.int32, (1, PAIR), 1)
    return jnp.where(lane // DH == member, 1.0, 0.0).astype(bf16)


def skew(table, length):
    return pltpu.roll(table, length + 1, 1, stride=1, stride_axis=0)[:, :length]


def unskew(scores):
    wide = jnp.concatenate([scores, jnp.zeros((TILE, TILE), f32)], axis=1)
    return pltpu.roll(wide, 0, 1, stride=1, stride_axis=0)


def add_pair(ref, member, start, value):
    here = pl.ds(start, value.shape[0])

    @pl.when(member == 0)
    def _():
        ref[here, :] = value

    @pl.when(member == 1)
    def _():
        ref[here, :] = ref[here, :] + value


def forward_kernel(
    lengths_ref,
    counts_ref,
    q_ref,
    k_ref,
    v_ref,
    ek_ref,
    eq_ref,
    context_ref,
    p1_ref,
    p2_ref,
    p3_ref,
    shift_scr,
):
    member = pl.program_id(1)
    mask = head_lanes(member)
    eye = unit_matrix(False)
    anti = unit_matrix(True)
    factor = (3.0 * DH) ** -0.5
    counts = live_counts(lengths_ref, counts_ref)
    for slot, (start, length) in enumerate(SLOTS):
        keys = k_ref[start : start + length, :] * mask
        values = v_ref[start : start + length, :] * mask
        live = lax.broadcasted_iota(jnp.int32, (1, length), 1) < counts[slot]
        for t in range(length // TILE):
            low = LEN3 - TILE - TILE * t
            table = dot_nt(keys[t * TILE : (t + 1) * TILE], eq_ref[low : low + length + TILE, :])
            shift_scr[t * TILE : (t + 1) * TILE, :length] = skew(table, length).astype(bf16)
        for t in range(length // TILE):
            low = LEN3 - TILE - TILE * t
            row = start + t * TILE
            queries = q_ref[row : row + TILE, :] * mask
            relative = skew(dot_nt(queries, ek_ref[low : low + length + TILE, :]), length)
            left = jnp.concatenate([queries, eye], axis=1)
            right = jnp.concatenate(
                [keys, shift_scr[:length, t * TILE : (t + 1) * TILE]], axis=1
            )
            scores = jnp.where(live, (dot_nt(left, right) + relative) * factor, masked_score)
            weights = jnp.exp(scores - jnp.max(scores, axis=1, keepdims=True))
            prob = (weights * (1.0 / jnp.sum(weights, axis=1, keepdims=True))).astype(bf16)
            add_pair(context_ref, member, row, dot_nn(prob, values).astype(bf16))
            turned = dot_nn(anti, prob).astype(bf16)
            if length == LEN1:
                p1_ref[0, row : row + TILE, :] = turned
            elif length == LEN3:
                p3_ref[0, t * TILE : (t + 1) * TILE, :] = turned
            else:
                p2_ref[0, t * TILE : (t + 1) * TILE, :] = turned


PAIR_SPEC = pl.BlockSpec((ROWS, PAIR), lambda p, e: (0, p))
PROB_SIZES = ((256, 128), (256, 256), (512, 512))
PROB_SPECS = [pl.BlockSpec((1, *size), lambda p, e: (2 * p + e, 0, 0)) for size in PROB_SIZES]


def attend_forward(lengths, counts, q, k, v, ek, eq):
    return pl.pallas_call(
        forward_kernel,
        grid=(H // 2, 2),
        in_specs=[pl.BlockSpec(memory_space=pltpu.SMEM)] * 2 + [PAIR_SPEC] * 5,
        out_specs=[PAIR_SPEC] + PROB_SPECS,
        out_shape=[jax.ShapeDtypeStruct((ROWS, D), bf16)]
        + [jax.ShapeDtypeStruct((H, *size), bf16) for size in PROB_SIZES],
        scratch_shapes=[pltpu.VMEM((LEN3, LEN3), bf16)],
        compiler_params=pltpu.CompilerParams(vmem_limit_bytes=MEMORY),
        name="attention_forward",
    )(lengths, counts, q, k, v, ek, eq)


def backward_kernel(
    q_ref,
    k_ref,
    v_ref,
    g_ref,
    ek_ref,
    fq_ref,
    p1_ref,
    p2_ref,
    p3_ref,
    gq_ref,
    gk_ref,
    gv_ref,
    gek_ref,
    gfq_ref,
    grad_scr,
    turned_scr,
    values_scr,
):
    member = pl.program_id(1)
    mask = head_lanes(member)
    eye = unit_matrix(False)
    anti = unit_matrix(True)
    factor = (3.0 * DH) ** -0.5

    @pl.when(member == 0)
    def _():
        gek_ref[...] = jnp.zeros_like(gek_ref)
        gfq_ref[...] = jnp.zeros_like(gfq_ref)

    for start, length in SLOTS:
        count = length // TILE
        keys = k_ref[start : start + length, :] * mask
        values = v_ref[start : start + length, :] * mask
        value_grad = jnp.zeros((PAIR, length), f32)
        for t in range(count):
            low = LEN3 - TILE - TILE * t
            row = start + t * TILE
            queries = dot_nn(anti, q_ref[row : row + TILE, :] * mask).astype(bf16)
            grads = dot_nn(anti, g_ref[row : row + TILE, :] * mask).astype(bf16)
            if length == LEN1:
                prob = p1_ref[0, row : row + TILE, :]
            elif length == LEN3:
                prob = p3_ref[0, t * TILE : (t + 1) * TILE, :]
            else:
                prob = p2_ref[0, t * TILE : (t + 1) * TILE, :]
            grad_prob = dot_nt(grads, values)
            wide = prob.astype(f32)
            delta = jnp.sum(wide * grad_prob, axis=1, keepdims=True)
            raw = (wide * ((grad_prob - delta) * factor)).astype(bf16)
            place = (count - 1 - t) * TILE
            grad_scr[place : place + TILE, :length] = raw
            turned_scr[place : place + TILE, :] = queries
            spread = unskew(raw.astype(f32)).astype(bf16)
            window = ek_ref[low : low + length + TILE, :] * mask
            query_grad = dot_nn(
                jnp.concatenate([raw, spread], axis=1), jnp.concatenate([keys, window], axis=0)
            )
            add_pair(gq_ref, member, row, dot_nn(anti, query_grad.astype(bf16)).astype(bf16))
            gek_ref[:, low : low + length + TILE] += dot_tn(queries, spread)
            value_grad = value_grad + dot_tn(grads, prob)
        values_scr[:, start : start + length] = value_grad
        turned = turned_scr[:length, :]
        for t in range(count):
            low = LEN3 - length + TILE * t
            row = start + t * TILE
            raw = dot_nt(eye, grad_scr[:length, t * TILE : (t + 1) * TILE])
            spread = unskew(raw).astype(bf16)
            window = fq_ref[low : low + length + TILE, :] * mask
            key_grad = dot_nn(
                jnp.concatenate([raw.astype(bf16), spread], axis=1),
                jnp.concatenate([turned, window], axis=0),
            )
            add_pair(gk_ref, member, row, key_grad.astype(bf16))
            gfq_ref[:, low : low + length + TILE] += dot_tn(
                keys[t * TILE : (t + 1) * TILE], spread
            )
    add_pair(gv_ref, member, 0, values_scr[...].T.astype(bf16))


def attend_backward(q, k, v, g, ek, fq, p1, p2, p3):
    table = pl.BlockSpec((PAIR, OFFSETS), lambda p, e: (p, 0))
    return pl.pallas_call(
        backward_kernel,
        grid=(H // 2, 2),
        in_specs=[PAIR_SPEC] * 6 + PROB_SPECS,
        out_specs=[PAIR_SPEC] * 3 + [table] * 2,
        out_shape=[jax.ShapeDtypeStruct((ROWS, D), bf16)] * 3
        + [jax.ShapeDtypeStruct((D, OFFSETS), f32)] * 2,
        scratch_shapes=[
            pltpu.VMEM((LEN3, LEN3), bf16),
            pltpu.VMEM((LEN3, PAIR), bf16),
            pltpu.VMEM((PAIR, ROWS), f32),
        ],
        compiler_params=pltpu.CompilerParams(vmem_limit_bytes=MEMORY),
        name="attention_backward",
    )(q, k, v, g, ek, fq, p1, p2, p3)


def gelu_pair(hidden):
    z = jnp.abs(hidden) * 0.7071067811865476
    t = 1.0 / (1.0 + 0.3275911 * z)
    poly = t * (
        0.127414796
        + t * (-0.142248368 + t * (0.7107068705 + t * (-0.7265760135 + t * 0.5307027145)))
    )
    bell = jnp.exp(-z * z)
    tail = poly * bell
    below = jnp.where(hidden >= 0, 1.0 - tail, tail)
    return hidden * below, below + hidden * (bell * 0.3989422804014327)


def norm_forward(values, gain, shift):
    centered = values - jnp.mean(values, axis=1, keepdims=True)
    inverse = lax.rsqrt(jnp.mean(centered * centered, axis=1, keepdims=True) + norm_epsilon)
    normal = centered * inverse
    return (normal * gain + shift, normal, inverse)


def norm_backward(grad_out, normal, inverse, gain):
    scaled = grad_out * gain
    return inverse * (
        scaled
        - jnp.mean(scaled, axis=1, keepdims=True)
        - normal * jnp.mean(scaled * normal, axis=1, keepdims=True)
    )


def middle_kernel(
    lengths_ref,
    counts_ref,
    tokens_ref,
    context_ref,
    out_grad_ref,
    weight_ref,
    packed_ref,
    factor_ref,
    scale_ref,
    norm_ref,
    mixed_ref,
    grad_one_ref,
    context_grad_ref,
    small_ref,
    hidden_ref,
    scale_grad_ref,
    active_scr,
    slope_scr,
):
    step = pl.program_id(0)
    chunks = packed_ref.shape[0]

    @pl.when(step == 0)
    def _():
        small_ref[...] = jnp.zeros_like(small_ref)
        hidden_ref[...] = jnp.zeros_like(hidden_ref)
        scale_grad_ref[...] = jnp.zeros_like(scale_grad_ref)

    row = lax.broadcasted_iota(jnp.int32, (BLOCK, 1), 0) + step * BLOCK
    live = jnp.zeros((BLOCK, 1), f32)
    for (start, length), used in zip(SLOTS, live_counts(lengths_ref, counts_ref)):
        live = jnp.where((row >= start) & (row < start + used), 1.0, live)
    gain_one, shift_one, gain_two, shift_two = (norm_ref[i : i + 1, :] for i in range(4))

    context = context_ref[...]
    weight = weight_ref[0]
    attended = dot_nn(context, weight)
    normed, normal_one, inverse_one = norm_forward(
        tokens_ref[...].astype(f32) + attended, gain_one, shift_one
    )
    normed_low = normed.astype(bf16)
    mlp = jnp.zeros((BLOCK, D), f32)
    back_coeff = jnp.zeros((PAD, BLOCK), f32)
    for c in range(chunks):
        hidden = dot_nn(normed_low, packed_ref[c, :D, :])
        active, slope = gelu_pair(hidden)
        active = active.astype(bf16)
        active_scr[c] = active
        slope_scr[c] = slope
        mlp = mlp + dot_nn(active, packed_ref[c, D : 2 * D, :])
        back_coeff = back_coeff + dot_nt(packed_ref[c, 2 * D + PAD :, :], active)
    result, normal_two, inverse_two = norm_forward(normed + mlp, gain_two, shift_two)
    mixed_ref[...] = (result * live).astype(bf16)
    grad_two = norm_backward(
        out_grad_ref[...].astype(f32) * live, normal_two, inverse_two, gain_two
    )
    grad_mlp = grad_two.astype(bf16)

    back_slope = dot_nt(factor_ref[9], grad_mlp)
    small_ref[3] += add_parts(dot_nn(two_parts(back_coeff * scale_ref[:, 5:6]), grad_mlp))
    scale_grad_ref[:, 5:6] += jnp.sum(back_coeff * back_slope, axis=1, keepdims=True)
    back_through = two_parts(back_slope * scale_ref[:, 5:6])
    in_coeff = dot_nt(factor_ref[4], normed_low)
    in_scaled = two_parts(in_coeff * scale_ref[:, 4:5])
    in_slope = jnp.zeros((PAD, BLOCK), f32)
    grad_normed = grad_two
    for c in range(chunks):
        grad_active = dot_nt(grad_mlp, packed_ref[c, D : 2 * D, :])
        grad_hidden = (grad_active * slope_scr[c]).astype(bf16)
        grad_normed = grad_normed + dot_nt(grad_hidden, packed_ref[c, :D, :])
        in_slope = in_slope + dot_nt(packed_ref[c, 2 * D : 2 * D + PAD, :], grad_hidden)
        hidden_ref[c] += add_parts(dot_nn(in_scaled, grad_hidden))
        hidden_ref[chunks + c] += add_parts(dot_nn(back_through, active_scr[c]))
    scale_grad_ref[:, 4:5] += jnp.sum(in_coeff * in_slope, axis=1, keepdims=True)
    small_ref[2] += add_parts(dot_nn(two_parts(in_slope * scale_ref[:, 4:5]), normed_low))

    grad_one = norm_backward(grad_normed, normal_one, inverse_one, gain_one)
    grad_one_ref[...] = grad_one
    grad_attended = grad_one.astype(bf16)
    context_grad_ref[...] = dot_nt(grad_attended, weight).astype(bf16)
    out_coeff = dot_nt(factor_ref[3], context)
    out_slope = dot_nt(factor_ref[8], grad_attended)
    small_ref[1] += add_parts(dot_nn(two_parts(out_coeff * scale_ref[:, 3:4]), grad_attended))
    small_ref[0] += add_parts(dot_nn(two_parts(out_slope * scale_ref[:, 3:4]), context))
    scale_grad_ref[:, 3:4] += jnp.sum(out_coeff * out_slope, axis=1, keepdims=True)


def middle(lengths, counts, tokens, context, out_grad, weights, packed, factors, scales, norms):
    chunks = packed.shape[0]
    tile = pl.BlockSpec((BLOCK, D), lambda i: (i, 0))
    return pl.pallas_call(
        middle_kernel,
        grid=(ROWS // BLOCK,),
        in_specs=[pl.BlockSpec(memory_space=pltpu.SMEM)] * 2
        + [tile] * 3
        + [
            pl.BlockSpec((1, D, D), lambda i: (3, 0, 0)),
            pl.BlockSpec(
                (chunks, PACKED, D), lambda i: (0, 0, 0), pipeline_mode=pl.Buffered(1)
            ),
            whole(12, PAD, D),
            whole(PAD, 128),
            whole(4, D),
        ],
        out_specs=[tile] * 3
        + [whole(4, PAD, D), whole(2 * chunks, PAD, D), whole(PAD, 128)],
        out_shape=[
            jax.ShapeDtypeStruct((ROWS, D), bf16),
            jax.ShapeDtypeStruct((ROWS, D), f32),
            jax.ShapeDtypeStruct((ROWS, D), bf16),
            jax.ShapeDtypeStruct((4, PAD, D), f32),
            jax.ShapeDtypeStruct((2 * chunks, PAD, D), f32),
            jax.ShapeDtypeStruct((PAD, 128), f32),
        ],
        scratch_shapes=[
            pltpu.VMEM((chunks, BLOCK, D), bf16),
            pltpu.VMEM((chunks, BLOCK, D), f32),
        ],
        compiler_params=pltpu.CompilerParams(vmem_limit_bytes=MEMORY),
        name="middle",
    )(lengths, counts, tokens, context, out_grad, weights, packed, factors, scales, norms)


def last_kernel(
    tokens_ref,
    gq_ref,
    gk_ref,
    gv_ref,
    grad_one_ref,
    coeff_ref,
    merged_ref,
    rel_ref,
    index_ref,
    rel_coeff_ref,
    gek_ref,
    gfq_ref,
    factor_ref,
    scale_ref,
    in_grad_ref,
    down_ref,
    up_ref,
    scale_grad_ref,
):
    step = pl.program_id(0)

    @pl.when(step == 0)
    def _():
        rel = rel_ref[...]
        scale_grad_ref[...] = jnp.zeros_like(scale_grad_ref)
        down_ref[2] = jnp.zeros((PAD, D), f32)
        up_ref[2] = jnp.zeros((PAD, D), f32)
        bucket = lax.broadcasted_iota(jnp.int32, (2 * SPAN, OFFSETS), 0)
        for member, ref, row in ((0, gfq_ref, 1), (1, gek_ref, 0)):
            scale = scale_ref[:, member : member + 1]
            chosen = jnp.where(bucket == index_ref[row : row + 1, :], 1.0, 0.0).astype(bf16)
            grad = dot_nt(ref[...].astype(bf16), chosen).astype(bf16)
            coeff = rel_coeff_ref[member]
            slope = dot_nn(factor_ref[5 + member], grad)
            up_ref[member] = add_parts(dot_nt(two_parts(coeff * scale), grad))
            down_ref[member] = add_parts(dot_nn(two_parts(slope * scale), rel))
            scale_grad_ref[:, member : member + 1] += jnp.sum(
                coeff * slope, axis=1, keepdims=True
            )

    tokens = tokens_ref[...]
    in_grad = grad_one_ref[...]
    for member, ref in enumerate((gq_ref, gk_ref, gv_ref)):
        grad = ref[...]
        scale = scale_ref[:, member : member + 1]
        in_grad = in_grad + dot_nt(grad, merged_ref[member])
        coeff = coeff_ref[member]
        slope = dot_nt(factor_ref[5 + member], grad)
        up_ref[member] += add_parts(dot_nn(two_parts(coeff * scale), grad))
        down_ref[member] += add_parts(dot_nn(two_parts(slope * scale), tokens))
        scale_grad_ref[:, member : member + 1] += jnp.sum(coeff * slope, axis=1, keepdims=True)
    in_grad_ref[...] = in_grad


def last(tokens, gq, gk, gv, grad_one, coeff, weights, rel, index, rel_coeff, gek, gfq, factors, scales):
    tile = pl.BlockSpec((BLOCK, D), lambda i: (i, 0))
    return pl.pallas_call(
        last_kernel,
        grid=(ROWS // BLOCK,),
        in_specs=[tile] * 5
        + [
            pl.BlockSpec((3, PAD, BLOCK), lambda i: (0, 0, i)),
            whole(3, D, D),
            whole(2 * SPAN, D),
            whole(2, OFFSETS),
            whole(2, PAD, 2 * SPAN),
            whole(D, OFFSETS),
            whole(D, OFFSETS),
            whole(12, PAD, D),
            whole(PAD, 128),
        ],
        out_specs=[tile, whole(3, PAD, D), whole(3, PAD, D), whole(PAD, 128)],
        out_shape=[
            jax.ShapeDtypeStruct((ROWS, D), f32),
            jax.ShapeDtypeStruct((3, PAD, D), f32),
            jax.ShapeDtypeStruct((3, PAD, D), f32),
            jax.ShapeDtypeStruct((PAD, 128), f32),
        ],
        compiler_params=pltpu.CompilerParams(vmem_limit_bytes=MEMORY),
        name="last",
    )(tokens, gq, gk, gv, grad_one, coeff, weights, rel, index, rel_coeff, gek, gfq, factors, scales)


def devices():
    return lax.axis_size("dp") * lax.axis_size("tensor")


def share_kernel(
    down_ref,
    up_ref,
    last_ref,
    middle_ref,
    early_ref,
    down_out,
    up_out,
    scale_out,
    stage_scr,
    mine_scr,
    land_scr,
    all_scr,
    send_sem,
    land_sem,
    spread_sem,
    all_sem,
):
    count = devices()
    inner = lax.axis_size("tensor")
    me = lax.axis_index("dp") * inner + lax.axis_index("tensor")

    def partner(off):
        other = lax.rem(me + off, count)
        return other, (other // inner, lax.rem(other, inner))

    barrier = pltpu.get_barrier_semaphore()

    @pl.loop(1, count)
    def _(off):
        pl.semaphore_signal(
            barrier, inc=1, device_id=partner(off)[1], device_id_type=pl.DeviceIdType.MESH
        )

    stage_scr[...] = jnp.zeros_like(stage_scr)
    for number in range(6):
        ref = down_ref if number < 3 else up_ref
        for block in range(D // 128):
            at = (number * (D // 128) + block) * RANK
            stage_scr[at : at + RANK, :] = ref[number % 3, :RANK, block * 128 : block * 128 + 128]
    at = 6 * (D // 128) * RANK
    stage_scr[at : at + PAD, :] = last_ref[...] + middle_ref[...]
    mine_scr[...] = stage_scr[...].astype(bf16).reshape(count, PAD, 128)
    pl.semaphore_wait(barrier, count - 1)

    def first(off):
        other, where = partner(off)
        return pltpu.make_async_remote_copy(
            src_ref=mine_scr.at[other],
            dst_ref=land_scr.at[off],
            send_sem=send_sem.at[off],
            recv_sem=land_sem.at[off],
            device_id=where,
            device_id_type=pl.DeviceIdType.MESH,
        )

    def second(off):
        other, where = partner(off)
        return pltpu.make_async_remote_copy(
            src_ref=all_scr.at[me],
            dst_ref=all_scr.at[me],
            send_sem=spread_sem.at[off],
            recv_sem=all_sem.at[off],
            device_id=where,
            device_id_type=pl.DeviceIdType.MESH,
        )

    def second_arrival(off):
        origin = lax.rem(me + count - off, count)
        return pltpu.make_async_remote_copy(
            src_ref=all_scr.at[origin],
            dst_ref=all_scr.at[origin],
            send_sem=spread_sem.at[off],
            recv_sem=all_sem.at[off],
            device_id=partner(off)[1],
            device_id_type=pl.DeviceIdType.MESH,
        )

    @pl.loop(1, count)
    def _(off):
        first(off).start()

    land_scr[0] = mine_scr[me]

    @pl.loop(1, count)
    def _(off):
        first(off).wait_recv()

    all_scr[me] = jnp.sum(land_scr[...].astype(f32), axis=0).astype(bf16)

    @pl.loop(1, count)
    def _(off):
        second(off).start()

    for index, place in ((0, 3), (2, 4)):
        down_out[place] = early_ref[index]
        up_out[place] = early_ref[index + 1]

    @pl.loop(1, count)
    def _(off):
        second_arrival(off).wait_recv()

    stage_scr[...] = all_scr[...].astype(f32).reshape(count * PAD, 128)
    for number in range(6):
        ref = down_out if number < 3 else up_out
        for block in range(D // 128):
            at = (number * (D // 128) + block) * RANK
            ref[number % 3, :, block * 128 : block * 128 + 128] = stage_scr[at : at + RANK, :]
    at = 6 * (D // 128) * RANK
    scale_out[...] = stage_scr[at : at + PAD, :].T[:6, :RANK]

    @pl.loop(1, count)
    def _(off):
        first(off).wait_send()
        second(off).wait_send()


def share(down, up, last_scale, middle_scale, early):
    count = devices()
    factor = jax.ShapeDtypeStruct((5, RANK, D), f32)
    return pl.pallas_call(
        share_kernel,
        in_specs=[pl.BlockSpec(memory_space=pltpu.VMEM)] * 5,
        out_specs=[pl.BlockSpec(memory_space=pltpu.VMEM)] * 3,
        out_shape=[factor, factor, jax.ShapeDtypeStruct((6, RANK), f32)],
        scratch_shapes=[
            pltpu.VMEM((count * PAD, 128), f32),
            pltpu.VMEM((count, PAD, 128), bf16),
            pltpu.VMEM((count, PAD, 128), bf16),
            pltpu.VMEM((count, PAD, 128), bf16),
        ]
        + [pltpu.SemaphoreType.DMA((count,))] * 4,
        compiler_params=pltpu.CompilerParams(
            collective_id=0, has_side_effects=True, vmem_limit_bytes=MEMORY
        ),
        name="share",
    )(down, up, last_scale, middle_scale, early)


def on_device(
    tokens,
    qkv_weight,
    out_weight,
    in_weight,
    back_weight,
    rel_embed,
    gain_one,
    shift_one,
    gain_two,
    shift_two,
    adapt_down,
    adapt_up,
    hidden_up,
    hidden_down,
    adapt_scale,
    seq_lengths,
    seq_counts,
    rel_bucket,
    out_grad,
):
    factors = jnp.pad(
        jnp.concatenate([adapt_down, adapt_up, hidden_up[None], hidden_down[None]], axis=0),
        ((0, 0), (0, PAD - RANK), (0, 0)),
    )
    scales = jnp.pad(adapt_scale.T, ((0, PAD - RANK), (0, 128 - 6)))
    index_rows = jnp.pad(
        jnp.stack([rel_bucket[::-1], rel_bucket]), ((0, 0), (0, 1)), constant_values=-1
    )
    norms = jnp.stack([gain_one, shift_one, gain_two, shift_two])
    packed = lax.all_gather(
        pack_weights(in_weight, back_weight, factors, scales), "tensor", axis=0
    )
    q, k, v, ek, eq, fq, weights, coeff, rel_coeff = project(
        tokens, qkv_weight, out_weight, rel_embed, index_rows, factors, scales
    )
    context, p1, p2, p3 = attend_forward(seq_lengths, seq_counts, q, k, v, ek, eq)
    mixed, grad_one, context_grad, small, hidden, middle_scale = middle(
        seq_lengths, seq_counts, tokens, context, out_grad, weights, packed, factors, scales, norms
    )
    chunks = packed.shape[0]
    small, hidden = lax.psum(
        (small[:, :RANK], hidden[:, :RANK].reshape(2, chunks, RANK, D)), ("dp", "tensor")
    )
    hidden = hidden[:, lax.axis_index("tensor")]
    gq, gk, gv, gek, gfq = attend_backward(q, k, v, context_grad, ek, fq, p1, p2, p3)
    in_grad, down, up, last_scale = last(
        tokens, gq, gk, gv, grad_one, coeff, weights, rel_embed, index_rows, rel_coeff, gek, gfq, factors, scales
    )
    down_grad, up_grad, scale_grad = share(down, up, last_scale, middle_scale, small)
    return (mixed, in_grad, down_grad, up_grad, hidden[0], hidden[1], scale_grad)


def solution(mesh):
    rows = P(("dp", "tensor"), None)
    return jax.shard_map(
        on_device,
        mesh=mesh,
        in_specs=(
            rows,
            P(),
            P(),
            P(None, "tensor"),
            P("tensor", None),
            P(),
            P(),
            P(),
            P(),
            P(),
            P(),
            P(),
            P(None, "tensor"),
            P(None, "tensor"),
            P(),
            rows,
            rows,
            P(),
            rows,
        ),
        out_specs=(rows, rows, P(), P(), P(None, "tensor"), P(None, "tensor"), P()),
        check_vma=False,
    )
```

time: 2710 us -> 334 us (0.12)
  local copies, waits for them, and re-layouts: 1610 us -> 8.8 us
  matrix products: 509 us -> 0 us
  waiting for transfers between devices: 475 us -> 0.06 us
  Pallas kernels: 0 us -> 308 us
  other arithmetic: 73.1 us -> 2.39 us
    reshape x72 -> x0, local copies, waits for them, and re-layouts: 508 us -> none  [rel_shift(): return window.reshape(heads, LEN3, 2 * LEN3 - 1)[:, :, :LEN3]]
    dot_general x230 -> x0, matrix products: 484 us -> none  [the longest x24 66.1 us: pair_scores(): jnp.einsum('ihd,jhd->hij', query_per_head, head_key, preferred_element_ty...]
    while x497 -> x0, local copies, waits for them, and re-layouts: 344 us -> none
    slice x96 -> x0, local copies, waits for them, and re-layouts: 318 us -> none  [the longest x48 279 us: rel_shift(): window = flat[:, LEN3 - 1:LEN3 - 1 + LEN3 * (2 * LEN3 - 1)]]
    pallas_call x0 -> x7, Pallas kernels: none -> 308 us  [the longest x1 130 us: attend_backward(): pl.pallas_call(backward_kernel, grid=(H // 2, 2), in_specs=[PAIR_SPEC] *...]
    psum x3 -> x1, waiting for transfers between devices: 289 us -> 0.02 us  [on_device(): lax.psum((small[:, :RANK], hidden[:, :RANK].reshape(2, chunks, RANK, D)),...]
    dynamic_update_slice x60 -> x0, local copies, waits for them, and re-layouts: 165 us -> none  [the longest x12 35.1 us: backward_piece(): lax.dynamic_update_slice(grad_key, new_key.reshape(LEN3, 2 * DH), (start_...]
    dynamic_slice x192 -> x0, local copies, waits for them, and re-layouts: 139 us -> none  [the longest x96 87 us: take_pair(): lax.dynamic_slice(source, (start_row, start_col), (LEN3, 2 * DH))]
  transfers between devices with their start and end apart: 7 -> 2, of which waited for: 7 -> 0; matrix products, arithmetic and copies ran while one was open for 3% -> 0% of each run, Pallas kernels for 0% -> 71%
where the time goes in v1:
time: 334 us
  Pallas kernels  308 us (92%)
  between operations  14.2 us (4%)
  local copies, waits for them, and re-layouts  8.8 us (3%)
    pallas_call x1, Pallas kernels, attend_backward(): pl.pallas_call(backward_kernel, grid=(H // 2, 2), in_specs=[PAIR_SPEC] *...  130 us
    pallas_call x1, Pallas kernels, attend_forward(): pl.pallas_call(forward_kernel, grid=(H // 2, 2), in_specs=[pl.BlockSpec(m...  73.5 us
    pallas_call x1, Pallas kernels, middle(): pl.pallas_call(middle_kernel, grid=(ROWS // BLOCK,), in_specs=[pl.BlockSp...  47.3 us
    pallas_call x1, Pallas kernels, share(): pl.pallas_call(share_kernel, in_specs=[pl.BlockSpec(memory_space=pltpu.VM...  20.9 us
    pallas_call x1, Pallas kernels, project(): pl.pallas_call(project_kernel, grid=(ROWS // BLOCK,), in_specs=[tile, who...  16.4 us
    pallas_call x1, Pallas kernels, last(): pl.pallas_call(last_kernel, grid=(ROWS // BLOCK,), in_specs=[tile] * 5 +...  16.2 us
  transfers between devices with their start and end apart: 2, of which 0 were waited for; matrix products, arithmetic and copies ran while one was open for 0% of the time, Pallas kernels for 71%

profile of v1, /device:TPU:0, one launch (start us, length us, event | category | flops | bytes accessed | tf_op | source)
XLA Modules:
  0.0 333.6 jit_solution(784992671827271461)
XLA Ops:
  7.2 0.0 all-gather.3.cloned.1.call-start
  7.2 0.8 copy.26
  8.0 0.6 pad.14.scale_ref
  8.6 1.8 fusion.6.factor_ref
  10.3 4.0 %pack_weights.1 = bf16[1568,768]{1,0:T(8,128)(2,1)} custom-call(bf16[768,768]{1,0:T(8,128)(2,1)} %in_ref.1, bf16[768,768]{1,0:T(8,128)(2,1)} %back_ref.1, bf16[12,16,768]{2,1,0:T(8,128)(2,1)} %fusion.6.factor_ref, f32[16,128]{1,0:T(8,128)} %pad.14.scale_ref), custom_call_target="tpu_custom_call" | custom-call | tf_op jit(solution)/shard_map/pack_weights/pallas_call | solution.py:74
  14.3 0.0 copy-start
  14.3 0.0 copy-start.1
  14.3 0.0 copy-start.2
  14.3 0.0 copy-start.3
  14.3 0.0 copy-start.4
  14.4 0.0 all-gather.3.cloned.1.call-update
  14.4 0.0 all-reduce.6.cloned.1.call-start
  14.4 0.6 copy-done
  15.0 0.1 reverse
  15.1 0.1 slice.18
  15.2 0.0 copy-done.1
  15.2 0.0 copy-done.2
  15.2 0.0 copy-done.3
  15.2 0.0 copy-done.4
  15.3 0.6 pad.12.index_ref
  15.9 16.4 %project.1 = (bf16[1024,768]{1,0:T(8,128)(2,1)}, bf16[1024,768]{1,0:T(8,128)(2,1)}, bf16[1024,768]{1,0:T(8,128)(2,1)}, bf16[1024,768]{1,0:T(8,128)(2,1)}, bf16[1...) custom-call(bf16[1024,768]{1,0:T(8,128)(2,1)} %tokens_ref.5, ...), custom_call_target="tpu_custom_call" | custom-call | tf_op jit(solution)/shard_map/project/pallas_call | solution.py:135
  32.2 73.5 %attention_forward.1 = (bf16[1024,768]{1,0:T(8,128)(2,1)}, bf16[12,256,128]{2,1,0:T(8,128)(2,1)}, bf16[12,256,256]{2,1,0:T(8,128)(2,1)}, bf16[12,512,512]{2,1,0:T(8,128)(2,1)}) custom-call(s32[1,4]{1,0:T(1,128)} %lengths_ref.3, s32[1,3]{1,0:T(1,128)} %counts_ref.3, bf16[1024,768]{1,0:T(8,128)(2,1)} %get-tuple-element.38.q_ref, ...), custom_call_target="tpu_custom_call" | custom-call | tf_op jit(solution)/shard_map/attention_forward/pallas_call | solution.py:253
  105.7 0.6 pad_maximum_fusion.norm_ref
  106.3 0.0 all-gather.3.cloned.1.call-done
  106.3 47.3 %middle.1 = (bf16[1024,768]{1,0:T(8,128)(2,1)}, f32[1024,768]{1,0:T(8,128)}, bf16[1024,768]{1,0:T(8,128)(2,1)}, f32[4,16,768]{2,1,0:T(8,128)}, f32[8,16,768]{2,1,0:T(8,128)}, /*index=5*/f32[16,128]{1,0:T(8,128)}) custom-call(s32[1,4]{1,0:T(1,128)} %lengths_ref.3, s32[1,3]{1,0:T(1,128)} %counts_ref.3, bf16[1024,768]{1,0:T(8,128)(2,1)} %tokens_ref.5, ...), custom_call_target="tpu_custom_call" | custom-call | tf_op jit(solution)/shard_map/middle/pallas_call | solution.py:485
  153.6 0.0 all-reduce.6.cloned.1.call-update
  153.7 129.9 %attention_backward.1 = (bf16[1024,768]{1,0:T(8,128)(2,1)}, bf16[1024,768]{1,0:T(8,128)(2,1)}, bf16[1024,768]{1,0:T(8,128)(2,1)}, f32[768,1024]{1,0:T(8,128)}, f32[768,1024]{1,0:T(8,128)}) custom-call(bf16[1024,768]{1,0:T(8,128)(2,1)} %get-tuple-element.38.q_ref, bf16[1024,768]{1,0:T(8,128)(2,1)} %get-tuple-element.39.k_ref, ...), custom_call_target="tpu_custom_call" | custom-call | tf_op jit(solution)/shard_map/attention_backward/pallas_call | solution.py:348
  283.6 16.2 %last.1 = (f32[1024,768]{1,0:T(8,128)}, f32[3,16,768]{2,1,0:T(8,128)}, f32[3,16,768]{2,1,0:T(8,128)}, f32[16,128]{1,0:T(8,128)}) custom-call(bf16[1024,768]{1,0:T(8,128)(2,1)} %tokens_ref.5, bf16[1024,768]{1,0:T(8,128)(2,1)} %get-tuple-element.51.gq_ref, bf16[1024,768]{1,0:T(8,128)(2,1)} %get-tuple-element.52.gk_ref, ...), custom_call_target="tpu_custom_call" | custom-call | tf_op jit(solution)/shard_map/last/pallas_call | solution.py:575
  299.8 0.0 all-reduce.6.cloned.1.call-done
  299.8 20.9 %share.1 = (f32[5,12,768]{2,1,0:T(8,128)}, f32[5,12,768]{2,1,0:T(8,128)}, f32[6,12]{1,0:T(8,128)}) custom-call(f32[3,16,768]{2,1,0:T(8,128)} %get-tuple-element.60.down_ref, f32[3,16,768]{2,1,0:T(8,128)} %get-tuple-element.61.up_ref, f32[16,128]{1,0:T(8,128)} %get-tuple-element.62.last_ref, f32[16,128]{1,0:T(8,128)} %get-tuple-element.63.middle_ref, ...), custom_call_target="tpu_custom_call" | custom-call | tf_op jit(solution)/shard_map/share/pallas_call | solution.py:726
  320.7 1.5 dynamic-slice_bitcast_fusion
  322.2 1.7 copy.32
  323.8 1.7 copy.33
  325.5 1.3 copy.34
  (5 shorter events, 0.0 us)
Async XLA Ops:
  7.2 99.2 %all-gather.3.cloned.1.call-start = ((), (), s32[]{:S(2)}) async-start(), calls=%async_computation | async-start | bytes 12042240 | tf_op jit(solution)/shard_map/all_gather | solution.py:775
  14.3 0.7 copy-start
  14.3 0.8 copy-start.1
  14.3 0.8 copy-start.2
  14.3 0.9 copy-start.3
  14.3 0.9 copy-start.4
  14.4 285.5 %all-reduce.6.cloned.1.call-start = ((), (), s32[]{:S(2)}) async-start(), calls=%async_computation.1 | async-start | bytes 1179648 | tf_op jit(solution)/shard_map/psum | solution.py:786
Sparse Core Ops, SparseCore 0:
  14.5 68.1 all-gather.2
  153.8 131.6 all-reduce.5

commit v2 on v1

--- a/solution.py
+++ b/solution.py
@@ -91,8 +91,9 @@
     k_ref,
     v_ref,
     ek_ref,
-    eq_ref,
     fq_ref,
+    ekt_ref,
+    eqt_ref,
     merged_ref,
     coeff_ref,
     rel_coeff_ref,
@@ -120,9 +121,13 @@
         ref[...] = dot_nn(tokens, merged_ref[member]).astype(bf16)
         coeff_ref[member] = dot_nt(factor_ref[member], tokens)
     bucket = lax.broadcasted_iota(jnp.int32, (2 * SPAN, BLOCK), 0)
-    for ref, row, member in ((ek_ref, 0, 1), (eq_ref, 0, 0), (fq_ref, 1, 0)):
-        chosen = jnp.where(bucket == index_ref[row : row + 1, :], 1.0, 0.0).astype(bf16)
-        ref[...] = dot_tn(chosen, pos_scr[member]).astype(bf16)
+    back, forth = (
+        jnp.where(bucket == index_ref[row : row + 1, :], 1.0, 0.0).astype(bf16) for row in range(2)
+    )
+    ek_ref[...] = dot_tn(back, pos_scr[1]).astype(bf16)
+    fq_ref[...] = dot_tn(forth, pos_scr[0]).astype(bf16)
+    ekt_ref[...] = dot_tn(pos_scr[1], back).astype(bf16)
+    eqt_ref[...] = dot_tn(pos_scr[0], back).astype(bf16)
 
 
 def whole(*shape):
@@ -144,13 +149,15 @@
             whole(12, PAD, D),
             whole(PAD, 128),
         ],
-        out_specs=[tile] * 6
+        out_specs=[tile] * 5
+        + [pl.BlockSpec((D, BLOCK), lambda i: (0, i))] * 2
         + [
             whole(4, D, D),
             pl.BlockSpec((3, PAD, BLOCK), lambda i: (0, 0, i)),
             whole(2, PAD, 2 * SPAN),
         ],
-        out_shape=[rows] * 6
+        out_shape=[rows] * 5
+        + [jax.ShapeDtypeStruct((D, OFFSETS), bf16)] * 2
         + [
             jax.ShapeDtypeStruct((4, D, D), bf16),
             jax.ShapeDtypeStruct((3, PAD, ROWS), f32),
@@ -173,25 +180,56 @@
     return jnp.where(lane // DH == member, 1.0, 0.0).astype(bf16)
 
 
+def each_head(rows):
+    return jnp.concatenate([rows * head_lanes(0), rows * head_lanes(1)], axis=0)
+
+
+def own_lanes(stacked):
+    lane = lax.broadcasted_iota(jnp.int32, (TILE, PAIR), 1)
+    return jnp.where(lane < DH, stacked[:TILE], stacked[TILE:])
+
+
+def lane_and_row():
+    lane = lax.broadcasted_iota(jnp.int32, (8, 128), 1)
+    return lane, lax.broadcasted_iota(jnp.int32, (8, 128), 0)
+
+
+def turn(block, shift):
+    return pltpu.roll(block, shift % 128, 1, stride=1, stride_axis=0)
+
+
 def skew(table, length):
-    return pltpu.roll(table, length + 1, 1, stride=1, stride_axis=0)[:, :length]
-
-
-def unskew(scores):
-    wide = jnp.concatenate([scores, jnp.zeros((TILE, TILE), f32)], axis=1)
-    return pltpu.roll(wide, 0, 1, stride=1, stride_axis=0)
-
-
-def add_pair(ref, member, start, value):
-    here = pl.ds(start, value.shape[0])
-
-    @pl.when(member == 0)
-    def _():
-        ref[here, :] = value
-
-    @pl.when(member == 1)
-    def _():
-        ref[here, :] = ref[here, :] + value
+    lane, row = lane_and_row()
+    count = length // 128
+    done = []
+    for at in range(0, TILE, 8):
+        blocks = [table[at : at + 8, 128 * c : 128 * c + 128] for c in range(count + 1)]
+        blocks[0] = jnp.where(lane + row >= 127 - at, blocks[0], blocks[count])
+        moved = [turn(block, at + 1) for block in blocks[:count]]
+        if count > 1:
+            inside = lane - row <= at
+            moved = [
+                jnp.where(inside, moved[c], moved[(c + 1) % count]) for c in range(count)
+            ]
+        done.append(jnp.concatenate(moved, axis=1))
+    return jnp.concatenate(done, axis=0)
+
+
+def unskew(scores, length):
+    lane, row = lane_and_row()
+    zero = jnp.zeros((8, 128), f32)
+    done = []
+    for at in range(0, TILE, 8):
+        moved = [
+            turn(scores[at : at + 8, 128 * c : 128 * c + 128], at) for c in range(length // 128)
+        ]
+        before = lane - row < at
+        done.append(
+            jnp.concatenate(
+                [jnp.where(before, x, y) for x, y in zip([zero] + moved, moved + [zero])], axis=1
+            )
+        )
+    return jnp.concatenate(done, axis=0)
 
 
 def forward_kernel(
@@ -208,56 +246,69 @@
     p3_ref,
     shift_scr,
 ):
-    member = pl.program_id(1)
-    mask = head_lanes(member)
     eye = unit_matrix(False)
     anti = unit_matrix(True)
     factor = (3.0 * DH) ** -0.5
     counts = live_counts(lengths_ref, counts_ref)
     for slot, (start, length) in enumerate(SLOTS):
-        keys = k_ref[start : start + length, :] * mask
-        values = v_ref[start : start + length, :] * mask
+        keys = k_ref[start : start + length, :]
+        values = v_ref[start : start + length, :]
         live = lax.broadcasted_iota(jnp.int32, (1, length), 1) < counts[slot]
         for t in range(length // TILE):
             low = LEN3 - TILE - TILE * t
-            table = dot_nt(keys[t * TILE : (t + 1) * TILE], eq_ref[low : low + length + TILE, :])
-            shift_scr[t * TILE : (t + 1) * TILE, :length] = skew(table, length).astype(bf16)
+            here = keys[t * TILE : (t + 1) * TILE]
+            table = dot_nn(each_head(here), eq_ref[:, low : low + length + TILE])
+            for member in range(2):
+                shift_scr[member, start + t * TILE : start + (t + 1) * TILE, :length] = skew(
+                    table[member * TILE : (member + 1) * TILE], length
+                ).astype(bf16)
         for t in range(length // TILE):
             low = LEN3 - TILE - TILE * t
             row = start + t * TILE
-            queries = q_ref[row : row + TILE, :] * mask
-            relative = skew(dot_nt(queries, ek_ref[low : low + length + TILE, :]), length)
-            left = jnp.concatenate([queries, eye], axis=1)
-            right = jnp.concatenate(
-                [keys, shift_scr[:length, t * TILE : (t + 1) * TILE]], axis=1
-            )
-            scores = jnp.where(live, (dot_nt(left, right) + relative) * factor, masked_score)
-            weights = jnp.exp(scores - jnp.max(scores, axis=1, keepdims=True))
-            prob = (weights * (1.0 / jnp.sum(weights, axis=1, keepdims=True))).astype(bf16)
-            add_pair(context_ref, member, row, dot_nn(prob, values).astype(bf16))
-            turned = dot_nn(anti, prob).astype(bf16)
-            if length == LEN1:
-                p1_ref[0, row : row + TILE, :] = turned
-            elif length == LEN3:
-                p3_ref[0, t * TILE : (t + 1) * TILE, :] = turned
-            else:
-                p2_ref[0, t * TILE : (t + 1) * TILE, :] = turned
-
-
-PAIR_SPEC = pl.BlockSpec((ROWS, PAIR), lambda p, e: (0, p))
+            queries = each_head(q_ref[row : row + TILE, :])
+            table = dot_nn(queries, ek_ref[:, low : low + length + TILE])
+            probs = []
+            for member in range(2):
+                mine = slice(member * TILE, (member + 1) * TILE)
+                left = jnp.concatenate([queries[mine], eye], axis=1)
+                shifted = shift_scr[
+                    member, start : start + length, t * TILE : (t + 1) * TILE
+                ]
+                right = jnp.concatenate([keys, shifted], axis=1)
+                scores = dot_nt(left, right) + skew(table[mine], length)
+                scores = jnp.where(live, scores * factor, masked_score)
+                weights = jnp.exp(scores - jnp.max(scores, axis=1, keepdims=True))
+                prob = weights * (1.0 / jnp.sum(weights, axis=1, keepdims=True))
+                probs.append(prob.astype(bf16))
+            context = dot_nn(jnp.concatenate(probs, axis=0), values)
+            context_ref[row : row + TILE, :] = own_lanes(context).astype(bf16)
+            for member in range(2):
+                turned = dot_nn(anti, probs[member]).astype(bf16)
+                if length == LEN1:
+                    p1_ref[member, row : row + TILE, :] = turned
+                elif length == LEN3:
+                    p3_ref[member, t * TILE : (t + 1) * TILE, :] = turned
+                else:
+                    p2_ref[member, t * TILE : (t + 1) * TILE, :] = turned
+
+
+PAIR_SPEC = pl.BlockSpec((ROWS, PAIR), lambda p: (0, p))
+TABLE_SPEC = pl.BlockSpec((PAIR, OFFSETS), lambda p: (p, 0))
 PROB_SIZES = ((256, 128), (256, 256), (512, 512))
-PROB_SPECS = [pl.BlockSpec((1, *size), lambda p, e: (2 * p + e, 0, 0)) for size in PROB_SIZES]
+PROB_SPECS = [pl.BlockSpec((2, *size), lambda p: (p, 0, 0)) for size in PROB_SIZES]
 
 
 def attend_forward(lengths, counts, q, k, v, ek, eq):
     return pl.pallas_call(
         forward_kernel,
-        grid=(H // 2, 2),
-        in_specs=[pl.BlockSpec(memory_space=pltpu.SMEM)] * 2 + [PAIR_SPEC] * 5,
+        grid=(H // 2,),
+        in_specs=[pl.BlockSpec(memory_space=pltpu.SMEM)] * 2
+        + [PAIR_SPEC] * 3
+        + [TABLE_SPEC] * 2,
         out_specs=[PAIR_SPEC] + PROB_SPECS,
         out_shape=[jax.ShapeDtypeStruct((ROWS, D), bf16)]
         + [jax.ShapeDtypeStruct((H, *size), bf16) for size in PROB_SIZES],
-        scratch_shapes=[pltpu.VMEM((LEN3, LEN3), bf16)],
+        scratch_shapes=[pltpu.VMEM((2, ROWS, LEN3), bf16)],
         compiler_params=pltpu.CompilerParams(vmem_limit_bytes=MEMORY),
         name="attention_forward",
     )(lengths, counts, q, k, v, ek, eq)
@@ -282,79 +333,91 @@
     turned_scr,
     values_scr,
 ):
-    member = pl.program_id(1)
-    mask = head_lanes(member)
     eye = unit_matrix(False)
     anti = unit_matrix(True)
     factor = (3.0 * DH) ** -0.5
-
-    @pl.when(member == 0)
-    def _():
-        gek_ref[...] = jnp.zeros_like(gek_ref)
-        gfq_ref[...] = jnp.zeros_like(gfq_ref)
-
+    gek_ref[...] = jnp.zeros_like(gek_ref)
+    gfq_ref[...] = jnp.zeros_like(gfq_ref)
     for start, length in SLOTS:
         count = length // TILE
-        keys = k_ref[start : start + length, :] * mask
-        values = v_ref[start : start + length, :] * mask
+        keys = k_ref[start : start + length, :]
+        values = v_ref[start : start + length, :]
         value_grad = jnp.zeros((PAIR, length), f32)
         for t in range(count):
             low = LEN3 - TILE - TILE * t
             row = start + t * TILE
-            queries = dot_nn(anti, q_ref[row : row + TILE, :] * mask).astype(bf16)
-            grads = dot_nn(anti, g_ref[row : row + TILE, :] * mask).astype(bf16)
-            if length == LEN1:
-                prob = p1_ref[0, row : row + TILE, :]
-            elif length == LEN3:
-                prob = p3_ref[0, t * TILE : (t + 1) * TILE, :]
-            else:
-                prob = p2_ref[0, t * TILE : (t + 1) * TILE, :]
+            place = start + (count - 1 - t) * TILE
+            both = jnp.concatenate([q_ref[row : row + TILE, :], g_ref[row : row + TILE, :]], axis=1)
+            both = dot_nn(anti, both).astype(bf16)
+            turned_scr[place : place + TILE, :] = both[:, :PAIR]
+            queries = each_head(both[:, :PAIR])
+            grads = each_head(both[:, PAIR:])
             grad_prob = dot_nt(grads, values)
-            wide = prob.astype(f32)
-            delta = jnp.sum(wide * grad_prob, axis=1, keepdims=True)
-            raw = (wide * ((grad_prob - delta) * factor)).astype(bf16)
-            place = (count - 1 - t) * TILE
-            grad_scr[place : place + TILE, :length] = raw
-            turned_scr[place : place + TILE, :] = queries
-            spread = unskew(raw.astype(f32)).astype(bf16)
-            window = ek_ref[low : low + length + TILE, :] * mask
-            query_grad = dot_nn(
-                jnp.concatenate([raw, spread], axis=1), jnp.concatenate([keys, window], axis=0)
+            probs, raws, spreads = [], [], []
+            for member in range(2):
+                if length == LEN1:
+                    prob = p1_ref[member, row : row + TILE, :]
+                elif length == LEN3:
+                    prob = p3_ref[member, t * TILE : (t + 1) * TILE, :]
+                else:
+                    prob = p2_ref[member, t * TILE : (t + 1) * TILE, :]
+                mine = grad_prob[member * TILE : (member + 1) * TILE]
+                wide = prob.astype(f32)
+                delta = jnp.sum(wide * mine, axis=1, keepdims=True)
+                raw = (wide * ((mine - delta) * factor)).astype(bf16)
+                grad_scr[member, place : place + TILE, :length] = raw
+                probs.append(prob)
+                raws.append(raw)
+                spreads.append(unskew(raw.astype(f32), length).astype(bf16))
+            raw = jnp.concatenate(raws, axis=0)
+            spread = jnp.concatenate(spreads, axis=0)
+            query_grad = own_lanes(
+                dot_nn(
+                    jnp.concatenate([raw, spread], axis=1),
+                    jnp.concatenate([keys, ek_ref[low : low + length + TILE, :]], axis=0),
+                )
             )
-            add_pair(gq_ref, member, row, dot_nn(anti, query_grad.astype(bf16)).astype(bf16))
+            gq_ref[row : row + TILE, :] = dot_nn(anti, query_grad.astype(bf16)).astype(bf16)
             gek_ref[:, low : low + length + TILE] += dot_tn(queries, spread)
-            value_grad = value_grad + dot_tn(grads, prob)
+            value_grad = value_grad + dot_tn(grads, jnp.concatenate(probs, axis=0))
         values_scr[:, start : start + length] = value_grad
-        turned = turned_scr[:length, :]
+        turned = turned_scr[start : start + length, :]
         for t in range(count):
             low = LEN3 - length + TILE * t
             row = start + t * TILE
-            raw = dot_nt(eye, grad_scr[:length, t * TILE : (t + 1) * TILE])
-            spread = unskew(raw).astype(bf16)
-            window = fq_ref[low : low + length + TILE, :] * mask
-            key_grad = dot_nn(
-                jnp.concatenate([raw.astype(bf16), spread], axis=1),
-                jnp.concatenate([turned, window], axis=0),
+            raws, spreads = [], []
+            for member in range(2):
+                raw = dot_nt(
+                    eye, grad_scr[member, start : start + length, t * TILE : (t + 1) * TILE]
+                )
+                raws.append(raw.astype(bf16))
+                spreads.append(unskew(raw, length).astype(bf16))
+            raw = jnp.concatenate(raws, axis=0)
+            spread = jnp.concatenate(spreads, axis=0)
+            key_grad = own_lanes(
+                dot_nn(
+                    jnp.concatenate([raw, spread], axis=1),
+                    jnp.concatenate([turned, fq_ref[low : low + length + TILE, :]], axis=0),
+                )
             )
-            add_pair(gk_ref, member, row, key_grad.astype(bf16))
+            gk_ref[row : row + TILE, :] = key_grad.astype(bf16)
             gfq_ref[:, low : low + length + TILE] += dot_tn(
-                keys[t * TILE : (t + 1) * TILE], spread
+                each_head(k_ref[row : row + TILE, :]), spread
             )
-    add_pair(gv_ref, member, 0, values_scr[...].T.astype(bf16))
+    gv_ref[...] = values_scr[...].T.astype(bf16)
 
 
 def attend_backward(q, k, v, g, ek, fq, p1, p2, p3):
-    table = pl.BlockSpec((PAIR, OFFSETS), lambda p, e: (p, 0))
     return pl.pallas_call(
         backward_kernel,
-        grid=(H // 2, 2),
+        grid=(H // 2,),
         in_specs=[PAIR_SPEC] * 6 + PROB_SPECS,
-        out_specs=[PAIR_SPEC] * 3 + [table] * 2,
+        out_specs=[PAIR_SPEC] * 3 + [TABLE_SPEC] * 2,
         out_shape=[jax.ShapeDtypeStruct((ROWS, D), bf16)] * 3
         + [jax.ShapeDtypeStruct((D, OFFSETS), f32)] * 2,
         scratch_shapes=[
-            pltpu.VMEM((LEN3, LEN3), bf16),
-            pltpu.VMEM((LEN3, PAIR), bf16),
+            pltpu.VMEM((2, ROWS, LEN3), bf16),
+            pltpu.VMEM((ROWS, PAIR), bf16),
             pltpu.VMEM((PAIR, ROWS), f32),
         ],
         compiler_params=pltpu.CompilerParams(vmem_limit_bytes=MEMORY),
@@ -775,10 +838,10 @@
     packed = lax.all_gather(
         pack_weights(in_weight, back_weight, factors, scales), "tensor", axis=0
     )
-    q, k, v, ek, eq, fq, weights, coeff, rel_coeff = project(
+    q, k, v, ek, fq, ekt, eqt, weights, coeff, rel_coeff = project(
         tokens, qkv_weight, out_weight, rel_embed, index_rows, factors, scales
     )
-    context, p1, p2, p3 = attend_forward(seq_lengths, seq_counts, q, k, v, ek, eq)
+    context, p1, p2, p3 = attend_forward(seq_lengths, seq_counts, q, k, v, ekt, eqt)
     mixed, grad_one, context_grad, small, hidden, middle_scale = middle(
         seq_lengths, seq_counts, tokens, context, out_grad, weights, packed, factors, scales, norms
     )

time: 334 us -> 290 us (0.87)
  Pallas kernels: 308 us -> 195 us
  waiting for transfers between devices: 0.06 us -> 69.2 us
    pallas_call x2, Pallas kernels: 203 us -> 91.7 us  [the longest x1 53.4 us: attend_backward(): pl.pallas_call(backward_kernel, grid=(H // 2,), in_specs=[PAIR_SPEC] * 6...]
    psum x1, waiting for transfers between devices: 0.02 us -> 58.7 us  [on_device(): lax.psum((small[:, :RANK], hidden[:, :RANK].reshape(2, chunks, RANK, D)),...]
    all_gather x1, waiting for transfers between devices: 0.01 us -> 10.5 us  [on_device(): lax.all_gather(pack_weights(in_weight, back_weight, factors, scales), 'te...]
  transfers between devices with their start and end apart: 2 -> 2, of which waited for: 0 -> 2; matrix products, arithmetic and copies ran while one was open for 0% -> 0% of each run, Pallas kernels for 71% -> 43%
where the time goes in v2:
time: 290 us; the launch traced here: 289 us
  Pallas kernels  195 us (67%)
  waiting for transfers between devices  69.2 us (24%)
  between operations  14.1 us (5%)
  local copies, waits for them, and re-layouts  8.8 us (3%)
    psum x1, waiting for transfers between devices, on_device(): lax.psum((small[:, :RANK], hidden[:, :RANK].reshape(2, chunks, RANK, D)),...  58.7 us
    pallas_call x1, Pallas kernels, attend_backward(): pl.pallas_call(backward_kernel, grid=(H // 2,), in_specs=[PAIR_SPEC] * 6...  53.4 us
    pallas_call x1, Pallas kernels, middle(): pl.pallas_call(middle_kernel, grid=(ROWS // BLOCK,), in_specs=[pl.BlockSp...  47.1 us
    pallas_call x1, Pallas kernels, attend_forward(): pl.pallas_call(forward_kernel, grid=(H // 2,), in_specs=[pl.BlockSpec(mem...  38.4 us
    pallas_call x1, Pallas kernels, share(): pl.pallas_call(share_kernel, in_specs=[pl.BlockSpec(memory_space=pltpu.VM...  18.4 us
    pallas_call x1, Pallas kernels, project(): pl.pallas_call(project_kernel, grid=(ROWS // BLOCK,), in_specs=[tile, who...  17.2 us
    pallas_call x1, Pallas kernels, last(): pl.pallas_call(last_kernel, grid=(ROWS // BLOCK,), in_specs=[tile] * 5 +...  16.3 us
    all_gather x1, waiting for transfers between devices, on_device(): lax.all_gather(pack_weights(in_weight, back_weight, factors, scales), 'te...  10.5 us
  transfers between devices with their start and end apart: 2, of which 2 were waited for; matrix products, arithmetic and copies ran while one was open for 0% of the time, Pallas kernels for 43%

profile of v2, /device:TPU:0, one launch (start us, length us, event | category | flops | bytes accessed | tf_op | source)
XLA Modules:
  0.0 289.4 jit_solution(3559908753528724975)
XLA Ops:
  7.2 0.0 all-gather.3.cloned.1.call-start
  7.2 0.8 copy.26
  8.0 0.6 pad.14.scale_ref
  8.6 1.8 fusion.6.factor_ref
  10.3 4.0 %pack_weights.1 = bf16[1568,768]{1,0:T(8,128)(2,1)} custom-call(bf16[768,768]{1,0:T(8,128)(2,1)} %in_ref.1, bf16[768,768]{1,0:T(8,128)(2,1)} %back_ref.1, bf16[12,16,768]{2,1,0:T(8,128)(2,1)} %fusion.6.factor_ref, f32[16,128]{1,0:T(8,128)} %pad.14.scale_ref), custom_call_target="tpu_custom_call" | custom-call | tf_op jit(solution)/shard_map/pack_weights/pallas_call | solution.py:74
  14.3 0.0 copy-start
  14.3 0.0 copy-start.1
  14.3 0.0 copy-start.2
  14.3 0.0 copy-start.3
  14.3 0.0 copy-start.4
  14.4 0.0 all-gather.3.cloned.1.call-update
  14.4 0.0 all-reduce.6.cloned.1.call-start
  14.4 0.6 copy-done
  15.0 0.1 reverse
  15.1 0.1 slice.18
  15.2 0.0 copy-done.1
  15.2 0.0 copy-done.2
  15.2 0.0 copy-done.3
  15.2 0.0 copy-done.4
  15.3 0.6 pad.12.index_ref
  15.9 17.2 %project.1 = (bf16[1024,768]{1,0:T(8,128)(2,1)}, bf16[1024,768]{1,0:T(8,128)(2,1)}, bf16[1024,768]{1,0:T(8,128)(2,1)}, bf16[1024,768]{1,0:T(8,128)(2,1)}, bf16[1...) custom-call(bf16[1024,768]{1,0:T(8,128)(2,1)} %tokens_ref.5, ...), custom_call_target="tpu_custom_call" | custom-call | tf_op jit(solution)/shard_map/project/pallas_call | solution.py:140
  33.1 38.4 %attention_forward.1 = (bf16[1024,768]{1,0:T(8,128)(2,1)}, bf16[12,256,128]{2,1,0:T(8,128)(2,1)}, bf16[12,256,256]{2,1,0:T(8,128)(2,1)}, bf16[12,512,512]{2,1,0:T(8,128)(2,1)}) custom-call(s32[1,4]{1,0:T(1,128)} %lengths_ref.3, s32[1,3]{1,0:T(1,128)} %counts_ref.3, bf16[1024,768]{1,0:T(8,128)(2,1)} %get-tuple-element.39.q_ref, ...), custom_call_target="tpu_custom_call" | custom-call | tf_op jit(solution)/shard_map/attention_forward/pallas_call | solution.py:302
  71.5 0.6 pad_maximum_fusion.norm_ref
  72.1 10.5 %all-gather.3.cloned.1.call-done = bf16[6272,768]{1,0:T(8,128)(2,1)} async-done(((bf16[1568,768]{1,0:T(8,128)(2,1)}), bf16[6272,768]{1,0:T(8,128)(2,1)}) %all-gather.3.cloned.1.call-update) | async-done | bytes 9633808 | tf_op jit(solution)/shard_map/all_gather | solution.py:838
  82.6 47.1 %middle.1 = (bf16[1024,768]{1,0:T(8,128)(2,1)}, f32[1024,768]{1,0:T(8,128)}, bf16[1024,768]{1,0:T(8,128)(2,1)}, f32[4,16,768]{2,1,0:T(8,128)}, f32[8,16,768]{2,1,0:T(8,128)}, /*index=5*/f32[16,128]{1,0:T(8,128)}) custom-call(s32[1,4]{1,0:T(1,128)} %lengths_ref.3, s32[1,3]{1,0:T(1,128)} %counts_ref.3, bf16[1024,768]{1,0:T(8,128)(2,1)} %tokens_ref.5, ...), custom_call_target="tpu_custom_call" | custom-call | tf_op jit(solution)/shard_map/middle/pallas_call | solution.py:548
  129.7 0.0 all-reduce.6.cloned.1.call-update
  129.8 53.4 %attention_backward.1 = (bf16[1024,768]{1,0:T(8,128)(2,1)}, bf16[1024,768]{1,0:T(8,128)(2,1)}, bf16[1024,768]{1,0:T(8,128)(2,1)}, f32[768,1024]{1,0:T(8,128)}, f32[768,1024]{1,0:T(8,128)}) custom-call(bf16[1024,768]{1,0:T(8,128)(2,1)} %get-tuple-element.39.q_ref, bf16[1024,768]{1,0:T(8,128)(2,1)} %get-tuple-element.40.k_ref, ...), custom_call_target="tpu_custom_call" | custom-call | tf_op jit(solution)/shard_map/attention_backward/pallas_call | solution.py:411
  183.1 16.3 %last.1 = (f32[1024,768]{1,0:T(8,128)}, f32[3,16,768]{2,1,0:T(8,128)}, f32[3,16,768]{2,1,0:T(8,128)}, f32[16,128]{1,0:T(8,128)}) custom-call(bf16[1024,768]{1,0:T(8,128)(2,1)} %tokens_ref.5, bf16[1024,768]{1,0:T(8,128)(2,1)} %get-tuple-element.53.gq_ref, bf16[1024,768]{1,0:T(8,128)(2,1)} %get-tuple-element.54.gk_ref, ...), custom_call_target="tpu_custom_call" | custom-call | tf_op jit(solution)/shard_map/last/pallas_call | solution.py:638
  199.4 58.7 %all-reduce.6.cloned.1.call-done = (f32[4,12,768]{2,1,0:T(8,128)}, f32[2,4,12,768]{3,2,1,0:T(8,128)}) async-done(((f32[4,12,768]{2,1,0:T(8,128)}, f32[2,4,12,768]{3,2,1,0:T(8,128)}), (f32[4,12,768]{2,1,0:T(8,128)}, f32[2,4,12,768]{3,2,1,0:T(8,128)})) %all-reduce.6.cloned.1.call-update) | async-done | bytes 442384 | tf_op jit(solution)/shard_map/psum | solution.py:849
  258.0 18.4 %share.1 = (f32[5,12,768]{2,1,0:T(8,128)}, f32[5,12,768]{2,1,0:T(8,128)}, f32[6,12]{1,0:T(8,128)}) custom-call(f32[3,16,768]{2,1,0:T(8,128)} %get-tuple-element.62.down_ref, f32[3,16,768]{2,1,0:T(8,128)} %get-tuple-element.63.up_ref, f32[16,128]{1,0:T(8,128)} %get-tuple-element.64.last_ref, f32[16,128]{1,0:T(8,128)} %get-tuple-element.65.middle_ref, ...), custom_call_target="tpu_custom_call" | custom-call | tf_op jit(solution)/shard_map/share/pallas_call | solution.py:789
  276.5 1.5 dynamic-slice_bitcast_fusion
  277.9 1.7 copy.32
  279.6 1.7 copy.33
  281.2 1.3 copy.34
  (5 shorter events, 0.0 us)
Async XLA Ops:
  7.2 75.4 %all-gather.3.cloned.1.call-start = ((), (), s32[]{:S(2)}) async-start(), calls=%async_computation | async-start | bytes 12042240 | tf_op jit(solution)/shard_map/all_gather | solution.py:838
  14.3 0.7 copy-start
  14.3 0.8 copy-start.1
  14.3 0.8 copy-start.2
  14.3 0.9 copy-start.3
  14.3 0.9 copy-start.4
  14.4 243.7 %all-reduce.6.cloned.1.call-start = ((), (), s32[]{:S(2)}) async-start(), calls=%async_computation.1 | async-start | bytes 1179648 | tf_op jit(solution)/shard_map/psum | solution.py:849
Sparse Core Ops, SparseCore 0:
  14.5 68.0 all-gather.2
  129.9 128.1 all-reduce.5

commit v3 on v2

--- a/solution.py
+++ b/solution.py
@@ -332,12 +332,14 @@
     grad_scr,
     turned_scr,
     values_scr,
+    gek_scr,
+    gfq_scr,
 ):
     eye = unit_matrix(False)
     anti = unit_matrix(True)
     factor = (3.0 * DH) ** -0.5
-    gek_ref[...] = jnp.zeros_like(gek_ref)
-    gfq_ref[...] = jnp.zeros_like(gfq_ref)
+    gek_scr[...] = jnp.zeros_like(gek_scr)
+    gfq_scr[...] = jnp.zeros_like(gfq_scr)
     for start, length in SLOTS:
         count = length // TILE
         keys = k_ref[start : start + length, :]
@@ -378,7 +380,7 @@
                 )
             )
             gq_ref[row : row + TILE, :] = dot_nn(anti, query_grad.astype(bf16)).astype(bf16)
-            gek_ref[:, low : low + length + TILE] += dot_tn(queries, spread)
+            gek_scr[:, low : low + length + TILE] += dot_tn(queries, spread)
             value_grad = value_grad + dot_tn(grads, jnp.concatenate(probs, axis=0))
         values_scr[:, start : start + length] = value_grad
         turned = turned_scr[start : start + length, :]
@@ -401,10 +403,12 @@
                 )
             )
             gk_ref[row : row + TILE, :] = key_grad.astype(bf16)
-            gfq_ref[:, low : low + length + TILE] += dot_tn(
+            gfq_scr[:, low : low + length + TILE] += dot_tn(
                 each_head(k_ref[row : row + TILE, :]), spread
             )
     gv_ref[...] = values_scr[...].T.astype(bf16)
+    gek_ref[...] = gek_scr[...].astype(bf16)
+    gfq_ref[...] = gfq_scr[...].astype(bf16)
 
 
 def attend_backward(q, k, v, g, ek, fq, p1, p2, p3):
@@ -414,11 +418,13 @@
         in_specs=[PAIR_SPEC] * 6 + PROB_SPECS,
         out_specs=[PAIR_SPEC] * 3 + [TABLE_SPEC] * 2,
         out_shape=[jax.ShapeDtypeStruct((ROWS, D), bf16)] * 3
-        + [jax.ShapeDtypeStruct((D, OFFSETS), f32)] * 2,
+        + [jax.ShapeDtypeStruct((D, OFFSETS), bf16)] * 2,
         scratch_shapes=[
             pltpu.VMEM((2, ROWS, LEN3), bf16),
             pltpu.VMEM((ROWS, PAIR), bf16),
             pltpu.VMEM((PAIR, ROWS), f32),
+            pltpu.VMEM((PAIR, OFFSETS), f32),
+            pltpu.VMEM((PAIR, OFFSETS), f32),
         ],
         compiler_params=pltpu.CompilerParams(vmem_limit_bytes=MEMORY),
         name="attention_backward",
@@ -578,6 +584,20 @@
     )(lengths, counts, tokens, context, out_grad, weights, packed, factors, scales, norms)
 
 
+LANES = 128
+BLOCKS = D // LANES
+MESH = pl.DeviceIdType.MESH
+
+
+def devices():
+    return lax.axis_size("dp") * lax.axis_size("tensor")
+
+
+def hidden_rows():
+    tiles = 2 * BLOCKS
+    return PAD * -(-tiles // lax.axis_size("dp"))
+
+
 def last_kernel(
     tokens_ref,
     gq_ref,
@@ -586,38 +606,184 @@
     grad_one_ref,
     coeff_ref,
     merged_ref,
-    rel_ref,
     index_ref,
     rel_coeff_ref,
-    gek_ref,
-    gfq_ref,
     factor_ref,
     scale_ref,
+    small_ref,
+    hidden_ref,
+    middle_scale_ref,
+    rel_any,
+    gek_any,
+    gfq_any,
     in_grad_ref,
-    down_ref,
-    up_ref,
-    scale_grad_ref,
+    down_out,
+    up_out,
+    hidden_out,
+    scale_out,
+    rel_scr,
+    gek_scr,
+    gfq_scr,
+    down_scr,
+    up_scr,
+    scale_scr,
+    stage_scr,
+    mine_late,
+    land_late,
+    mine_small,
+    land_small,
+    mine_hidden,
+    land_hidden,
+    all_sums,
+    all_hidden,
+    load_sem,
+    late_out_sem,
+    late_in_sem,
+    small_out_sem,
+    small_in_sem,
+    hidden_out_sem,
+    hidden_in_sem,
+    sums_out_sem,
+    sums_in_sem,
+    spread_out_sem,
+    spread_in_sem,
 ):
     step = pl.program_id(0)
+    final = ROWS // BLOCK - 1
+    outer = lax.axis_size("dp")
+    inner = lax.axis_size("tensor")
+    count = outer * inner
+    my_outer = lax.axis_index("dp")
+    my_inner = lax.axis_index("tensor")
+    me = my_outer * inner + my_inner
+    barrier = pltpu.get_barrier_semaphore()
+
+    def partner(off):
+        other = lax.rem(me + off, count)
+        return other, other // inner, lax.rem(other, inner)
+
+    def send(src, dst, out_sem, in_sem, place):
+        return pltpu.make_async_remote_copy(
+            src_ref=src,
+            dst_ref=dst,
+            send_sem=out_sem,
+            recv_sem=in_sem,
+            device_id=place,
+            device_id_type=MESH,
+        )
+
+    def late(off):
+        other, row, col = partner(off)
+        return send(
+            mine_late.at[other],
+            land_late.at[off],
+            late_out_sem.at[off],
+            late_in_sem.at[off],
+            (row, col),
+        )
+
+    def small(off):
+        other, row, col = partner(off)
+        return send(
+            mine_small.at[other],
+            land_small.at[off],
+            small_out_sem.at[off],
+            small_in_sem.at[off],
+            (row, col),
+        )
+
+    def hidden(off):
+        other, row, col = partner(off)
+        return send(
+            mine_hidden.at[col, row],
+            land_hidden.at[off],
+            hidden_out_sem.at[off],
+            hidden_in_sem.at[off],
+            (row, col),
+        )
+
+    def sums(off, origin):
+        other, row, col = partner(off)
+        return send(
+            all_sums.at[origin],
+            all_sums.at[origin],
+            sums_out_sem.at[off],
+            sums_in_sem.at[off],
+            (row, col),
+        )
+
+    def spread(off, origin):
+        return send(
+            all_hidden.at[origin],
+            all_hidden.at[origin],
+            spread_out_sem.at[off],
+            spread_in_sem.at[off],
+            (lax.rem(my_outer + off, outer), my_inner),
+        )
+
+    def load(number, src, dst):
+        return pltpu.make_async_copy(src, dst, load_sem.at[number])
+
+    loads = ((0, rel_any, rel_scr), (1, gek_any, gek_scr), (2, gfq_any, gfq_scr))
 
     @pl.when(step == 0)
     def _():
-        rel = rel_ref[...]
-        scale_grad_ref[...] = jnp.zeros_like(scale_grad_ref)
-        down_ref[2] = jnp.zeros((PAD, D), f32)
-        up_ref[2] = jnp.zeros((PAD, D), f32)
+        for piece in loads:
+            load(*piece).start()
+
+        @pl.loop(1, count)
+        def _(off):
+            _, row, col = partner(off)
+            pl.semaphore_signal(barrier, inc=1, device_id=(row, col), device_id_type=MESH)
+
+        scale_scr[...] = jnp.zeros_like(scale_scr)
+        down_scr[...] = jnp.zeros_like(down_scr)
+        up_scr[...] = jnp.zeros_like(up_scr)
+
+    @pl.when(step == 1)
+    def _():
+        if count > 4 * BLOCKS:
+            mine_small[4 * BLOCKS :] = jnp.zeros((count - 4 * BLOCKS, PAD, LANES), bf16)
+        for number in range(4):
+            for block in range(BLOCKS):
+                mine_small[number * BLOCKS + block] = small_ref[
+                    number, :, block * LANES : (block + 1) * LANES
+                ].astype(bf16)
+        mine_hidden[...] = jnp.zeros_like(mine_hidden)
+        tiles = mine_hidden.shape[2] // PAD
+        for chunk in range(inner):
+            for which in range(2):
+                for block in range(BLOCKS):
+                    tile = which * BLOCKS + block
+                    at = tile % tiles * PAD
+                    mine_hidden[chunk, tile // tiles, at : at + PAD] = hidden_ref[
+                        which * inner + chunk, :, block * LANES : (block + 1) * LANES
+                    ].astype(bf16)
+        pl.semaphore_wait(barrier, count - 1)
+
+        @pl.loop(1, count)
+        def _(off):
+            small(off).start()
+            hidden(off).start()
+
+        land_small[0] = mine_small[me]
+        land_hidden[0] = mine_hidden[my_inner, my_outer]
+
+    @pl.when(step == 2)
+    def _():
+        for piece in loads:
+            load(*piece).wait()
+        rel = rel_scr[...]
         bucket = lax.broadcasted_iota(jnp.int32, (2 * SPAN, OFFSETS), 0)
-        for member, ref, row in ((0, gfq_ref, 1), (1, gek_ref, 0)):
+        for member, ref, row in ((0, gfq_scr, 1), (1, gek_scr, 0)):
             scale = scale_ref[:, member : member + 1]
             chosen = jnp.where(bucket == index_ref[row : row + 1, :], 1.0, 0.0).astype(bf16)
-            grad = dot_nt(ref[...].astype(bf16), chosen).astype(bf16)
+            grad = dot_nt(ref[...], chosen).astype(bf16)
             coeff = rel_coeff_ref[member]
             slope = dot_nn(factor_ref[5 + member], grad)
-            up_ref[member] = add_parts(dot_nt(two_parts(coeff * scale), grad))
-            down_ref[member] = add_parts(dot_nn(two_parts(slope * scale), rel))
-            scale_grad_ref[:, member : member + 1] += jnp.sum(
-                coeff * slope, axis=1, keepdims=True
-            )
+            up_scr[member] += add_parts(dot_nt(two_parts(coeff * scale), grad))
+            down_scr[member] += add_parts(dot_nn(two_parts(slope * scale), rel))
+            scale_scr[:, member : member + 1] += jnp.sum(coeff * slope, axis=1, keepdims=True)
 
     tokens = tokens_ref[...]
     in_grad = grad_one_ref[...]
@@ -627,14 +793,112 @@
         in_grad = in_grad + dot_nt(grad, merged_ref[member])
         coeff = coeff_ref[member]
         slope = dot_nt(factor_ref[5 + member], grad)
-        up_ref[member] += add_parts(dot_nn(two_parts(coeff * scale), grad))
-        down_ref[member] += add_parts(dot_nn(two_parts(slope * scale), tokens))
-        scale_grad_ref[:, member : member + 1] += jnp.sum(coeff * slope, axis=1, keepdims=True)
+        up_scr[member] += add_parts(dot_nn(two_parts(coeff * scale), grad))
+        down_scr[member] += add_parts(dot_nn(two_parts(slope * scale), tokens))
+        scale_scr[:, member : member + 1] += jnp.sum(coeff * slope, axis=1, keepdims=True)
     in_grad_ref[...] = in_grad
 
-
-def last(tokens, gq, gk, gv, grad_one, coeff, weights, rel, index, rel_coeff, gek, gfq, factors, scales):
+    @pl.when(step == final)
+    def _():
+        used = 2 * 3 * BLOCKS * RANK
+        for number in range(6):
+            ref = down_scr if number < 3 else up_scr
+            for block in range(BLOCKS):
+                at = (number * BLOCKS + block) * RANK
+                stage_scr[at : at + RANK, :] = ref[
+                    number % 3, :RANK, block * LANES : (block + 1) * LANES
+                ]
+        stage_scr[used : used + PAD, :] = scale_scr[...] + middle_scale_ref[...]
+        stage_scr[used + PAD :, :] = jnp.zeros((count * PAD - used - PAD, LANES), f32)
+        mine_late[...] = stage_scr[...].astype(bf16).reshape(count, PAD, LANES)
+
+        @pl.loop(1, count)
+        def _(off):
+            late(off).start()
+
+        land_late[0] = mine_late[me]
+
+        @pl.loop(1, count)
+        def _(off):
+            small(off).wait_recv()
+            hidden(off).wait_recv()
+
+        all_hidden[my_outer] = jnp.sum(land_hidden[...].astype(f32), axis=0).astype(bf16)
+
+        @pl.loop(1, outer)
+        def _(off):
+            spread(off, my_outer).start()
+
+        all_sums[me, PAD:] = jnp.sum(land_small[...].astype(f32), axis=0).astype(bf16)
+
+        @pl.loop(1, count)
+        def _(off):
+            late(off).wait_recv()
+
+        all_sums[me, :PAD] = jnp.sum(land_late[...].astype(f32), axis=0).astype(bf16)
+
+        @pl.loop(1, count)
+        def _(off):
+            sums(off, me).start()
+
+        @pl.loop(1, outer)
+        def _(off):
+            spread(off, lax.rem(my_outer + outer - off, outer)).wait_recv()
+
+        tiles = all_hidden.shape[1] // PAD
+        for which in range(2):
+            for block in range(BLOCKS):
+                tile = which * BLOCKS + block
+                at = tile % tiles * PAD
+                hidden_out[which, :, block * LANES : (block + 1) * LANES] = all_hidden[
+                    tile // tiles, at : at + PAD
+                ].astype(f32)[:RANK]
+
+        @pl.loop(1, count)
+        def _(off):
+            sums(off, lax.rem(me + count - off, count)).wait_recv()
+
+        stage_scr[...] = all_sums[:, :PAD].astype(f32).reshape(count * PAD, LANES)
+        for number in range(6):
+            ref = down_out if number < 3 else up_out
+            for block in range(BLOCKS):
+                at = (number * BLOCKS + block) * RANK
+                ref[number % 3, :, block * LANES : (block + 1) * LANES] = stage_scr[
+                    at : at + RANK, :
+                ]
+        scale_out[...] = stage_scr[used : used + PAD, :].T[:6, :RANK]
+        for number, (ref, place) in enumerate(
+            ((down_out, 3), (up_out, 3), (down_out, 4), (up_out, 4))
+        ):
+            for block in range(BLOCKS):
+                ref[place, :, block * LANES : (block + 1) * LANES] = all_sums[
+                    number * BLOCKS + block, PAD:
+                ].astype(f32)[:RANK]
+
+        @pl.loop(1, count)
+        def _(off):
+            small(off).wait_send()
+            hidden(off).wait_send()
+            late(off).wait_send()
+            sums(off, me).wait_send()
+
+        @pl.loop(1, outer)
+        def _(off):
+            spread(off, my_outer).wait_send()
+
+
+def last(
+    tokens, gq, gk, gv, grad_one, coeff, weights, index, rel_coeff, factors, scales,
+    small, hidden, middle_scale, rel, gek, gfq,
+):
+    count = devices()
+    outer = lax.axis_size("dp")
+    inner = lax.axis_size("tensor")
+    piece = hidden_rows()
     tile = pl.BlockSpec((BLOCK, D), lambda i: (i, 0))
+    factor = jax.ShapeDtypeStruct((5, RANK, D), f32)
+    block = pltpu.VMEM((count, PAD, LANES), bf16)
+    all_pairs = pltpu.SemaphoreType.DMA((count,))
     return pl.pallas_call(
         last_kernel,
         grid=(ROWS // BLOCK,),
@@ -642,167 +906,57 @@
         + [
             pl.BlockSpec((3, PAD, BLOCK), lambda i: (0, 0, i)),
             whole(3, D, D),
-            whole(2 * SPAN, D),
             whole(2, OFFSETS),
             whole(2, PAD, 2 * SPAN),
-            whole(D, OFFSETS),
-            whole(D, OFFSETS),
             whole(12, PAD, D),
-            whole(PAD, 128),
+            whole(PAD, LANES),
+            whole(4, PAD, D),
+            whole(2 * inner, PAD, D),
+            whole(PAD, LANES),
+        ]
+        + [pl.BlockSpec(memory_space=pl.ANY)] * 3,
+        out_specs=[
+            tile,
+            whole(5, RANK, D),
+            whole(5, RANK, D),
+            whole(2, RANK, D),
+            whole(6, RANK),
         ],
-        out_specs=[tile, whole(3, PAD, D), whole(3, PAD, D), whole(PAD, 128)],
         out_shape=[
             jax.ShapeDtypeStruct((ROWS, D), f32),
-            jax.ShapeDtypeStruct((3, PAD, D), f32),
-            jax.ShapeDtypeStruct((3, PAD, D), f32),
-            jax.ShapeDtypeStruct((PAD, 128), f32),
+            factor,
+            factor,
+            jax.ShapeDtypeStruct((2, RANK, D), f32),
+            jax.ShapeDtypeStruct((6, RANK), f32),
         ],
-        compiler_params=pltpu.CompilerParams(vmem_limit_bytes=MEMORY),
-        name="last",
-    )(tokens, gq, gk, gv, grad_one, coeff, weights, rel, index, rel_coeff, gek, gfq, factors, scales)
-
-
-def devices():
-    return lax.axis_size("dp") * lax.axis_size("tensor")
-
-
-def share_kernel(
-    down_ref,
-    up_ref,
-    last_ref,
-    middle_ref,
-    early_ref,
-    down_out,
-    up_out,
-    scale_out,
-    stage_scr,
-    mine_scr,
-    land_scr,
-    all_scr,
-    send_sem,
-    land_sem,
-    spread_sem,
-    all_sem,
-):
-    count = devices()
-    inner = lax.axis_size("tensor")
-    me = lax.axis_index("dp") * inner + lax.axis_index("tensor")
-
-    def partner(off):
-        other = lax.rem(me + off, count)
-        return other, (other // inner, lax.rem(other, inner))
-
-    barrier = pltpu.get_barrier_semaphore()
-
-    @pl.loop(1, count)
-    def _(off):
-        pl.semaphore_signal(
-            barrier, inc=1, device_id=partner(off)[1], device_id_type=pl.DeviceIdType.MESH
-        )
-
-    stage_scr[...] = jnp.zeros_like(stage_scr)
-    for number in range(6):
-        ref = down_ref if number < 3 else up_ref
-        for block in range(D // 128):
-            at = (number * (D // 128) + block) * RANK
-            stage_scr[at : at + RANK, :] = ref[number % 3, :RANK, block * 128 : block * 128 + 128]
-    at = 6 * (D // 128) * RANK
-    stage_scr[at : at + PAD, :] = last_ref[...] + middle_ref[...]
-    mine_scr[...] = stage_scr[...].astype(bf16).reshape(count, PAD, 128)
-    pl.semaphore_wait(barrier, count - 1)
-
-    def first(off):
-        other, where = partner(off)
-        return pltpu.make_async_remote_copy(
-            src_ref=mine_scr.at[other],
-            dst_ref=land_scr.at[off],
-            send_sem=send_sem.at[off],
-            recv_sem=land_sem.at[off],
-            device_id=where,
-            device_id_type=pl.DeviceIdType.MESH,
-        )
-
-    def second(off):
-        other, where = partner(off)
-        return pltpu.make_async_remote_copy(
-            src_ref=all_scr.at[me],
-            dst_ref=all_scr.at[me],
-            send_sem=spread_sem.at[off],
-            recv_sem=all_sem.at[off],
-            device_id=where,
-            device_id_type=pl.DeviceIdType.MESH,
-        )
-
-    def second_arrival(off):
-        origin = lax.rem(me + count - off, count)
-        return pltpu.make_async_remote_copy(
-            src_ref=all_scr.at[origin],
-            dst_ref=all_scr.at[origin],
-            send_sem=spread_sem.at[off],
-            recv_sem=all_sem.at[off],
-            device_id=partner(off)[1],
-            device_id_type=pl.DeviceIdType.MESH,
-        )
-
-    @pl.loop(1, count)
-    def _(off):
-        first(off).start()
-
-    land_scr[0] = mine_scr[me]
-
-    @pl.loop(1, count)
-    def _(off):
-        first(off).wait_recv()
-
-    all_scr[me] = jnp.sum(land_scr[...].astype(f32), axis=0).astype(bf16)
-
-    @pl.loop(1, count)
-    def _(off):
-        second(off).start()
-
-    for index, place in ((0, 3), (2, 4)):
-        down_out[place] = early_ref[index]
-        up_out[place] = early_ref[index + 1]
-
-    @pl.loop(1, count)
-    def _(off):
-        second_arrival(off).wait_recv()
-
-    stage_scr[...] = all_scr[...].astype(f32).reshape(count * PAD, 128)
-    for number in range(6):
-        ref = down_out if number < 3 else up_out
-        for block in range(D // 128):
-            at = (number * (D // 128) + block) * RANK
-            ref[number % 3, :, block * 128 : block * 128 + 128] = stage_scr[at : at + RANK, :]
-    at = 6 * (D // 128) * RANK
-    scale_out[...] = stage_scr[at : at + PAD, :].T[:6, :RANK]
-
-    @pl.loop(1, count)
-    def _(off):
-        first(off).wait_send()
-        second(off).wait_send()
-
-
-def share(down, up, last_scale, middle_scale, early):
-    count = devices()
-    factor = jax.ShapeDtypeStruct((5, RANK, D), f32)
-    return pl.pallas_call(
-        share_kernel,
-        in_specs=[pl.BlockSpec(memory_space=pltpu.VMEM)] * 5,
-        out_specs=[pl.BlockSpec(memory_space=pltpu.VMEM)] * 3,
-        out_shape=[factor, factor, jax.ShapeDtypeStruct((6, RANK), f32)],
         scratch_shapes=[
-            pltpu.VMEM((count * PAD, 128), f32),
-            pltpu.VMEM((count, PAD, 128), bf16),
-            pltpu.VMEM((count, PAD, 128), bf16),
-            pltpu.VMEM((count, PAD, 128), bf16),
+            pltpu.VMEM((2 * SPAN, D), bf16),
+            pltpu.VMEM((D, OFFSETS), bf16),
+            pltpu.VMEM((D, OFFSETS), bf16),
+            pltpu.VMEM((3, PAD, D), f32),
+            pltpu.VMEM((3, PAD, D), f32),
+            pltpu.VMEM((PAD, LANES), f32),
+            pltpu.VMEM((count * PAD, LANES), f32),
+            block,
+            block,
+            block,
+            block,
+            pltpu.VMEM((inner, outer, piece, LANES), bf16),
+            pltpu.VMEM((count, piece, LANES), bf16),
+            pltpu.VMEM((count, 2 * PAD, LANES), bf16),
+            pltpu.VMEM((outer, piece, LANES), bf16),
+            pltpu.SemaphoreType.DMA((3,)),
         ]
-        + [pltpu.SemaphoreType.DMA((count,))] * 4,
+        + [all_pairs] * 8
+        + [pltpu.SemaphoreType.DMA((outer,))] * 2,
         compiler_params=pltpu.CompilerParams(
             collective_id=0, has_side_effects=True, vmem_limit_bytes=MEMORY
         ),
-        name="share",
-    )(down, up, last_scale, middle_scale, early)
+        name="last",
+    )(
+        tokens, gq, gk, gv, grad_one, coeff, weights, index, rel_coeff, factors, scales,
+        small, hidden, middle_scale, rel, gek, gfq,
+    )
 
 
 def on_device(
@@ -845,17 +999,12 @@
     mixed, grad_one, context_grad, small, hidden, middle_scale = middle(
         seq_lengths, seq_counts, tokens, context, out_grad, weights, packed, factors, scales, norms
     )
-    chunks = packed.shape[0]
-    small, hidden = lax.psum(
-        (small[:, :RANK], hidden[:, :RANK].reshape(2, chunks, RANK, D)), ("dp", "tensor")
-    )
-    hidden = hidden[:, lax.axis_index("tensor")]
     gq, gk, gv, gek, gfq = attend_backward(q, k, v, context_grad, ek, fq, p1, p2, p3)
-    in_grad, down, up, last_scale = last(
-        tokens, gq, gk, gv, grad_one, coeff, weights, rel_embed, index_rows, rel_coeff, gek, gfq, factors, scales
-    )
-    down_grad, up_grad, scale_grad = share(down, up, last_scale, middle_scale, small)
-    return (mixed, in_grad, down_grad, up_grad, hidden[0], hidden[1], scale_grad)
+    in_grad, down_grad, up_grad, hidden_grad, scale_grad = last(
+        tokens, gq, gk, gv, grad_one, coeff, weights, index_rows, rel_coeff, factors, scales,
+        small, hidden, middle_scale, rel_embed, gek, gfq,
+    )
+    return (mixed, in_grad, down_grad, up_grad, hidden_grad[0], hidden_grad[1], scale_grad)
 
 
 def solution(mesh):

time: 290 us -> 230 us (0.79)
  waiting for transfers between devices: 69.2 us -> 10.5 us
  Pallas kernels: 195 us -> 192 us
    psum x1 -> x0, waiting for transfers between devices: 58.7 us -> none  [on_device(): lax.psum((small[:, :RANK], hidden[:, :RANK].reshape(2, chunks, RANK, D)),...]
    pallas_call x1 -> x0, Pallas kernels: 18.4 us -> none  [share(): pl.pallas_call(share_kernel, in_specs=[pl.BlockSpec(memory_space=pltpu.VM...]
    pallas_call x1, Pallas kernels: 16.3 us -> 32.3 us  [last(): pl.pallas_call(last_kernel, grid=(ROWS // BLOCK,), in_specs=[tile] * 5 +...]
    unnamed x16 -> x23, local copies, waits for them, and re-layouts: 6.11 us -> 7.42 us
  transfers between devices with their start and end apart: 2 -> 1, of which waited for: 2 -> 1; matrix products, arithmetic and copies ran while one was open for 0% -> 1% of each run, Pallas kernels for 43% -> 24%
where the time goes in v3:
time: 230 us
  Pallas kernels  192 us (83%)
  between operations  14.1 us (6%)
  waiting for transfers between devices  10.5 us (5%)
  local copies, waits for them, and re-layouts  10.1 us (4%)
  other arithmetic  2.4 us (1%)
    pallas_call x1, Pallas kernels, attend_backward(): pl.pallas_call(backward_kernel, grid=(H // 2,), in_specs=[PAIR_SPEC] * 6...  53.3 us
    pallas_call x1, Pallas kernels, middle(): pl.pallas_call(middle_kernel, grid=(ROWS // BLOCK,), in_specs=[pl.BlockSp...  47.2 us
    pallas_call x1, Pallas kernels, attend_forward(): pl.pallas_call(forward_kernel, grid=(H // 2,), in_specs=[pl.BlockSpec(mem...  38.4 us
    pallas_call x1, Pallas kernels, last(): pl.pallas_call(last_kernel, grid=(ROWS // BLOCK,), in_specs=[tile] * 5 +...  32.3 us
    pallas_call x1, Pallas kernels, project(): pl.pallas_call(project_kernel, grid=(ROWS // BLOCK,), in_specs=[tile, who...  17.2 us
    all_gather x1, waiting for transfers between devices, on_device(): lax.all_gather(pack_weights(in_weight, back_weight, factors, scales), 'te...  10.5 us
    unnamed x23, local copies, waits for them, and re-layouts  7.42 us
  transfers between devices with their start and end apart: 1, of which 1 were waited for; matrix products, arithmetic and copies ran while one was open for 1% of the time, Pallas kernels for 24%

profile of v3, /device:TPU:0, one launch (start us, length us, event | category | flops | bytes accessed | tf_op | source)
XLA Modules:
  0.0 229.5 jit_solution(18227843473176235639)
XLA Ops:
  7.2 0.0 all-gather.3.cloned.1.call-start
  7.2 0.8 copy.26
  8.0 0.6 pad.14.scale_ref
  8.6 1.8 fusion.6.factor_ref
  10.4 4.0 %pack_weights.1 = bf16[1568,768]{1,0:T(8,128)(2,1)} custom-call(bf16[768,768]{1,0:T(8,128)(2,1)} %in_ref.1, bf16[768,768]{1,0:T(8,128)(2,1)} %back_ref.1, bf16[12,16,768]{2,1,0:T(8,128)(2,1)} %fusion.6.factor_ref, f32[16,128]{1,0:T(8,128)} %pad.14.scale_ref), custom_call_target="tpu_custom_call" | custom-call | tf_op jit(solution)/shard_map/pack_weights/pallas_call | solution.py:74
  14.3 0.0 copy-start.3
  14.3 0.0 copy-start.4
  14.3 0.0 copy-start.5
  14.3 0.0 copy-start.6
  14.4 0.0 copy-start.2
  14.4 0.0 all-gather.3.cloned.1.call-update
  14.4 0.6 copy-done.3
  15.0 0.0 copy-done.4
  15.0 0.0 copy-done.5
  15.1 0.0 copy-done.6
  15.1 0.0 copy-done.2
  15.1 0.1 reverse
  15.2 0.1 slice.10
  15.3 0.6 pad.12.index_ref
  15.9 17.2 %project.1 = (bf16[1024,768]{1,0:T(8,128)(2,1)}, bf16[1024,768]{1,0:T(8,128)(2,1)}, bf16[1024,768]{1,0:T(8,128)(2,1)}, bf16[1024,768]{1,0:T(8,128)(2,1)}, bf16[1...) custom-call(bf16[1024,768]{1,0:T(8,128)(2,1)} %tokens_ref.5, ...), custom_call_target="tpu_custom_call" | custom-call | tf_op jit(solution)/shard_map/project/pallas_call | solution.py:140
  33.1 38.4 %attention_forward.1 = (bf16[1024,768]{1,0:T(8,128)(2,1)}, bf16[12,256,128]{2,1,0:T(8,128)(2,1)}, bf16[12,256,256]{2,1,0:T(8,128)(2,1)}, bf16[12,512,512]{2,1,0:T(8,128)(2,1)}) custom-call(s32[1,4]{1,0:T(1,128)} %lengths_ref.3, s32[1,3]{1,0:T(1,128)} %counts_ref.3, bf16[1024,768]{1,0:T(8,128)(2,1)} %get-tuple-element.37.q_ref, ...), custom_call_target="tpu_custom_call" | custom-call | tf_op jit(solution)/shard_map/attention_forward/pallas_call | solution.py:302
  71.5 0.6 pad_maximum_fusion.norm_ref
  72.1 10.5 %all-gather.3.cloned.1.call-done = bf16[6272,768]{1,0:T(8,128)(2,1)} async-done(((bf16[1568,768]{1,0:T(8,128)(2,1)}), bf16[6272,768]{1,0:T(8,128)(2,1)}) %all-gather.3.cloned.1.call-update) | async-done | bytes 9633808 | tf_op jit(solution)/shard_map/all_gather | solution.py:992
  82.6 47.2 %middle.1 = (bf16[1024,768]{1,0:T(8,128)(2,1)}, f32[1024,768]{1,0:T(8,128)}, bf16[1024,768]{1,0:T(8,128)(2,1)}, f32[4,16,768]{2,1,0:T(8,128)}, f32[8,16,768]{2,1,0:T(8,128)}, /*index=5*/f32[16,128]{1,0:T(8,128)}) custom-call(s32[1,4]{1,0:T(1,128)} %lengths_ref.3, s32[1,3]{1,0:T(1,128)} %counts_ref.3, bf16[1024,768]{1,0:T(8,128)(2,1)} %tokens_ref.5, ...), custom_call_target="tpu_custom_call" | custom-call | tf_op jit(solution)/shard_map/middle/pallas_call | solution.py:554
  129.8 53.3 %attention_backward.1 = (bf16[1024,768]{1,0:T(8,128)(2,1)}, bf16[1024,768]{1,0:T(8,128)(2,1)}, bf16[1024,768]{1,0:T(8,128)(2,1)}, bf16[768,1024]{1,0:T(8,128)(2,1)}, bf16[768,1024]{1,0:T(8,128)(2,1)}) custom-call(bf16[1024,768]{1,0:T(8,128)(2,1)} %get-tuple-element.37.q_ref, bf16[1024,768]{1,0:T(8,128)(2,1)} %get-tuple-element.38.k_ref, ...), custom_call_target="tpu_custom_call" | custom-call | tf_op jit(solution)/shard_map/attention_backward/pallas_call | solution.py:415
  183.1 32.3 %last.1 = (f32[1024,768]{1,0:T(8,128)}, f32[5,12,768]{2,1,0:T(8,128)}, f32[5,12,768]{2,1,0:T(8,128)}, f32[2,12,768]{2,1,0:T(8,128)}, f32[6,12]{1,0:T(8,128)}) custom-call(bf16[1024,768]{1,0:T(8,128)(2,1)} %tokens_ref.5, bf16[1024,768]{1,0:T(8,128)(2,1)} %get-tuple-element.51.gq_ref, bf16[1024,768]{1,0:T(8,128)(2,1)} %get-tuple-element.52.gk_ref, ...), custom_call_target="tpu_custom_call" | custom-call | tf_op jit(solution)/shard_map/last/pallas_call | solution.py:902
  215.4 1.5 slice_bitcast_fusion
  216.9 0.0 copy-start.1
  216.9 0.0 copy-start
  216.9 0.0 copy-start.7
  216.9 3.8 %copy.31 = f32[1024,768]{1,0:T(8,128)} copy(f32[1024,768]{1,0:T(8,128)} %get-tuple-element.77) | data formatting | bytes 6291456
  220.7 0.0 copy-done.1
  220.7 0.7 copy.32
  221.4 0.0 copy-done
  221.4 0.7 copy.33
  222.1 0.0 copy-done.7
  222.1 0.6 copy.34
  (5 shorter events, 0.0 us)
Async XLA Ops:
  7.2 75.5 %all-gather.3.cloned.1.call-start = ((), (), s32[]{:S(2)}) async-start(), calls=%async_computation | async-start | bytes 12042240 | tf_op jit(solution)/shard_map/all_gather | solution.py:992
  14.3 0.7 copy-start.3
  14.3 0.7 copy-start.4
  14.3 0.7 copy-start.5
  14.3 0.7 copy-start.6
  14.4 0.7 copy-start.2
  216.9 3.8 %copy-start.1 = (f32[5,12,768]{2,1,0:T(8,128)S(1)}, f32[5,12,768]{2,1,0:T(8,128)}, u32[]{:S(2)}) copy-start(f32[5,12,768]{2,1,0:T(8,128)} %get-tuple-element.78) | copy-start | bytes 552964
  216.9 4.5 %copy-start = (f32[5,12,768]{2,1,0:T(8,128)S(1)}, f32[5,12,768]{2,1,0:T(8,128)}, u32[]{:S(2)}) copy-start(f32[5,12,768]{2,1,0:T(8,128)} %get-tuple-element.79) | copy-start | bytes 552964
  216.9 5.2 %copy-start.7 = (f32[6,12]{1,0:T(8,128)S(1)}, f32[6,12]{1,0:T(8,128)}, u32[]{:S(2)}) copy-start(f32[6,12]{1,0:T(8,128)} %get-tuple-element.82) | copy-start | bytes 868
Sparse Core Ops, SparseCore 0:
  14.5 68.0 all-gather.2

commit v4 on v3

--- a/solution.py
+++ b/solution.py
@@ -19,7 +19,12 @@
 TILE = 128
 BLOCK = 256
 SLOTS = ((0, 128), (128, 128), (256, 256), (512, 512))
-PACKED = 2 * D + 2 * PAD
+PACKED = 1600
+HALF = PACKED // 2
+CHUNK = HALF // 5
+LANES = 128
+BLOCKS = D // LANES
+MESH = pl.DeviceIdType.MESH
 norm_epsilon = 1e-07
 masked_score = -1e30
 bf16 = jnp.bfloat16
@@ -63,46 +68,58 @@
     ]
 
 
-def pack_kernel(in_ref, back_ref, factor_ref, scale_ref, packed_ref):
-    packed_ref[:D] = merged(in_ref[...], factor_ref[4], factor_ref[10], scale_ref[:, 4:5])
-    packed_ref[D : 2 * D] = merged(back_ref[...], factor_ref[11], factor_ref[9], scale_ref[:, 5:6])
-    packed_ref[2 * D : 2 * D + PAD] = factor_ref[10]
-    packed_ref[2 * D + PAD :] = factor_ref[11]
-
-
-def pack_weights(in_weight, back_weight, factors, scales):
-    return pl.pallas_call(
-        pack_kernel,
-        out_shape=jax.ShapeDtypeStruct((PACKED, D), bf16),
-        compiler_params=pltpu.CompilerParams(vmem_limit_bytes=MEMORY),
-        name="pack_weights",
-    )(in_weight, back_weight, factors, scales)
+def padded(rows):
+    return jnp.concatenate([rows.astype(f32), jnp.zeros((PAD - RANK, D), f32)], axis=0).astype(bf16)
 
 
 def project_kernel(
     tokens_ref,
     qkv_ref,
-    out_ref,
     rel_ref,
     index_ref,
-    factor_ref,
-    scale_ref,
+    down_ref,
+    up_ref,
+    hidden_up_ref,
+    hidden_down_ref,
+    adapt_scale_ref,
+    out_any,
+    in_any,
+    back_any,
     q_ref,
     k_ref,
     v_ref,
-    ek_ref,
-    fq_ref,
+    eq_ref,
+    fk_ref,
     ekt_ref,
     eqt_ref,
     merged_ref,
+    packed_ref,
     coeff_ref,
     rel_coeff_ref,
+    factor_ref,
+    scale_ref,
     pos_scr,
+    load_scr,
+    load_sem,
 ):
     step = pl.program_id(0)
+    loads = [
+        pltpu.make_async_copy(ref, load_scr.at[number], load_sem.at[number])
+        for number, ref in enumerate((out_any, in_any, back_any))
+    ]
 
     @pl.when(step == 0)
     def _():
+        for load in loads:
+            load.start()
+        for number in range(5):
+            factor_ref[number] = padded(down_ref[number])
+            factor_ref[5 + number] = padded(up_ref[number])
+        factor_ref[10] = padded(hidden_up_ref[...])
+        factor_ref[11] = padded(hidden_down_ref[...])
+        wide = jnp.concatenate([adapt_scale_ref[...], jnp.zeros((6, LANES - RANK), f32)], axis=1)
+        wide = jnp.concatenate([wide, jnp.zeros((LANES - 6, LANES), f32)], axis=0)
+        scale_ref[...] = wide.T[:PAD]
         for member in range(3):
             merged_ref[member] = merged(
                 qkv_ref[member],
@@ -110,22 +127,39 @@
                 factor_ref[5 + member],
                 scale_ref[:, member : member + 1],
             )
-        merged_ref[3] = merged(out_ref[...], factor_ref[3], factor_ref[8], scale_ref[:, 3:4])
         rel = rel_ref[...]
         for member in range(2):
             pos_scr[member] = dot_nn(rel, merged_ref[member]).astype(bf16)
-            rel_coeff_ref[member] = dot_nt(factor_ref[member], rel)
+        coeff = dot_nt(factor_ref[:2].reshape(2 * PAD, D), rel)
+        rel_coeff_ref[...] = coeff.reshape(2, PAD, 2 * SPAN)
+
+    @pl.when(step == 1)
+    def _():
+        for load in loads:
+            load.wait()
+        packed_ref[:D] = merged(load_scr[1], factor_ref[4], factor_ref[10], scale_ref[:, 4:5])
+        packed_ref[2 * D : 2 * D + PAD] = factor_ref[10]
+        packed_ref[2 * D + PAD : 2 * D + 2 * PAD] = factor_ref[11]
+        packed_ref[2 * D + 2 * PAD :] = jnp.zeros((PACKED - 2 * D - 2 * PAD, D), bf16)
+
+    @pl.when(step == 2)
+    def _():
+        packed_ref[D : 2 * D] = merged(load_scr[2], factor_ref[11], factor_ref[9], scale_ref[:, 5:6])
+
+    @pl.when(step == 3)
+    def _():
+        merged_ref[3] = merged(load_scr[0], factor_ref[3], factor_ref[8], scale_ref[:, 3:4])
 
     tokens = tokens_ref[...]
     for member, ref in enumerate((q_ref, k_ref, v_ref)):
         ref[...] = dot_nn(tokens, merged_ref[member]).astype(bf16)
-        coeff_ref[member] = dot_nt(factor_ref[member], tokens)
+    coeff_ref[...] = dot_nt(factor_ref[:3].reshape(3 * PAD, D), tokens).reshape(3, PAD, BLOCK)
     bucket = lax.broadcasted_iota(jnp.int32, (2 * SPAN, BLOCK), 0)
     back, forth = (
         jnp.where(bucket == index_ref[row : row + 1, :], 1.0, 0.0).astype(bf16) for row in range(2)
     )
-    ek_ref[...] = dot_tn(back, pos_scr[1]).astype(bf16)
-    fq_ref[...] = dot_tn(forth, pos_scr[0]).astype(bf16)
+    eq_ref[...] = dot_tn(back, pos_scr[0]).astype(bf16)
+    fk_ref[...] = dot_tn(forth, pos_scr[1]).astype(bf16)
     ekt_ref[...] = dot_tn(pos_scr[1], back).astype(bf16)
     eqt_ref[...] = dot_tn(pos_scr[0], back).astype(bf16)
 
@@ -134,7 +168,14 @@
     return pl.BlockSpec(shape, lambda *at: (0,) * len(shape))
 
 
-def project(tokens, qkv_weight, out_weight, rel_embed, index_rows, factors, scales):
+def once(*shape):
+    return pl.BlockSpec(shape, lambda *at: (0,) * len(shape), pipeline_mode=pl.Buffered(1))
+
+
+def project(
+    tokens, qkv_weight, rel_embed, index_rows, down, up, hidden_up, hidden_down, adapt_scale,
+    out_weight, in_weight, back_weight,
+):
     tile = pl.BlockSpec((BLOCK, D), lambda i: (i, 0))
     rows = jax.ShapeDtypeStruct((ROWS, D), bf16)
     return pl.pallas_call(
@@ -142,31 +183,47 @@
         grid=(ROWS // BLOCK,),
         in_specs=[
             tile,
-            whole(3, D, D),
-            whole(D, D),
-            whole(2 * SPAN, D),
+            once(3, D, D),
+            once(2 * SPAN, D),
             pl.BlockSpec((2, BLOCK), lambda i: (0, i)),
-            whole(12, PAD, D),
-            whole(PAD, 128),
-        ],
+            once(5, RANK, D),
+            once(5, RANK, D),
+            once(RANK, D),
+            once(RANK, D),
+            once(6, RANK),
+        ]
+        + [pl.BlockSpec(memory_space=pl.ANY)] * 3,
         out_specs=[tile] * 5
         + [pl.BlockSpec((D, BLOCK), lambda i: (0, i))] * 2
         + [
             whole(4, D, D),
+            whole(PACKED, D),
             pl.BlockSpec((3, PAD, BLOCK), lambda i: (0, 0, i)),
             whole(2, PAD, 2 * SPAN),
+            whole(12, PAD, D),
+            whole(PAD, LANES),
         ],
         out_shape=[rows] * 5
         + [jax.ShapeDtypeStruct((D, OFFSETS), bf16)] * 2
         + [
             jax.ShapeDtypeStruct((4, D, D), bf16),
+            jax.ShapeDtypeStruct((PACKED, D), bf16),
             jax.ShapeDtypeStruct((3, PAD, ROWS), f32),
             jax.ShapeDtypeStruct((2, PAD, 2 * SPAN), f32),
+            jax.ShapeDtypeStruct((12, PAD, D), bf16),
+            jax.ShapeDtypeStruct((PAD, LANES), f32),
         ],
-        scratch_shapes=[pltpu.VMEM((2, 2 * SPAN, D), bf16)],
+        scratch_shapes=[
+            pltpu.VMEM((2, 2 * SPAN, D), bf16),
+            pltpu.VMEM((3, D, D), bf16),
+            pltpu.SemaphoreType.DMA((3,)),
+        ],
         compiler_params=pltpu.CompilerParams(vmem_limit_bytes=MEMORY),
         name="project",
-    )(tokens, qkv_weight, out_weight, rel_embed, index_rows, factors, scales)
+    )(
+        tokens, qkv_weight, rel_embed, index_rows, down, up, hidden_up, hidden_down, adapt_scale,
+        out_weight, in_weight, back_weight,
+    )
 
 
 def unit_matrix(flipped):
@@ -215,6 +272,33 @@
     return jnp.concatenate(done, axis=0)
 
 
+def flip_rows(block):
+    row = lax.broadcasted_iota(jnp.int32, (8, LANES), 0)
+    done = []
+    for at in range(TILE - 8, -1, -8):
+        done.append(
+            jnp.concatenate(
+                [
+                    jnp.take_along_axis(block[at : at + 8, c : c + LANES], 7 - row, axis=0)
+                    for c in range(0, block.shape[1], LANES)
+                ],
+                axis=1,
+            )
+        )
+    return jnp.concatenate(done, axis=0)
+
+
+def slot_tiles(slot):
+    return [(slot, t) for t in range(SLOTS[slot][1] // TILE)]
+
+
+def prob_block(refs, slot, t, member):
+    start, length = SLOTS[slot]
+    at = start + t * TILE if length == LEN1 else t * TILE
+    ref = refs[{LEN1: 0, LEN3: 2}.get(length, 1)]
+    return ref.at[member, at : at + TILE, :]
+
+
 def unskew(scores, length):
     lane, row = lane_and_row()
     zero = jnp.zeros((8, 128), f32)
@@ -232,6 +316,104 @@
     return jnp.concatenate(done, axis=0)
 
 
+def gather_moves(packed, gathered, own_sem, sems):
+    step = pl.program_id(0)
+    final = pl.num_programs(0) - 1
+    d = lax.axis_index("dp")
+    t = lax.axis_index("tensor")
+    near = t + 1 - 2 * lax.rem(t, 2)
+    far = t + 2 - 4 * (t // 2)
+    mate = d + 1 - 2 * lax.rem(d, 2)
+    half = lax.rem(d, 2)
+    chunks = HALF // CHUNK
+    near_out, near_in, far_out, far_in, mate_out, mate_in, pass_out, pass_in, late_out, late_in = sems
+    barrier = pltpu.get_barrier_semaphore()
+    places = ((d, near), (d, far), (mate, t))
+
+    def rows(which, chunk):
+        return pl.ds(pl.multiple_of(which * HALF + chunk * CHUNK, PAD), CHUNK)
+
+    def send(src, dst, out_sem, in_sem, place):
+        return pltpu.make_async_remote_copy(
+            src_ref=src, dst_ref=dst, send_sem=out_sem, recv_sem=in_sem, device_id=place, device_id_type=MESH
+        )
+
+    def to_near():
+        return send(packed, gathered.at[t], near_out.at[0], near_in.at[0], places[0])
+
+    def to_far(chunk):
+        here = rows(half, chunk)
+        return send(
+            packed.at[here], gathered.at[t, here], far_out.at[chunk], far_in.at[chunk], places[1]
+        )
+
+    def onward(which, chunk, out_sems, in_sems, place):
+        here = gathered.at[far, rows(which, chunk)]
+        return send(here, here, out_sems.at[chunk], in_sems.at[chunk], place)
+
+    def to_mate(chunk):
+        return onward(half, chunk, mate_out, mate_in, places[2])
+
+    def pass_near(chunk):
+        return onward(half, chunk, pass_out, pass_in, places[0])
+
+    def late_near(chunk):
+        return onward(1 - half, chunk, late_out, late_in, places[0])
+
+    def own():
+        return pltpu.make_async_copy(packed, gathered.at[t], own_sem.at[0])
+
+    def begin():
+        @pl.when(step == 0)
+        def _():
+            for place in places:
+                pl.semaphore_signal(barrier, inc=1, device_id=place, device_id_type=MESH)
+            own().start()
+
+    def go_on():
+        @pl.when(step == 0)
+        def _():
+            pl.semaphore_wait(barrier, len(places))
+            to_far(0).start()
+            to_far(1).start()
+            to_near().start()
+
+        @pl.when((step > 0) & (step < chunks - 1))
+        def _():
+            to_far(step + 1).start()
+
+        @pl.when(step > 0)
+        def _():
+            chunk = step - 1
+            to_far(chunk).wait_recv()
+            to_mate(chunk).start()
+            pass_near(chunk).start()
+
+        @pl.when(step > 2)
+        def _():
+            chunk = step - 3
+            to_mate(chunk).wait_recv()
+            late_near(chunk).start()
+
+    def finish():
+        @pl.when(step == final)
+        def _():
+            for chunk in (chunks - 2, chunks - 1):
+                to_mate(chunk).wait_recv()
+                late_near(chunk).start()
+            own().wait()
+            to_near().wait()
+            for chunk in range(chunks):
+                pass_near(chunk).wait_recv()
+                late_near(chunk).wait_recv()
+                to_far(chunk).wait_send()
+                to_mate(chunk).wait_send()
+                pass_near(chunk).wait_send()
+                late_near(chunk).wait_send()
+
+    return begin, go_on, finish
+
+
 def forward_kernel(
     lengths_ref,
     counts_ref,
@@ -240,56 +422,134 @@
     v_ref,
     ek_ref,
     eq_ref,
+    packed_any,
     context_ref,
     p1_ref,
     p2_ref,
     p3_ref,
+    gathered_any,
     shift_scr,
+    score_scr,
+    prob_scr,
+    own_sem,
+    *gather_sems,
 ):
+    gather_start, gather_step, gather_end = gather_moves(
+        packed_any, gathered_any, own_sem, gather_sems
+    )
+    gather_start()
     eye = unit_matrix(False)
-    anti = unit_matrix(True)
-    factor = (3.0 * DH) ** -0.5
+    factor = 1.4426950408889634 * (3.0 * DH) ** -0.5
     counts = live_counts(lengths_ref, counts_ref)
-    for slot, (start, length) in enumerate(SLOTS):
-        keys = k_ref[start : start + length, :]
-        values = v_ref[start : start + length, :]
-        live = lax.broadcasted_iota(jnp.int32, (1, length), 1) < counts[slot]
-        for t in range(length // TILE):
-            low = LEN3 - TILE - TILE * t
-            here = keys[t * TILE : (t + 1) * TILE]
-            table = dot_nn(each_head(here), eq_ref[:, low : low + length + TILE])
-            for member in range(2):
-                shift_scr[member, start + t * TILE : start + (t + 1) * TILE, :length] = skew(
-                    table[member * TILE : (member + 1) * TILE], length
-                ).astype(bf16)
-        for t in range(length // TILE):
-            low = LEN3 - TILE - TILE * t
-            row = start + t * TILE
-            queries = each_head(q_ref[row : row + TILE, :])
-            table = dot_nn(queries, ek_ref[:, low : low + length + TILE])
-            probs = []
-            for member in range(2):
-                mine = slice(member * TILE, (member + 1) * TILE)
-                left = jnp.concatenate([queries[mine], eye], axis=1)
-                shifted = shift_scr[
-                    member, start : start + length, t * TILE : (t + 1) * TILE
-                ]
-                right = jnp.concatenate([keys, shifted], axis=1)
-                scores = dot_nt(left, right) + skew(table[mine], length)
-                scores = jnp.where(live, scores * factor, masked_score)
-                weights = jnp.exp(scores - jnp.max(scores, axis=1, keepdims=True))
-                prob = weights * (1.0 / jnp.sum(weights, axis=1, keepdims=True))
-                probs.append(prob.astype(bf16))
-            context = dot_nn(jnp.concatenate(probs, axis=0), values)
-            context_ref[row : row + TILE, :] = own_lanes(context).astype(bf16)
-            for member in range(2):
-                turned = dot_nn(anti, probs[member]).astype(bf16)
-                if length == LEN1:
-                    p1_ref[member, row : row + TILE, :] = turned
-                elif length == LEN3:
-                    p3_ref[member, t * TILE : (t + 1) * TILE, :] = turned
-                else:
-                    p2_ref[member, t * TILE : (t + 1) * TILE, :] = turned
+    turned_values = v_ref[...].T
+    head_rows = [
+        jnp.where(
+            lax.broadcasted_iota(jnp.int32, (PAIR, 1), 0) // DH == member, 1.0, 0.0
+        ).astype(bf16)
+        for member in range(2)
+    ]
+
+    def place(slot, t):
+        start, length = SLOTS[slot]
+        low = LEN3 - TILE - TILE * t
+        row = start + t * TILE
+        return start, length, slice(row, row + TILE), slice(low, low + length + TILE)
+
+    def shift_unit(slot, t):
+        start, length, rows, window = place(slot, t)
+        table = dot_nn(each_head(q_ref[rows, :]), ek_ref[:, window])
+        for member in range(2):
+            shift_scr[member, rows, :length] = skew(
+                table[member * TILE : (member + 1) * TILE], length
+            ).astype(bf16)
+
+    def score_unit(slot, t):
+        start, length, rows, window = place(slot, t)
+        keys = each_head(k_ref[rows, :])
+        table = dot_nn(keys, eq_ref[:, window])
+        queries = q_ref[start : start + length, :]
+        live = lax.broadcasted_iota(jnp.int32, (TILE, 1), 0) < counts[slot] - t * TILE
+        tops = []
+        for member in range(2):
+            mine = slice(member * TILE, (member + 1) * TILE)
+            left = jnp.concatenate([keys[mine], eye], axis=1)
+            shifted = shift_scr[member, start : start + length, t * TILE : (t + 1) * TILE]
+            right = jnp.concatenate([queries, shifted], axis=1)
+            raw = dot_nt(left, right) + skew(table[mine], length)
+            raw = jnp.where(live, raw * factor, masked_score)
+            score_scr[member, rows, :length] = raw
+            tops.append(jnp.max(raw, axis=0, keepdims=True))
+        return tops
+
+    def weight_unit(slot, t, tops):
+        start, length, rows, window = place(slot, t)
+        sums = []
+        for member in range(2):
+            weights = jnp.exp2(score_scr[member, rows, :length] - tops[member])
+            score_scr[member, rows, :length] = weights
+            sums.append(jnp.sum(weights, axis=0, keepdims=True))
+        return sums
+
+    def prob_unit(slot, t, inverses):
+        start, length, rows, window = place(slot, t)
+        for member in range(2):
+            prob = score_scr[member, rows, :length] * inverses[member]
+            prob_scr[member, rows, :length] = prob.astype(bf16)
+            prob_block((p1_ref, p2_ref, p3_ref), slot, t, member)[...] = flip_rows(prob).astype(
+                bf16
+            )
+
+    def context_unit(slot):
+        start, length = SLOTS[slot]
+        here = slice(start, start + length)
+        left = jnp.concatenate([turned_values[:, here] * rows for rows in head_rows], axis=1)
+        right = jnp.concatenate([prob_scr[member, here, :length] for member in range(2)], axis=0)
+        context_ref[here, :] = dot_nn(left, right).astype(bf16).T
+
+    def both(function, parts):
+        return [function(member_parts) for member_parts in zip(*parts)]
+
+    def largest(parts):
+        total = parts[0]
+        for part in parts[1:]:
+            total = jnp.maximum(total, part)
+        return total
+
+    groups = ((3,), (2, 1, 0))
+    tiles = [[unit for slot in group for unit in slot_tiles(slot)] for group in groups]
+    held = {}
+
+    def settle(slot):
+        held[slot] = both(largest, [held.pop(unit) for unit in slot_tiles(slot)])
+
+    def invert(slot):
+        total = both(sum, [held.pop(unit) for unit in slot_tiles(slot)])
+        held[slot] = [1.0 / part for part in total]
+
+    for unit in tiles[0]:
+        shift_unit(*unit)
+    gather_step()
+    for first, second in zip(tiles[0], tiles[1]):
+        held[first] = score_unit(*first)
+        shift_unit(*second)
+    settle(3)
+    for first, second in zip(tiles[0], tiles[1]):
+        held[second] = score_unit(*second)
+        held[first] = weight_unit(*first, held[3])
+    invert(3)
+    for slot in groups[1]:
+        settle(slot)
+    for first, second in zip(tiles[0], tiles[1]):
+        held[second] = weight_unit(*second, held[second[0]])
+        prob_unit(*first, held[3])
+    for slot in groups[1]:
+        invert(slot)
+    context_unit(3)
+    for second in tiles[1]:
+        prob_unit(*second, held[second[0]])
+    for slot in groups[1]:
+        context_unit(slot)
+    gather_end()
 
 
 PAIR_SPEC = pl.BlockSpec((ROWS, PAIR), lambda p: (0, p))
@@ -298,20 +558,35 @@
 PROB_SPECS = [pl.BlockSpec((2, *size), lambda p: (p, 0, 0)) for size in PROB_SIZES]
 
 
-def attend_forward(lengths, counts, q, k, v, ek, eq):
+def attend_forward(lengths, counts, q, k, v, ek, eq, packed):
+    chunks = HALF // CHUNK
+    single, several = (pltpu.SemaphoreType.DMA((n,)) for n in (1, chunks))
+    inner = lax.axis_size("tensor")
+    assert inner == 4 and lax.axis_size("dp") % 2 == 0
     return pl.pallas_call(
         forward_kernel,
         grid=(H // 2,),
         in_specs=[pl.BlockSpec(memory_space=pltpu.SMEM)] * 2
         + [PAIR_SPEC] * 3
-        + [TABLE_SPEC] * 2,
-        out_specs=[PAIR_SPEC] + PROB_SPECS,
+        + [TABLE_SPEC] * 2
+        + [once(PACKED, D)],
+        out_specs=[PAIR_SPEC] + PROB_SPECS + [pl.BlockSpec(memory_space=pl.ANY)],
         out_shape=[jax.ShapeDtypeStruct((ROWS, D), bf16)]
-        + [jax.ShapeDtypeStruct((H, *size), bf16) for size in PROB_SIZES],
-        scratch_shapes=[pltpu.VMEM((2, ROWS, LEN3), bf16)],
-        compiler_params=pltpu.CompilerParams(vmem_limit_bytes=MEMORY),
+        + [jax.ShapeDtypeStruct((H, *size), bf16) for size in PROB_SIZES]
+        + [jax.ShapeDtypeStruct((inner, PACKED, D), bf16)],
+        scratch_shapes=[
+            pltpu.VMEM((2, ROWS, LEN3), bf16),
+            pltpu.VMEM((2, ROWS, LEN3), f32),
+            pltpu.VMEM((2, ROWS, LEN3), bf16),
+            pltpu.SemaphoreType.DMA((1,)),
+        ]
+        + [single] * 2
+        + [several] * 8,
+        compiler_params=pltpu.CompilerParams(
+            collective_id=1, has_side_effects=True, vmem_limit_bytes=MEMORY
+        ),
         name="attention_forward",
-    )(lengths, counts, q, k, v, ek, eq)
+    )(lengths, counts, q, k, v, ek, eq, packed)
 
 
 def backward_kernel(
@@ -319,116 +594,150 @@
     k_ref,
     v_ref,
     g_ref,
-    ek_ref,
-    fq_ref,
+    context_ref,
+    eq_ref,
+    fk_ref,
     p1_ref,
     p2_ref,
     p3_ref,
     gq_ref,
     gk_ref,
     gv_ref,
-    gek_ref,
-    gfq_ref,
+    geq_ref,
+    gfk_ref,
     grad_scr,
     turned_scr,
-    values_scr,
-    gek_scr,
-    gfq_scr,
+    geq_scr,
+    gfk_scr,
 ):
-    eye = unit_matrix(False)
     anti = unit_matrix(True)
     factor = (3.0 * DH) ** -0.5
-    gek_scr[...] = jnp.zeros_like(gek_scr)
-    gfq_scr[...] = jnp.zeros_like(gfq_scr)
-    for start, length in SLOTS:
-        count = length // TILE
-        keys = k_ref[start : start + length, :]
-        values = v_ref[start : start + length, :]
-        value_grad = jnp.zeros((PAIR, length), f32)
-        for t in range(count):
-            low = LEN3 - TILE - TILE * t
-            row = start + t * TILE
-            place = start + (count - 1 - t) * TILE
-            both = jnp.concatenate([q_ref[row : row + TILE, :], g_ref[row : row + TILE, :]], axis=1)
-            both = dot_nn(anti, both).astype(bf16)
-            turned_scr[place : place + TILE, :] = both[:, :PAIR]
-            queries = each_head(both[:, :PAIR])
-            grads = each_head(both[:, PAIR:])
-            grad_prob = dot_nt(grads, values)
-            probs, raws, spreads = [], [], []
-            for member in range(2):
-                if length == LEN1:
-                    prob = p1_ref[member, row : row + TILE, :]
-                elif length == LEN3:
-                    prob = p3_ref[member, t * TILE : (t + 1) * TILE, :]
-                else:
-                    prob = p2_ref[member, t * TILE : (t + 1) * TILE, :]
-                mine = grad_prob[member * TILE : (member + 1) * TILE]
-                wide = prob.astype(f32)
-                delta = jnp.sum(wide * mine, axis=1, keepdims=True)
-                raw = (wide * ((mine - delta) * factor)).astype(bf16)
-                grad_scr[member, place : place + TILE, :length] = raw
-                probs.append(prob)
-                raws.append(raw)
-                spreads.append(unskew(raw.astype(f32), length).astype(bf16))
-            raw = jnp.concatenate(raws, axis=0)
-            spread = jnp.concatenate(spreads, axis=0)
-            query_grad = own_lanes(
-                dot_nn(
-                    jnp.concatenate([raw, spread], axis=1),
-                    jnp.concatenate([keys, ek_ref[low : low + length + TILE, :]], axis=0),
-                )
-            )
-            gq_ref[row : row + TILE, :] = dot_nn(anti, query_grad.astype(bf16)).astype(bf16)
-            gek_scr[:, low : low + length + TILE] += dot_tn(queries, spread)
-            value_grad = value_grad + dot_tn(grads, jnp.concatenate(probs, axis=0))
-        values_scr[:, start : start + length] = value_grad
-        turned = turned_scr[start : start + length, :]
-        for t in range(count):
-            low = LEN3 - length + TILE * t
-            row = start + t * TILE
-            raws, spreads = [], []
-            for member in range(2):
-                raw = dot_nt(
-                    eye, grad_scr[member, start : start + length, t * TILE : (t + 1) * TILE]
-                )
-                raws.append(raw.astype(bf16))
-                spreads.append(unskew(raw, length).astype(bf16))
-            raw = jnp.concatenate(raws, axis=0)
-            spread = jnp.concatenate(spreads, axis=0)
-            key_grad = own_lanes(
-                dot_nn(
-                    jnp.concatenate([raw, spread], axis=1),
-                    jnp.concatenate([turned, fq_ref[low : low + length + TILE, :]], axis=0),
-                )
-            )
-            gk_ref[row : row + TILE, :] = key_grad.astype(bf16)
-            gfq_scr[:, low : low + length + TILE] += dot_tn(
-                each_head(k_ref[row : row + TILE, :]), spread
-            )
-    gv_ref[...] = values_scr[...].T.astype(bf16)
-    gek_ref[...] = gek_scr[...].astype(bf16)
-    gfq_ref[...] = gfq_scr[...].astype(bf16)
-
-
-def attend_backward(q, k, v, g, ek, fq, p1, p2, p3):
+    geq_scr[...] = jnp.zeros_like(geq_scr)
+    gfk_scr[...] = jnp.zeros_like(gfk_scr)
+    product = g_ref[...].astype(f32) * context_ref[...].astype(f32)
+    high = product.astype(bf16)
+    rest = (product - high.astype(f32)).astype(bf16)
+    lane = lax.broadcasted_iota(jnp.int32, (PAD, 2 * PAIR), 1) % PAIR
+    row = lax.broadcasted_iota(jnp.int32, (PAD, 2 * PAIR), 0)
+    summing = jnp.where(lane // DH == row, 1.0, 0.0).astype(bf16)
+    delta = dot_nt(summing, jnp.concatenate([high, rest], axis=1))
+
+    def place(slot, t):
+        start, length = SLOTS[slot]
+        row = start + t * TILE
+        return start, length, slice(row, row + TILE)
+
+    def spot(slot, t):
+        start, length = SLOTS[slot]
+        row = start + length - (t + 1) * TILE
+        return slice(row, row + TILE)
+
+    def open_unit(slot, t):
+        start, length, rows = place(slot, t)
+        both = jnp.concatenate([k_ref[rows, :], v_ref[rows, :]], axis=1)
+        both = dot_nn(anti, both).astype(bf16)
+        turned_scr[spot(slot, t), :] = both[:, :PAIR]
+        return dot_nt(each_head(both[:, PAIR:]), g_ref[start : start + length, :])
+
+    def raw_unit(slot, t, grad_prob):
+        start, length, rows = place(slot, t)
+        spreads = []
+        for member in range(2):
+            prob = prob_block((p1_ref, p2_ref, p3_ref), slot, t, member)[...].astype(f32)
+            mine = grad_prob[member * TILE : (member + 1) * TILE]
+            raw = (prob * (mine - delta[member : member + 1, start : start + length])).astype(bf16)
+            grad_scr[member, spot(slot, t), :length] = raw
+            spreads.append(unskew(raw.astype(f32), length).astype(bf16))
+        return jnp.concatenate(spreads, axis=0)
+
+    def key_unit(slot, t, spread):
+        start, length, rows = place(slot, t)
+        low = LEN3 - TILE - TILE * t
+        window = slice(low, low + length + TILE)
+        here = slice(start, start + length)
+        raw = jnp.concatenate(
+            [grad_scr[member, spot(slot, t), :length] for member in range(2)], axis=0
+        )
+        probs = jnp.concatenate(
+            [prob_block((p1_ref, p2_ref, p3_ref), slot, t, member)[...] for member in range(2)],
+            axis=0,
+        )
+        key_grad = dot_nn(
+            jnp.concatenate([raw, spread], axis=1),
+            jnp.concatenate([q_ref[here, :], eq_ref[window, :]], axis=0),
+        )
+        value_grad = dot_nn(probs, g_ref[here, :])
+        both = jnp.concatenate([own_lanes(key_grad) * factor, own_lanes(value_grad)], axis=1)
+        both = dot_nn(anti, both.astype(bf16)).astype(bf16)
+        gk_ref[rows, :] = both[:, :PAIR]
+        gv_ref[rows, :] = both[:, PAIR:]
+        geq_scr[:, window] += dot_tn(each_head(turned_scr[spot(slot, t), :]), spread)
+
+    def turn_unit(slot, t):
+        start, length, rows = place(slot, t)
+        raws, spreads = [], []
+        for member in range(2):
+            raw = grad_scr[member, start : start + length, t * TILE : (t + 1) * TILE].T
+            raws.append(raw)
+            spreads.append(unskew(raw.astype(f32), length).astype(bf16))
+        return jnp.concatenate(raws, axis=0), jnp.concatenate(spreads, axis=0)
+
+    def query_unit(slot, t, raw, spread):
+        start, length, rows = place(slot, t)
+        low = LEN3 - length + TILE * t
+        window = slice(low, low + length + TILE)
+        query_grad = dot_nn(
+            jnp.concatenate([raw, spread], axis=1),
+            jnp.concatenate(
+                [turned_scr[start : start + length, :], fk_ref[window, :]], axis=0
+            ),
+        )
+        gq_ref[rows, :] = (own_lanes(query_grad) * factor).astype(bf16)
+        gfk_scr[:, window] += dot_tn(each_head(q_ref[rows, :]), spread)
+
+    first, second = slot_tiles(3), slot_tiles(2) + slot_tiles(1) + slot_tiles(0)
+    jobs = [("key", unit) for unit in first]
+    for one, other in zip(second, first):
+        jobs += [("key", one), ("query", other)]
+    jobs += [("query", unit) for unit in second]
+    held = {}
+    for at in range(len(jobs) + 2):
+        if at < len(jobs):
+            kind, unit = jobs[at]
+            held[at] = open_unit(*unit) if kind == "key" else None
+        if 0 <= at - 1 < len(jobs):
+            kind, unit = jobs[at - 1]
+            if kind == "key":
+                held[at - 1] = raw_unit(*unit, held[at - 1])
+            else:
+                held[at - 1] = turn_unit(*unit)
+        if 0 <= at - 2 < len(jobs):
+            kind, unit = jobs[at - 2]
+            if kind == "key":
+                key_unit(*unit, held.pop(at - 2))
+            else:
+                query_unit(*unit, *held.pop(at - 2))
+    geq_ref[...] = (geq_scr[...] * factor).astype(bf16)
+    gfk_ref[...] = (gfk_scr[...] * factor).astype(bf16)
+
+
+def attend_backward(q, k, v, g, context, eq, fk, p1, p2, p3):
     return pl.pallas_call(
         backward_kernel,
         grid=(H // 2,),
-        in_specs=[PAIR_SPEC] * 6 + PROB_SPECS,
+        in_specs=[PAIR_SPEC] * 7 + PROB_SPECS,
         out_specs=[PAIR_SPEC] * 3 + [TABLE_SPEC] * 2,
         out_shape=[jax.ShapeDtypeStruct((ROWS, D), bf16)] * 3
         + [jax.ShapeDtypeStruct((D, OFFSETS), bf16)] * 2,
         scratch_shapes=[
             pltpu.VMEM((2, ROWS, LEN3), bf16),
             pltpu.VMEM((ROWS, PAIR), bf16),
-            pltpu.VMEM((PAIR, ROWS), f32),
             pltpu.VMEM((PAIR, OFFSETS), f32),
             pltpu.VMEM((PAIR, OFFSETS), f32),
         ],
         compiler_params=pltpu.CompilerParams(vmem_limit_bytes=MEMORY),
         name="attention_backward",
-    )(q, k, v, g, ek, fq, p1, p2, p3)
+    )(q, k, v, g, context, eq, fk, p1, p2, p3)
 
 
 def gelu_pair(hidden):
@@ -470,7 +779,10 @@
     packed_ref,
     factor_ref,
     scale_ref,
-    norm_ref,
+    gain_one_ref,
+    shift_one_ref,
+    gain_two_ref,
+    shift_two_ref,
     mixed_ref,
     grad_one_ref,
     context_grad_ref,
@@ -493,7 +805,10 @@
     live = jnp.zeros((BLOCK, 1), f32)
     for (start, length), used in zip(SLOTS, live_counts(lengths_ref, counts_ref)):
         live = jnp.where((row >= start) & (row < start + used), 1.0, live)
-    gain_one, shift_one, gain_two, shift_two = (norm_ref[i : i + 1, :] for i in range(4))
+    gain_one, shift_one, gain_two, shift_two = (
+        ref[...].reshape(1, D)
+        for ref in (gain_one_ref, shift_one_ref, gain_two_ref, shift_two_ref)
+    )
 
     context = context_ref[...]
     weight = weight_ref[0]
@@ -511,7 +826,7 @@
         active_scr[c] = active
         slope_scr[c] = slope
         mlp = mlp + dot_nn(active, packed_ref[c, D : 2 * D, :])
-        back_coeff = back_coeff + dot_nt(packed_ref[c, 2 * D + PAD :, :], active)
+        back_coeff = back_coeff + dot_nt(packed_ref[c, 2 * D + PAD : 2 * D + 2 * PAD, :], active)
     result, normal_two, inverse_two = norm_forward(normed + mlp, gain_two, shift_two)
     mixed_ref[...] = (result * live).astype(bf16)
     grad_two = norm_backward(
@@ -563,8 +878,8 @@
             ),
             whole(12, PAD, D),
             whole(PAD, 128),
-            whole(4, D),
-        ],
+        ]
+        + [whole(D)] * 4,
         out_specs=[tile] * 3
         + [whole(4, PAD, D), whole(2 * chunks, PAD, D), whole(PAD, 128)],
         out_shape=[
@@ -581,12 +896,7 @@
         ],
         compiler_params=pltpu.CompilerParams(vmem_limit_bytes=MEMORY),
         name="middle",
-    )(lengths, counts, tokens, context, out_grad, weights, packed, factors, scales, norms)
-
-
-LANES = 128
-BLOCKS = D // LANES
-MESH = pl.DeviceIdType.MESH
+    )(lengths, counts, tokens, context, out_grad, weights, packed, factors, scales, *norms)
 
 
 def devices():
@@ -614,16 +924,17 @@
     hidden_ref,
     middle_scale_ref,
     rel_any,
-    gek_any,
-    gfq_any,
+    geq_any,
+    gfk_any,
     in_grad_ref,
     down_out,
     up_out,
-    hidden_out,
+    hidden_up_out,
+    hidden_down_out,
     scale_out,
     rel_scr,
-    gek_scr,
-    gfq_scr,
+    geq_scr,
+    gfk_scr,
     down_scr,
     up_scr,
     scale_scr,
@@ -724,7 +1035,7 @@
     def load(number, src, dst):
         return pltpu.make_async_copy(src, dst, load_sem.at[number])
 
-    loads = ((0, rel_any, rel_scr), (1, gek_any, gek_scr), (2, gfq_any, gfq_scr))
+    loads = ((0, rel_any, rel_scr), (1, geq_any, geq_scr), (2, gfk_any, gfk_scr))
 
     @pl.when(step == 0)
     def _():
@@ -775,7 +1086,7 @@
             load(*piece).wait()
         rel = rel_scr[...]
         bucket = lax.broadcasted_iota(jnp.int32, (2 * SPAN, OFFSETS), 0)
-        for member, ref, row in ((0, gfq_scr, 1), (1, gek_scr, 0)):
+        for member, ref, row in ((0, geq_scr, 0), (1, gfk_scr, 1)):
             scale = scale_ref[:, member : member + 1]
             chosen = jnp.where(bucket == index_ref[row : row + 1, :], 1.0, 0.0).astype(bf16)
             grad = dot_nt(ref[...], chosen).astype(bf16)
@@ -850,7 +1161,8 @@
             for block in range(BLOCKS):
                 tile = which * BLOCKS + block
                 at = tile % tiles * PAD
-                hidden_out[which, :, block * LANES : (block + 1) * LANES] = all_hidden[
+                out = (hidden_up_out, hidden_down_out)[which]
+                out[:, block * LANES : (block + 1) * LANES] = all_hidden[
                     tile // tiles, at : at + PAD
                 ].astype(f32)[:RANK]
 
@@ -889,7 +1201,7 @@
 
 def last(
     tokens, gq, gk, gv, grad_one, coeff, weights, index, rel_coeff, factors, scales,
-    small, hidden, middle_scale, rel, gek, gfq,
+    small, hidden, middle_scale, rel, geq, gfk,
 ):
     count = devices()
     outer = lax.axis_size("dp")
@@ -919,14 +1231,16 @@
             tile,
             whole(5, RANK, D),
             whole(5, RANK, D),
-            whole(2, RANK, D),
+            whole(RANK, D),
+            whole(RANK, D),
             whole(6, RANK),
         ],
         out_shape=[
             jax.ShapeDtypeStruct((ROWS, D), f32),
             factor,
             factor,
-            jax.ShapeDtypeStruct((2, RANK, D), f32),
+            jax.ShapeDtypeStruct((RANK, D), f32),
+            jax.ShapeDtypeStruct((RANK, D), f32),
             jax.ShapeDtypeStruct((6, RANK), f32),
         ],
         scratch_shapes=[
@@ -955,7 +1269,7 @@
         name="last",
     )(
         tokens, gq, gk, gv, grad_one, coeff, weights, index, rel_coeff, factors, scales,
-        small, hidden, middle_scale, rel, gek, gfq,
+        small, hidden, middle_scale, rel, geq, gfk,
     )
 
 
@@ -980,31 +1294,28 @@
     rel_bucket,
     out_grad,
 ):
-    factors = jnp.pad(
-        jnp.concatenate([adapt_down, adapt_up, hidden_up[None], hidden_down[None]], axis=0),
-        ((0, 0), (0, PAD - RANK), (0, 0)),
-    )
-    scales = jnp.pad(adapt_scale.T, ((0, PAD - RANK), (0, 128 - 6)))
     index_rows = jnp.pad(
         jnp.stack([rel_bucket[::-1], rel_bucket]), ((0, 0), (0, 1)), constant_values=-1
     )
-    norms = jnp.stack([gain_one, shift_one, gain_two, shift_two])
-    packed = lax.all_gather(
-        pack_weights(in_weight, back_weight, factors, scales), "tensor", axis=0
-    )
-    q, k, v, ek, fq, ekt, eqt, weights, coeff, rel_coeff = project(
-        tokens, qkv_weight, out_weight, rel_embed, index_rows, factors, scales
-    )
-    context, p1, p2, p3 = attend_forward(seq_lengths, seq_counts, q, k, v, ekt, eqt)
+    norms = (gain_one, shift_one, gain_two, shift_two)
+    q, k, v, eq, fk, ekt, eqt, weights, packed, coeff, rel_coeff, factors, scales = project(
+        tokens, qkv_weight, rel_embed, index_rows, adapt_down, adapt_up, hidden_up, hidden_down,
+        adapt_scale, out_weight, in_weight, back_weight,
+    )
+    context, p1, p2, p3, gathered = attend_forward(
+        seq_lengths, seq_counts, q, k, v, ekt, eqt, packed
+    )
     mixed, grad_one, context_grad, small, hidden, middle_scale = middle(
-        seq_lengths, seq_counts, tokens, context, out_grad, weights, packed, factors, scales, norms
-    )
-    gq, gk, gv, gek, gfq = attend_backward(q, k, v, context_grad, ek, fq, p1, p2, p3)
-    in_grad, down_grad, up_grad, hidden_grad, scale_grad = last(
+        seq_lengths, seq_counts, tokens, context, out_grad, weights, gathered, factors, scales, norms
+    )
+    gq, gk, gv, geq, gfk = attend_backward(
+        q, k, v, context_grad, context, eq, fk, p1, p2, p3
+    )
+    in_grad, down_grad, up_grad, hidden_up_grad, hidden_down_grad, scale_grad = last(
         tokens, gq, gk, gv, grad_one, coeff, weights, index_rows, rel_coeff, factors, scales,
-        small, hidden, middle_scale, rel_embed, gek, gfq,
-    )
-    return (mixed, in_grad, down_grad, up_grad, hidden_grad[0], hidden_grad[1], scale_grad)
+        small, hidden, middle_scale, rel_embed, geq, gfk,
+    )
+    return (mixed, in_grad, down_grad, up_grad, hidden_up_grad, hidden_down_grad, scale_grad)
 
 
 def solution(mesh):

time: 230 us -> 190 us (0.83)
  between operations: 14.1 us -> 0.72 us
  Pallas kernels: 192 us -> 180 us
  waiting for transfers between devices: 10.5 us -> 0 us
    pallas_call x3 -> x2, Pallas kernels: 74.5 us -> 56.6 us  [the longest x1 38.3 us: attend_backward(): pl.pallas_call(backward_kernel, grid=(H // 2,), in_specs=[PAIR_SPEC] * 7...]
    all_gather x1 -> x0, waiting for transfers between devices: 10.5 us -> none  [on_device(): lax.all_gather(pack_weights(in_weight, back_weight, factors, scales), 'te...]
    pallas_call x1, Pallas kernels: 38.4 us -> 43.5 us  [attend_forward(): pl.pallas_call(forward_kernel, grid=(H // 2,), in_specs=[pl.BlockSpec(mem...]
    unnamed x23 -> x18, local copies, waits for them, and re-layouts: 7.42 us -> 7.9 us
  transfers between devices with their start and end apart: 1 -> 0, of which waited for: 1 -> 0; matrix products, arithmetic and copies ran while one was open for 1% -> 0% of each run, Pallas kernels for 24% -> 0%
where the time goes in v4:
time: 190 us
  Pallas kernels  180 us (95%)
  local copies, waits for them, and re-layouts  8.5 us (4%)
    pallas_call x1, Pallas kernels, middle(): pl.pallas_call(middle_kernel, grid=(ROWS // BLOCK,), in_specs=[pl.BlockSp...  47.4 us
    pallas_call x1, Pallas kernels, attend_forward(): pl.pallas_call(forward_kernel, grid=(H // 2,), in_specs=[pl.BlockSpec(mem...  43.5 us
    pallas_call x1, Pallas kernels, attend_backward(): pl.pallas_call(backward_kernel, grid=(H // 2,), in_specs=[PAIR_SPEC] * 7...  38.3 us
    pallas_call x1, Pallas kernels, last(): pl.pallas_call(last_kernel, grid=(ROWS // BLOCK,), in_specs=[tile] * 5 +...  32.3 us
    pallas_call x1, Pallas kernels, project(): pl.pallas_call(project_kernel, grid=(ROWS // BLOCK,), in_specs=[tile, onc...  18.3 us
    unnamed x18, local copies, waits for them, and re-layouts  7.9 us

profile of v4, /device:TPU:0, one launch (start us, length us, event | category | flops | bytes accessed | tf_op | source)
XLA Modules:
  0.0 189.7 jit_solution(10615738777759507307)
XLA Ops:
  0.6 0.8 reverse
  1.4 0.1 slice
  1.5 0.7 pad_add_fusion
  2.2 0.6 pad.4.index_ref
  2.8 18.3 %project.1 = (bf16[1024,768]{1,0:T(8,128)(2,1)}, bf16[1024,768]{1,0:T(8,128)(2,1)}, bf16[1024,768]{1,0:T(8,128)(2,1)}, bf16[1024,768]{1,0:T(8,128)(2,1)}, bf16[1...) custom-call(bf16[1024,768]{1,0:T(8,128)(2,1)} %tokens_ref.5, ...), custom_call_target="tpu_custom_call" | custom-call | tf_op jit(solution)/shard_map/project/pallas_call | solution.py:181
  21.1 43.5 %attention_forward.1 = (bf16[1024,768]{1,0:T(8,128)(2,1)}, bf16[12,256,128]{2,1,0:T(8,128)(2,1)}, bf16[12,256,256]{2,1,0:T(8,128)(2,1)}, bf16[12,512,512]{2,1,0:T(8,128)(2,1)}, bf16[4,1600,768]{2,1,0:T(8,128)(2,1)}) custom-call(s32[1,4]{1,0:T(1,128)} %lengths_ref.3, s32[1,3]{1,0:T(1,128)} %counts_ref.3, bf16[1024,768]{1,0:T(8,128)(2,1)} %get-tuple-element.42.q_ref, ...), custom_call_target="tpu_custom_call" | custom-call | tf_op jit(solution)/shard_map/attention_forward/pallas_call | solution.py:566
  64.6 47.4 %middle.1 = (bf16[1024,768]{1,0:T(8,128)(2,1)}, f32[1024,768]{1,0:T(8,128)}, bf16[1024,768]{1,0:T(8,128)(2,1)}, f32[4,16,768]{2,1,0:T(8,128)}, f32[8,16,768]{2,1,0:T(8,128)}, /*index=5*/f32[16,128]{1,0:T(8,128)}) custom-call(s32[1,4]{1,0:T(1,128)} %lengths_ref.3, s32[1,3]{1,0:T(1,128)} %counts_ref.3, bf16[1024,768]{1,0:T(8,128)(2,1)} %tokens_ref.5, ...), custom_call_target="tpu_custom_call" | custom-call | tf_op jit(solution)/shard_map/middle/pallas_call | solution.py:869
  112.0 38.3 %attention_backward.1 = (bf16[1024,768]{1,0:T(8,128)(2,1)}, bf16[1024,768]{1,0:T(8,128)(2,1)}, bf16[1024,768]{1,0:T(8,128)(2,1)}, bf16[768,1024]{1,0:T(8,128)(2,1)}, bf16[768,1024]{1,0:T(8,128)(2,1)}) custom-call(bf16[1024,768]{1,0:T(8,128)(2,1)} %get-tuple-element.42.q_ref, bf16[1024,768]{1,0:T(8,128)(2,1)} %get-tuple-element.43.k_ref, ...), custom_call_target="tpu_custom_call" | custom-call | tf_op jit(solution)/shard_map/attention_backward/pallas_call | solution.py:725
  150.3 32.3 %last.1 = (f32[1024,768]{1,0:T(8,128)}, f32[5,12,768]{2,1,0:T(8,128)}, f32[5,12,768]{2,1,0:T(8,128)}, f32[12,768]{1,0:T(8,128)}, f32[12,768]{1,0:T(8,128)}, /*index=5*/f32[6,12]{1,0:T(8,128)}) custom-call(bf16[1024,768]{1,0:T(8,128)(2,1)} %tokens_ref.5, bf16[1024,768]{1,0:T(8,128)(2,1)} %get-tuple-element.60.gq_ref, ...), custom_call_target="tpu_custom_call" | custom-call | tf_op jit(solution)/shard_map/last/pallas_call | solution.py:1214
  182.6 0.0 copy-start.1
  182.6 0.0 copy-start
  182.6 0.0 copy-start.3
  182.6 0.0 copy-start.2
  182.6 0.0 copy-start.4
  182.6 3.8 %copy.32 = f32[1024,768]{1,0:T(8,128)} copy(f32[1024,768]{1,0:T(8,128)} %get-tuple-element.85) | data formatting | bytes 6291456
  186.5 0.0 copy-done.1
  186.5 0.7 copy.33
  187.2 0.0 copy-done
  187.2 0.7 copy.34
  187.9 0.0 copy-done.3
  187.9 0.6 copy.35
  188.5 0.0 copy-done.2
  188.5 0.6 copy.36
  189.1 0.0 copy-done.4
  189.1 0.6 copy.37
Async XLA Ops:
  182.6 3.9 %copy-start.1 = (f32[5,12,768]{2,1,0:T(8,128)S(1)}, f32[5,12,768]{2,1,0:T(8,128)}, u32[]{:S(2)}) copy-start(f32[5,12,768]{2,1,0:T(8,128)} %get-tuple-element.86) | copy-start | bytes 552964
  182.6 4.6 %copy-start = (f32[5,12,768]{2,1,0:T(8,128)S(1)}, f32[5,12,768]{2,1,0:T(8,128)}, u32[]{:S(2)}) copy-start(f32[5,12,768]{2,1,0:T(8,128)} %get-tuple-element.87) | copy-start | bytes 552964
  182.6 5.3 %copy-start.3 = (f32[12,768]{1,0:T(8,128)S(1)}, f32[12,768]{1,0:T(8,128)}, u32[]{:S(2)}) copy-start(f32[12,768]{1,0:T(8,128)} %get-tuple-element.88) | copy-start | bytes 110596
  182.6 5.9 %copy-start.2 = (f32[12,768]{1,0:T(8,128)S(1)}, f32[12,768]{1,0:T(8,128)}, u32[]{:S(2)}) copy-start(f32[12,768]{1,0:T(8,128)} %get-tuple-element.89) | copy-start | bytes 110596
  182.6 6.5 %copy-start.4 = (f32[6,12]{1,0:T(8,128)S(1)}, f32[6,12]{1,0:T(8,128)}, u32[]{:S(2)}) copy-start(f32[6,12]{1,0:T(8,128)} %get-tuple-element.90) | copy-start | bytes 868

commit v5 on v4

--- a/solution.py
+++ b/solution.py
@@ -22,6 +22,10 @@
 PACKED = 1600
 HALF = PACKED // 2
 CHUNK = HALF // 5
+TILES = ROWS // BLOCK
+SUMMED = 2
+WIDE = 1 * BLOCK
+LAG = 1
 LANES = 128
 BLOCKS = D // LANES
 MESH = pl.DeviceIdType.MESH
@@ -72,158 +76,12 @@
     return jnp.concatenate([rows.astype(f32), jnp.zeros((PAD - RANK, D), f32)], axis=0).astype(bf16)
 
 
-def project_kernel(
-    tokens_ref,
-    qkv_ref,
-    rel_ref,
-    index_ref,
-    down_ref,
-    up_ref,
-    hidden_up_ref,
-    hidden_down_ref,
-    adapt_scale_ref,
-    out_any,
-    in_any,
-    back_any,
-    q_ref,
-    k_ref,
-    v_ref,
-    eq_ref,
-    fk_ref,
-    ekt_ref,
-    eqt_ref,
-    merged_ref,
-    packed_ref,
-    coeff_ref,
-    rel_coeff_ref,
-    factor_ref,
-    scale_ref,
-    pos_scr,
-    load_scr,
-    load_sem,
-):
-    step = pl.program_id(0)
-    loads = [
-        pltpu.make_async_copy(ref, load_scr.at[number], load_sem.at[number])
-        for number, ref in enumerate((out_any, in_any, back_any))
-    ]
-
-    @pl.when(step == 0)
-    def _():
-        for load in loads:
-            load.start()
-        for number in range(5):
-            factor_ref[number] = padded(down_ref[number])
-            factor_ref[5 + number] = padded(up_ref[number])
-        factor_ref[10] = padded(hidden_up_ref[...])
-        factor_ref[11] = padded(hidden_down_ref[...])
-        wide = jnp.concatenate([adapt_scale_ref[...], jnp.zeros((6, LANES - RANK), f32)], axis=1)
-        wide = jnp.concatenate([wide, jnp.zeros((LANES - 6, LANES), f32)], axis=0)
-        scale_ref[...] = wide.T[:PAD]
-        for member in range(3):
-            merged_ref[member] = merged(
-                qkv_ref[member],
-                factor_ref[member],
-                factor_ref[5 + member],
-                scale_ref[:, member : member + 1],
-            )
-        rel = rel_ref[...]
-        for member in range(2):
-            pos_scr[member] = dot_nn(rel, merged_ref[member]).astype(bf16)
-        coeff = dot_nt(factor_ref[:2].reshape(2 * PAD, D), rel)
-        rel_coeff_ref[...] = coeff.reshape(2, PAD, 2 * SPAN)
-
-    @pl.when(step == 1)
-    def _():
-        for load in loads:
-            load.wait()
-        packed_ref[:D] = merged(load_scr[1], factor_ref[4], factor_ref[10], scale_ref[:, 4:5])
-        packed_ref[2 * D : 2 * D + PAD] = factor_ref[10]
-        packed_ref[2 * D + PAD : 2 * D + 2 * PAD] = factor_ref[11]
-        packed_ref[2 * D + 2 * PAD :] = jnp.zeros((PACKED - 2 * D - 2 * PAD, D), bf16)
-
-    @pl.when(step == 2)
-    def _():
-        packed_ref[D : 2 * D] = merged(load_scr[2], factor_ref[11], factor_ref[9], scale_ref[:, 5:6])
-
-    @pl.when(step == 3)
-    def _():
-        merged_ref[3] = merged(load_scr[0], factor_ref[3], factor_ref[8], scale_ref[:, 3:4])
-
-    tokens = tokens_ref[...]
-    for member, ref in enumerate((q_ref, k_ref, v_ref)):
-        ref[...] = dot_nn(tokens, merged_ref[member]).astype(bf16)
-    coeff_ref[...] = dot_nt(factor_ref[:3].reshape(3 * PAD, D), tokens).reshape(3, PAD, BLOCK)
-    bucket = lax.broadcasted_iota(jnp.int32, (2 * SPAN, BLOCK), 0)
-    back, forth = (
-        jnp.where(bucket == index_ref[row : row + 1, :], 1.0, 0.0).astype(bf16) for row in range(2)
-    )
-    eq_ref[...] = dot_tn(back, pos_scr[0]).astype(bf16)
-    fk_ref[...] = dot_tn(forth, pos_scr[1]).astype(bf16)
-    ekt_ref[...] = dot_tn(pos_scr[1], back).astype(bf16)
-    eqt_ref[...] = dot_tn(pos_scr[0], back).astype(bf16)
-
-
 def whole(*shape):
     return pl.BlockSpec(shape, lambda *at: (0,) * len(shape))
 
 
 def once(*shape):
     return pl.BlockSpec(shape, lambda *at: (0,) * len(shape), pipeline_mode=pl.Buffered(1))
-
-
-def project(
-    tokens, qkv_weight, rel_embed, index_rows, down, up, hidden_up, hidden_down, adapt_scale,
-    out_weight, in_weight, back_weight,
-):
-    tile = pl.BlockSpec((BLOCK, D), lambda i: (i, 0))
-    rows = jax.ShapeDtypeStruct((ROWS, D), bf16)
-    return pl.pallas_call(
-        project_kernel,
-        grid=(ROWS // BLOCK,),
-        in_specs=[
-            tile,
-            once(3, D, D),
-            once(2 * SPAN, D),
-            pl.BlockSpec((2, BLOCK), lambda i: (0, i)),
-            once(5, RANK, D),
-            once(5, RANK, D),
-            once(RANK, D),
-            once(RANK, D),
-            once(6, RANK),
-        ]
-        + [pl.BlockSpec(memory_space=pl.ANY)] * 3,
-        out_specs=[tile] * 5
-        + [pl.BlockSpec((D, BLOCK), lambda i: (0, i))] * 2
-        + [
-            whole(4, D, D),
-            whole(PACKED, D),
-            pl.BlockSpec((3, PAD, BLOCK), lambda i: (0, 0, i)),
-            whole(2, PAD, 2 * SPAN),
-            whole(12, PAD, D),
-            whole(PAD, LANES),
-        ],
-        out_shape=[rows] * 5
-        + [jax.ShapeDtypeStruct((D, OFFSETS), bf16)] * 2
-        + [
-            jax.ShapeDtypeStruct((4, D, D), bf16),
-            jax.ShapeDtypeStruct((PACKED, D), bf16),
-            jax.ShapeDtypeStruct((3, PAD, ROWS), f32),
-            jax.ShapeDtypeStruct((2, PAD, 2 * SPAN), f32),
-            jax.ShapeDtypeStruct((12, PAD, D), bf16),
-            jax.ShapeDtypeStruct((PAD, LANES), f32),
-        ],
-        scratch_shapes=[
-            pltpu.VMEM((2, 2 * SPAN, D), bf16),
-            pltpu.VMEM((3, D, D), bf16),
-            pltpu.SemaphoreType.DMA((3,)),
-        ],
-        compiler_params=pltpu.CompilerParams(vmem_limit_bytes=MEMORY),
-        name="project",
-    )(
-        tokens, qkv_weight, rel_embed, index_rows, down, up, hidden_up, hidden_down, adapt_scale,
-        out_weight, in_weight, back_weight,
-    )
 
 
 def unit_matrix(flipped):
@@ -318,7 +176,6 @@
 
 def gather_moves(packed, gathered, own_sem, sems):
     step = pl.program_id(0)
-    final = pl.num_programs(0) - 1
     d = lax.axis_index("dp")
     t = lax.axis_index("tensor")
     near = t + 1 - 2 * lax.rem(t, 2)
@@ -364,80 +221,57 @@
         return pltpu.make_async_copy(packed, gathered.at[t], own_sem.at[0])
 
     def begin():
-        @pl.when(step == 0)
-        def _():
-            for place in places:
-                pl.semaphore_signal(barrier, inc=1, device_id=place, device_id_type=MESH)
-            own().start()
+        for place in places:
+            pl.semaphore_signal(barrier, inc=1, device_id=place, device_id_type=MESH)
 
     def go_on():
         @pl.when(step == 0)
         def _():
+            own().start()
             pl.semaphore_wait(barrier, len(places))
             to_far(0).start()
             to_far(1).start()
             to_near().start()
 
-        @pl.when((step > 0) & (step < chunks - 1))
+        for chunk, when in ((2, 2), (3, 4), (4, 5)):
+
+            @pl.when(step == when)
+            def _(chunk=chunk):
+                to_far(chunk).start()
+
+        @pl.when((step >= TILES) & (step < TILES + chunks))
         def _():
-            to_far(step + 1).start()
-
-        @pl.when(step > 0)
-        def _():
-            chunk = step - 1
+            chunk = step - TILES
             to_far(chunk).wait_recv()
             to_mate(chunk).start()
             pass_near(chunk).start()
 
-        @pl.when(step > 2)
+        @pl.when((step >= TILES + 2) & (step < TILES + 1 + chunks))
         def _():
-            chunk = step - 3
+            chunk = step - TILES - 2
             to_mate(chunk).wait_recv()
             late_near(chunk).start()
 
     def finish():
-        @pl.when(step == final)
-        def _():
-            for chunk in (chunks - 2, chunks - 1):
-                to_mate(chunk).wait_recv()
-                late_near(chunk).start()
-            own().wait()
-            to_near().wait()
-            for chunk in range(chunks):
-                pass_near(chunk).wait_recv()
-                late_near(chunk).wait_recv()
-                to_far(chunk).wait_send()
-                to_mate(chunk).wait_send()
-                pass_near(chunk).wait_send()
-                late_near(chunk).wait_send()
+        to_mate(chunks - 1).wait_recv()
+        late_near(chunks - 1).start()
+        own().wait()
+        to_near().wait()
+        for chunk in range(chunks):
+            pass_near(chunk).wait_recv()
+            late_near(chunk).wait_recv()
+            to_far(chunk).wait_send()
+            to_mate(chunk).wait_send()
+            pass_near(chunk).wait_send()
+            late_near(chunk).wait_send()
 
     return begin, go_on, finish
 
 
-def forward_kernel(
-    lengths_ref,
-    counts_ref,
-    q_ref,
-    k_ref,
-    v_ref,
-    ek_ref,
-    eq_ref,
-    packed_any,
-    context_ref,
-    p1_ref,
-    p2_ref,
-    p3_ref,
-    gathered_any,
-    shift_scr,
-    score_scr,
-    prob_scr,
-    own_sem,
-    *gather_sems,
+def attend(
+    lengths_ref, counts_ref, q_ref, k_ref, v_ref, ek_ref, eq_ref, context_ref, p1_ref, p2_ref, p3_ref,
+    shift_scr, score_scr, prob_scr,
 ):
-    gather_start, gather_step, gather_end = gather_moves(
-        packed_any, gathered_any, own_sem, gather_sems
-    )
-    gather_start()
     eye = unit_matrix(False)
     factor = 1.4426950408889634 * (3.0 * DH) ** -0.5
     counts = live_counts(lengths_ref, counts_ref)
@@ -528,7 +362,6 @@
 
     for unit in tiles[0]:
         shift_unit(*unit)
-    gather_step()
     for first, second in zip(tiles[0], tiles[1]):
         held[first] = score_unit(*first)
         shift_unit(*second)
@@ -549,7 +382,175 @@
         prob_unit(*second, held[second[0]])
     for slot in groups[1]:
         context_unit(slot)
-    gather_end()
+
+
+def front_kernel(
+    lengths_ref,
+    counts_ref,
+    tokens_ref,
+    index_ref,
+    down_ref,
+    up_ref,
+    hidden_up_ref,
+    hidden_down_ref,
+    adapt_scale_ref,
+    in_any,
+    back_any,
+    qkv_any,
+    rel_any,
+    out_any,
+    eq_ref,
+    fk_ref,
+    coeff_ref,
+    rel_coeff_ref,
+    factor_ref,
+    scale_ref,
+    context_ref,
+    p1_ref,
+    p2_ref,
+    p3_ref,
+    q_any,
+    k_any,
+    v_any,
+    merged_any,
+    gathered_any,
+    q_scr,
+    k_scr,
+    v_scr,
+    ekt_scr,
+    eqt_scr,
+    merged_scr,
+    packed_scr,
+    pos_scr,
+    in_scr,
+    back_scr,
+    qkv_scr,
+    rel_scr,
+    out_scr,
+    shift_scr,
+    score_scr,
+    prob_scr,
+    load_sem,
+    store_sem,
+    own_sem,
+    *gather_sems,
+):
+    step = pl.program_id(0)
+    gather_start, gather_step, gather_end = gather_moves(
+        packed_scr, gathered_any, own_sem, gather_sems
+    )
+    loads = [
+        pltpu.make_async_copy(src, dst, load_sem.at[number])
+        for number, (src, dst) in enumerate(
+            (
+                (in_any, in_scr),
+                (back_any, back_scr),
+                (qkv_any, qkv_scr),
+                (rel_any, rel_scr),
+                (out_any, out_scr),
+            )
+        )
+    ]
+    stores = [
+        pltpu.make_async_copy(src, dst, store_sem.at[number])
+        for number, (src, dst) in enumerate(
+            ((q_scr, q_any), (k_scr, k_any), (v_scr, v_any), (merged_scr, merged_any))
+        )
+    ]
+
+    @pl.when(step == 0)
+    def _():
+        gather_start()
+        for load in loads:
+            load.start()
+        for number in range(5):
+            factor_ref[number] = padded(down_ref[number])
+            factor_ref[5 + number] = padded(up_ref[number])
+        factor_ref[10] = padded(hidden_up_ref[...])
+        factor_ref[11] = padded(hidden_down_ref[...])
+        wide = jnp.concatenate([adapt_scale_ref[...], jnp.zeros((6, LANES - RANK), f32)], axis=1)
+        wide = jnp.concatenate([wide, jnp.zeros((LANES - 6, LANES), f32)], axis=0)
+        scale_ref[...] = wide.T[:PAD]
+        packed_scr[2 * D : 2 * D + PAD] = factor_ref[10]
+        packed_scr[2 * D + PAD : 2 * D + 2 * PAD] = factor_ref[11]
+        packed_scr[2 * D + 2 * PAD :] = jnp.zeros((PACKED - 2 * D - 2 * PAD, D), bf16)
+        loads[0].wait()
+        packed_scr[:D] = merged(in_scr[...], factor_ref[4], factor_ref[10], scale_ref[:, 4:5])
+        loads[1].wait()
+        packed_scr[D : 2 * D] = merged(back_scr[...], factor_ref[11], factor_ref[9], scale_ref[:, 5:6])
+
+    gather_step()
+
+    @pl.when(step == 0)
+    def _():
+        loads[2].wait()
+        for member in range(3):
+            merged_scr[member] = merged(
+                qkv_scr[member],
+                factor_ref[member],
+                factor_ref[5 + member],
+                scale_ref[:, member : member + 1],
+            )
+        loads[3].wait()
+        rel = rel_scr[...]
+        for member in range(2):
+            pos_scr[member] = dot_nn(rel, merged_scr[member]).astype(bf16)
+        coeff = dot_nt(factor_ref[:2].reshape(2 * PAD, D), rel)
+        rel_coeff_ref[...] = coeff.reshape(2, PAD, 2 * SPAN)
+
+    @pl.when(step == 1)
+    def _():
+        loads[4].wait()
+        merged_scr[3] = merged(out_scr[...], factor_ref[3], factor_ref[8], scale_ref[:, 3:4])
+
+    @pl.when(step < TILES)
+    def _():
+        rows = pl.ds(pl.multiple_of(step * BLOCK, BLOCK), BLOCK)
+        tokens = tokens_ref[...]
+        for member, ref in enumerate((q_scr, k_scr, v_scr)):
+            ref[rows, :] = dot_nn(tokens, merged_scr[member]).astype(bf16)
+        coeff = dot_nt(factor_ref[:3].reshape(3 * PAD, D), tokens)
+        coeff_ref[...] = coeff.reshape(3, PAD, BLOCK)
+        bucket = lax.broadcasted_iota(jnp.int32, (2 * SPAN, BLOCK), 0)
+        back, forth = (
+            jnp.where(bucket == index_ref[row : row + 1, :], 1.0, 0.0).astype(bf16)
+            for row in range(2)
+        )
+        eq_ref[...] = dot_tn(back, pos_scr[0]).astype(bf16)
+        fk_ref[...] = dot_tn(forth, pos_scr[1]).astype(bf16)
+        ekt_scr[:, rows] = dot_tn(pos_scr[1], back).astype(bf16)
+        eqt_scr[:, rows] = dot_tn(pos_scr[0], back).astype(bf16)
+
+    @pl.when(step == TILES)
+    def _():
+        for store in stores:
+            store.start()
+
+    @pl.when(step >= TILES)
+    def _():
+        lanes = pl.ds(pl.multiple_of((step - TILES) * PAIR, PAIR), PAIR)
+        attend(
+            lengths_ref,
+            counts_ref,
+            q_scr.at[:, lanes],
+            k_scr.at[:, lanes],
+            v_scr.at[:, lanes],
+            ekt_scr.at[lanes, :],
+            eqt_scr.at[lanes, :],
+            context_ref,
+            p1_ref,
+            p2_ref,
+            p3_ref,
+            shift_scr,
+            score_scr,
+            prob_scr,
+        )
+
+    @pl.when(step == pl.num_programs(0) - 1)
+    def _():
+        for store in stores:
+            store.wait()
+        gather_end()
 
 
 PAIR_SPEC = pl.BlockSpec((ROWS, PAIR), lambda p: (0, p))
@@ -558,26 +559,78 @@
 PROB_SPECS = [pl.BlockSpec((2, *size), lambda p: (p, 0, 0)) for size in PROB_SIZES]
 
 
-def attend_forward(lengths, counts, q, k, v, ek, eq, packed):
+def front(
+    lengths, counts, tokens, qkv_weight, rel_embed, index_rows, down, up, hidden_up, hidden_down,
+    adapt_scale, out_weight, in_weight, back_weight,
+):
     chunks = HALF // CHUNK
     single, several = (pltpu.SemaphoreType.DMA((n,)) for n in (1, chunks))
     inner = lax.axis_size("tensor")
     assert inner == 4 and lax.axis_size("dp") % 2 == 0
+
+    def tile_at(i):
+        return jnp.minimum(i, TILES - 1)
+
+    def pair_at(i):
+        return jnp.maximum(i - TILES, 0)
+
+    tile = pl.BlockSpec((BLOCK, D), lambda i: (tile_at(i), 0))
+    rows = jax.ShapeDtypeStruct((ROWS, D), bf16)
+    anywhere = pl.BlockSpec(memory_space=pl.ANY)
     return pl.pallas_call(
-        forward_kernel,
-        grid=(H // 2,),
+        front_kernel,
+        grid=(TILES + H // 2,),
         in_specs=[pl.BlockSpec(memory_space=pltpu.SMEM)] * 2
-        + [PAIR_SPEC] * 3
-        + [TABLE_SPEC] * 2
-        + [once(PACKED, D)],
-        out_specs=[PAIR_SPEC] + PROB_SPECS + [pl.BlockSpec(memory_space=pl.ANY)],
-        out_shape=[jax.ShapeDtypeStruct((ROWS, D), bf16)]
+        + [
+            tile,
+            pl.BlockSpec((2, BLOCK), lambda i: (0, tile_at(i))),
+            once(5, RANK, D),
+            once(5, RANK, D),
+            once(RANK, D),
+            once(RANK, D),
+            once(6, RANK),
+        ]
+        + [anywhere] * 5,
+        out_specs=[tile] * 2
+        + [
+            pl.BlockSpec((3, PAD, BLOCK), lambda i: (0, 0, tile_at(i))),
+            whole(2, PAD, 2 * SPAN),
+            whole(12, PAD, D),
+            whole(PAD, LANES),
+            pl.BlockSpec((ROWS, PAIR), lambda i: (0, pair_at(i))),
+        ]
+        + [pl.BlockSpec((2, *size), lambda i: (pair_at(i), 0, 0)) for size in PROB_SIZES]
+        + [anywhere] * 5,
+        out_shape=[rows] * 2
+        + [
+            jax.ShapeDtypeStruct((3, PAD, ROWS), f32),
+            jax.ShapeDtypeStruct((2, PAD, 2 * SPAN), f32),
+            jax.ShapeDtypeStruct((12, PAD, D), bf16),
+            jax.ShapeDtypeStruct((PAD, LANES), f32),
+            rows,
+        ]
         + [jax.ShapeDtypeStruct((H, *size), bf16) for size in PROB_SIZES]
-        + [jax.ShapeDtypeStruct((inner, PACKED, D), bf16)],
-        scratch_shapes=[
+        + [rows] * 3
+        + [
+            jax.ShapeDtypeStruct((4, D, D), bf16),
+            jax.ShapeDtypeStruct((inner, PACKED, D), bf16),
+        ],
+        scratch_shapes=[pltpu.VMEM((ROWS, D), bf16)] * 3
+        + [pltpu.VMEM((D, OFFSETS), bf16)] * 2
+        + [
+            pltpu.VMEM((4, D, D), bf16),
+            pltpu.VMEM((PACKED, D), bf16),
+            pltpu.VMEM((2, 2 * SPAN, D), bf16),
+            pltpu.VMEM((D, D), bf16),
+            pltpu.VMEM((D, D), bf16),
+            pltpu.VMEM((3, D, D), bf16),
+            pltpu.VMEM((2 * SPAN, D), bf16),
+            pltpu.VMEM((D, D), bf16),
             pltpu.VMEM((2, ROWS, LEN3), bf16),
             pltpu.VMEM((2, ROWS, LEN3), f32),
             pltpu.VMEM((2, ROWS, LEN3), bf16),
+            pltpu.SemaphoreType.DMA((5,)),
+            pltpu.SemaphoreType.DMA((4,)),
             pltpu.SemaphoreType.DMA((1,)),
         ]
         + [single] * 2
@@ -585,8 +638,11 @@
         compiler_params=pltpu.CompilerParams(
             collective_id=1, has_side_effects=True, vmem_limit_bytes=MEMORY
         ),
-        name="attention_forward",
-    )(lengths, counts, q, k, v, ek, eq, packed)
+        name="front",
+    )(
+        lengths, counts, tokens, index_rows, down, up, hidden_up, hidden_down, adapt_scale,
+        in_weight, back_weight, qkv_weight, rel_embed, out_weight,
+    )
 
 
 def backward_kernel(
@@ -801,74 +857,101 @@
         hidden_ref[...] = jnp.zeros_like(hidden_ref)
         scale_grad_ref[...] = jnp.zeros_like(scale_grad_ref)
 
-    row = lax.broadcasted_iota(jnp.int32, (BLOCK, 1), 0) + step * BLOCK
-    live = jnp.zeros((BLOCK, 1), f32)
-    for (start, length), used in zip(SLOTS, live_counts(lengths_ref, counts_ref)):
-        live = jnp.where((row >= start) & (row < start + used), 1.0, live)
     gain_one, shift_one, gain_two, shift_two = (
         ref[...].reshape(1, D)
         for ref in (gain_one_ref, shift_one_ref, gain_two_ref, shift_two_ref)
     )
-
-    context = context_ref[...]
+    used_rows = live_counts(lengths_ref, counts_ref)
     weight = weight_ref[0]
-    attended = dot_nn(context, weight)
-    normed, normal_one, inverse_one = norm_forward(
-        tokens_ref[...].astype(f32) + attended, gain_one, shift_one
-    )
-    normed_low = normed.astype(bf16)
-    mlp = jnp.zeros((BLOCK, D), f32)
-    back_coeff = jnp.zeros((PAD, BLOCK), f32)
-    for c in range(chunks):
-        hidden = dot_nn(normed_low, packed_ref[c, :D, :])
-        active, slope = gelu_pair(hidden)
-        active = active.astype(bf16)
-        active_scr[c] = active
-        slope_scr[c] = slope
-        mlp = mlp + dot_nn(active, packed_ref[c, D : 2 * D, :])
-        back_coeff = back_coeff + dot_nt(packed_ref[c, 2 * D + PAD : 2 * D + 2 * PAD, :], active)
-    result, normal_two, inverse_two = norm_forward(normed + mlp, gain_two, shift_two)
-    mixed_ref[...] = (result * live).astype(bf16)
-    grad_two = norm_backward(
-        out_grad_ref[...].astype(f32) * live, normal_two, inverse_two, gain_two
-    )
-    grad_mlp = grad_two.astype(bf16)
-
-    back_slope = dot_nt(factor_ref[9], grad_mlp)
-    small_ref[3] += add_parts(dot_nn(two_parts(back_coeff * scale_ref[:, 5:6]), grad_mlp))
-    scale_grad_ref[:, 5:6] += jnp.sum(back_coeff * back_slope, axis=1, keepdims=True)
-    back_through = two_parts(back_slope * scale_ref[:, 5:6])
-    in_coeff = dot_nt(factor_ref[4], normed_low)
-    in_scaled = two_parts(in_coeff * scale_ref[:, 4:5])
-    in_slope = jnp.zeros((PAD, BLOCK), f32)
-    grad_normed = grad_two
-    for c in range(chunks):
-        grad_active = dot_nt(grad_mlp, packed_ref[c, D : 2 * D, :])
-        grad_hidden = (grad_active * slope_scr[c]).astype(bf16)
-        grad_normed = grad_normed + dot_nt(grad_hidden, packed_ref[c, :D, :])
-        in_slope = in_slope + dot_nt(packed_ref[c, 2 * D : 2 * D + PAD, :], grad_hidden)
-        hidden_ref[c] += add_parts(dot_nn(in_scaled, grad_hidden))
-        hidden_ref[chunks + c] += add_parts(dot_nn(back_through, active_scr[c]))
-    scale_grad_ref[:, 4:5] += jnp.sum(in_coeff * in_slope, axis=1, keepdims=True)
-    small_ref[2] += add_parts(dot_nn(two_parts(in_slope * scale_ref[:, 4:5]), normed_low))
-
-    grad_one = norm_backward(grad_normed, normal_one, inverse_one, gain_one)
-    grad_one_ref[...] = grad_one
-    grad_attended = grad_one.astype(bf16)
-    context_grad_ref[...] = dot_nt(grad_attended, weight).astype(bf16)
-    out_coeff = dot_nt(factor_ref[3], context)
-    out_slope = dot_nt(factor_ref[8], grad_attended)
-    small_ref[1] += add_parts(dot_nn(two_parts(out_coeff * scale_ref[:, 3:4]), grad_attended))
-    small_ref[0] += add_parts(dot_nn(two_parts(out_slope * scale_ref[:, 3:4]), context))
-    scale_grad_ref[:, 3:4] += jnp.sum(out_coeff * out_slope, axis=1, keepdims=True)
+
+    def work(number):
+        rows = slice(number * BLOCK, (number + 1) * BLOCK)
+        row = lax.broadcasted_iota(jnp.int32, (BLOCK, 1), 0) + step * WIDE + number * BLOCK
+        live = jnp.zeros((BLOCK, 1), f32)
+        for (start, length), used in zip(SLOTS, used_rows):
+            live = jnp.where((row >= start) & (row < start + used), 1.0, live)
+        context = context_ref[rows, :]
+        attended = dot_nn(context, weight)
+        normed, normal_one, inverse_one = norm_forward(
+            tokens_ref[rows, :].astype(f32) + attended, gain_one, shift_one
+        )
+        normed_low = normed.astype(bf16)
+        yield
+        mlp = jnp.zeros((BLOCK, D), f32)
+        back_coeff = jnp.zeros((PAD, BLOCK), f32)
+        ahead = dot_nn(normed_low, packed_ref[0, :D, :])
+        for c in range(chunks):
+            hidden = ahead
+            if c + 1 < chunks:
+                ahead = dot_nn(normed_low, packed_ref[c + 1, :D, :])
+            active, slope = gelu_pair(hidden)
+            active = active.astype(bf16)
+            active_scr[c, rows, :] = active
+            slope_scr[c, rows, :] = slope
+            mlp = mlp + dot_nn(active, packed_ref[c, D : 2 * D, :])
+            back_coeff = back_coeff + dot_nt(
+                packed_ref[c, 2 * D + PAD : 2 * D + 2 * PAD, :], active
+            )
+            yield
+        result, normal_two, inverse_two = norm_forward(normed + mlp, gain_two, shift_two)
+        mixed_ref[rows, :] = (result * live).astype(bf16)
+        grad_two = norm_backward(
+            out_grad_ref[rows, :].astype(f32) * live, normal_two, inverse_two, gain_two
+        )
+        grad_mlp = grad_two.astype(bf16)
+        yield
+        back_slope = dot_nt(factor_ref[9], grad_mlp)
+        small_ref[3] += add_parts(dot_nn(two_parts(back_coeff * scale_ref[:, 5:6]), grad_mlp))
+        scale_grad_ref[:, 5:6] += jnp.sum(back_coeff * back_slope, axis=1, keepdims=True)
+        back_through = two_parts(back_slope * scale_ref[:, 5:6])
+        in_coeff = dot_nt(factor_ref[4], normed_low)
+        in_scaled = two_parts(in_coeff * scale_ref[:, 4:5])
+        in_slope = jnp.zeros((PAD, BLOCK), f32)
+        grad_normed = grad_two
+        ahead = dot_nt(grad_mlp, packed_ref[0, D : 2 * D, :])
+        for c in range(chunks):
+            grad_active = ahead
+            if c + 1 < chunks:
+                ahead = dot_nt(grad_mlp, packed_ref[c + 1, D : 2 * D, :])
+            grad_hidden = (grad_active * slope_scr[c, rows, :]).astype(bf16)
+            grad_normed = grad_normed + dot_nt(grad_hidden, packed_ref[c, :D, :])
+            in_slope = in_slope + dot_nt(packed_ref[c, 2 * D : 2 * D + PAD, :], grad_hidden)
+            hidden_ref[c] += add_parts(dot_nn(in_scaled, grad_hidden))
+            hidden_ref[chunks + c] += add_parts(dot_nn(back_through, active_scr[c, rows, :]))
+            yield
+        scale_grad_ref[:, 4:5] += jnp.sum(in_coeff * in_slope, axis=1, keepdims=True)
+        small_ref[2] += add_parts(dot_nn(two_parts(in_slope * scale_ref[:, 4:5]), normed_low))
+        grad_one = norm_backward(grad_normed, normal_one, inverse_one, gain_one)
+        grad_one_ref[rows, :] = grad_one
+        grad_attended = grad_one.astype(bf16)
+        yield
+        context_grad_ref[rows, :] = dot_nt(grad_attended, weight).astype(bf16)
+        out_coeff = dot_nt(factor_ref[3], context)
+        out_slope = dot_nt(factor_ref[8], grad_attended)
+        small_ref[1] += add_parts(dot_nn(two_parts(out_coeff * scale_ref[:, 3:4]), grad_attended))
+        small_ref[0] += add_parts(dot_nn(two_parts(out_slope * scale_ref[:, 3:4]), context))
+        scale_grad_ref[:, 3:4] += jnp.sum(out_coeff * out_slope, axis=1, keepdims=True)
+
+    waiting = [work(number) for number in range(WIDE // BLOCK)]
+    running = []
+    turn_number = 0
+    while waiting or running:
+        if waiting and turn_number % LAG == 0:
+            running.append(waiting.pop(0))
+        turn_number += 1
+        for job in list(running):
+            try:
+                next(job)
+            except StopIteration:
+                running.remove(job)
 
 
 def middle(lengths, counts, tokens, context, out_grad, weights, packed, factors, scales, norms):
     chunks = packed.shape[0]
-    tile = pl.BlockSpec((BLOCK, D), lambda i: (i, 0))
+    tile = pl.BlockSpec((WIDE, D), lambda i: (i, 0))
     return pl.pallas_call(
         middle_kernel,
-        grid=(ROWS // BLOCK,),
+        grid=(ROWS // WIDE,),
         in_specs=[pl.BlockSpec(memory_space=pltpu.SMEM)] * 2
         + [tile] * 3
         + [
@@ -891,8 +974,8 @@
             jax.ShapeDtypeStruct((PAD, 128), f32),
         ],
         scratch_shapes=[
-            pltpu.VMEM((chunks, BLOCK, D), bf16),
-            pltpu.VMEM((chunks, BLOCK, D), f32),
+            pltpu.VMEM((chunks, WIDE, D), bf16),
+            pltpu.VMEM((chunks, WIDE, D), f32),
         ],
         compiler_params=pltpu.CompilerParams(vmem_limit_bytes=MEMORY),
         name="middle",
@@ -909,13 +992,8 @@
 
 
 def last_kernel(
-    tokens_ref,
-    gq_ref,
-    gk_ref,
-    gv_ref,
     grad_one_ref,
     coeff_ref,
-    merged_ref,
     index_ref,
     rel_coeff_ref,
     factor_ref,
@@ -923,18 +1001,26 @@
     small_ref,
     hidden_ref,
     middle_scale_ref,
+    tokens_any,
+    gq_any,
+    gk_any,
+    gv_any,
     rel_any,
     geq_any,
     gfk_any,
+    merged_any,
     in_grad_ref,
     down_out,
     up_out,
     hidden_up_out,
     hidden_down_out,
     scale_out,
+    tokens_scr,
+    grads_scr,
     rel_scr,
     geq_scr,
     gfk_scr,
+    merged_scr,
     down_scr,
     up_scr,
     scale_scr,
@@ -960,7 +1046,8 @@
     spread_in_sem,
 ):
     step = pl.program_id(0)
-    final = ROWS // BLOCK - 1
+    final = TILES
+    used = 2 * 3 * BLOCKS * RANK
     outer = lax.axis_size("dp")
     inner = lax.axis_size("tensor")
     count = outer * inner
@@ -1032,15 +1119,26 @@
             (lax.rem(my_outer + off, outer), my_inner),
         )
 
-    def load(number, src, dst):
-        return pltpu.make_async_copy(src, dst, load_sem.at[number])
-
-    loads = ((0, rel_any, rel_scr), (1, geq_any, geq_scr), (2, gfk_any, gfk_scr))
+    loads = [
+        pltpu.make_async_copy(src, dst, load_sem.at[number])
+        for number, (src, dst) in enumerate(
+            (
+                (tokens_any, tokens_scr),
+                (gq_any, grads_scr.at[0]),
+                (gk_any, grads_scr.at[1]),
+                (gv_any, grads_scr.at[2]),
+                (rel_any, rel_scr),
+                (geq_any, geq_scr),
+                (gfk_any, gfk_scr),
+                (merged_any.at[pl.ds(0, 3)], merged_scr),
+            )
+        )
+    ]
 
     @pl.when(step == 0)
     def _():
-        for piece in loads:
-            load(*piece).start()
+        for load in loads:
+            load.start()
 
         @pl.loop(1, count)
         def _(off):
@@ -1048,11 +1146,6 @@
             pl.semaphore_signal(barrier, inc=1, device_id=(row, col), device_id_type=MESH)
 
         scale_scr[...] = jnp.zeros_like(scale_scr)
-        down_scr[...] = jnp.zeros_like(down_scr)
-        up_scr[...] = jnp.zeros_like(up_scr)
-
-    @pl.when(step == 1)
-    def _():
         if count > 4 * BLOCKS:
             mine_small[4 * BLOCKS :] = jnp.zeros((count - 4 * BLOCKS, PAD, LANES), bf16)
         for number in range(4):
@@ -1079,11 +1172,19 @@
 
         land_small[0] = mine_small[me]
         land_hidden[0] = mine_hidden[my_inner, my_outer]
-
-    @pl.when(step == 2)
-    def _():
-        for piece in loads:
-            load(*piece).wait()
+        loads[0].wait()
+        tokens = tokens_scr[...]
+        for member in range(3):
+            loads[1 + member].wait()
+            grad = grads_scr[member]
+            scale = scale_ref[:, member : member + 1]
+            coeff = coeff_ref[member]
+            slope = dot_nt(factor_ref[5 + member], grad)
+            up_scr[member] = add_parts(dot_nn(two_parts(coeff * scale), grad))
+            down_scr[member] = add_parts(dot_nn(two_parts(slope * scale), tokens))
+            scale_scr[:, member : member + 1] += jnp.sum(coeff * slope, axis=1, keepdims=True)
+        for load in loads[4:7]:
+            load.wait()
         rel = rel_scr[...]
         bucket = lax.broadcasted_iota(jnp.int32, (2 * SPAN, OFFSETS), 0)
         for member, ref, row in ((0, geq_scr, 0), (1, gfk_scr, 1)):
@@ -1095,23 +1196,6 @@
             up_scr[member] += add_parts(dot_nt(two_parts(coeff * scale), grad))
             down_scr[member] += add_parts(dot_nn(two_parts(slope * scale), rel))
             scale_scr[:, member : member + 1] += jnp.sum(coeff * slope, axis=1, keepdims=True)
-
-    tokens = tokens_ref[...]
-    in_grad = grad_one_ref[...]
-    for member, ref in enumerate((gq_ref, gk_ref, gv_ref)):
-        grad = ref[...]
-        scale = scale_ref[:, member : member + 1]
-        in_grad = in_grad + dot_nt(grad, merged_ref[member])
-        coeff = coeff_ref[member]
-        slope = dot_nt(factor_ref[5 + member], grad)
-        up_scr[member] += add_parts(dot_nn(two_parts(coeff * scale), grad))
-        down_scr[member] += add_parts(dot_nn(two_parts(slope * scale), tokens))
-        scale_scr[:, member : member + 1] += jnp.sum(coeff * slope, axis=1, keepdims=True)
-    in_grad_ref[...] = in_grad
-
-    @pl.when(step == final)
-    def _():
-        used = 2 * 3 * BLOCKS * RANK
         for number in range(6):
             ref = down_scr if number < 3 else up_scr
             for block in range(BLOCKS):
@@ -1128,7 +1212,18 @@
             late(off).start()
 
         land_late[0] = mine_late[me]
-
+        loads[7].wait()
+
+    @pl.when(step > 0)
+    def _():
+        rows = pl.ds(pl.multiple_of((step - 1) * BLOCK, BLOCK), BLOCK)
+        in_grad = grad_one_ref[...]
+        for member in range(3):
+            in_grad = in_grad + dot_nt(grads_scr[member, rows, :], merged_scr[member])
+        in_grad_ref[...] = in_grad
+
+    @pl.when(step == SUMMED)
+    def _():
         @pl.loop(1, count)
         def _(off):
             small(off).wait_recv()
@@ -1152,6 +1247,8 @@
         def _(off):
             sums(off, me).start()
 
+    @pl.when(step == final)
+    def _():
         @pl.loop(1, outer)
         def _(off):
             spread(off, lax.rem(my_outer + outer - off, outer)).wait_recv()
@@ -1207,26 +1304,25 @@
     outer = lax.axis_size("dp")
     inner = lax.axis_size("tensor")
     piece = hidden_rows()
-    tile = pl.BlockSpec((BLOCK, D), lambda i: (i, 0))
+    tile = pl.BlockSpec((BLOCK, D), lambda i: (jnp.maximum(i - 1, 0), 0))
     factor = jax.ShapeDtypeStruct((5, RANK, D), f32)
     block = pltpu.VMEM((count, PAD, LANES), bf16)
     all_pairs = pltpu.SemaphoreType.DMA((count,))
     return pl.pallas_call(
         last_kernel,
-        grid=(ROWS // BLOCK,),
-        in_specs=[tile] * 5
-        + [
-            pl.BlockSpec((3, PAD, BLOCK), lambda i: (0, 0, i)),
-            whole(3, D, D),
-            whole(2, OFFSETS),
-            whole(2, PAD, 2 * SPAN),
-            whole(12, PAD, D),
-            whole(PAD, LANES),
-            whole(4, PAD, D),
-            whole(2 * inner, PAD, D),
-            whole(PAD, LANES),
+        grid=(1 + TILES,),
+        in_specs=[
+            tile,
+            once(3, PAD, ROWS),
+            once(2, OFFSETS),
+            once(2, PAD, 2 * SPAN),
+            once(12, PAD, D),
+            once(PAD, LANES),
+            once(4, PAD, D),
+            once(2 * inner, PAD, D),
+            once(PAD, LANES),
         ]
-        + [pl.BlockSpec(memory_space=pl.ANY)] * 3,
+        + [pl.BlockSpec(memory_space=pl.ANY)] * 8,
         out_specs=[
             tile,
             whole(5, RANK, D),
@@ -1244,9 +1340,12 @@
             jax.ShapeDtypeStruct((6, RANK), f32),
         ],
         scratch_shapes=[
+            pltpu.VMEM((ROWS, D), bf16),
+            pltpu.VMEM((3, ROWS, D), bf16),
             pltpu.VMEM((2 * SPAN, D), bf16),
             pltpu.VMEM((D, OFFSETS), bf16),
             pltpu.VMEM((D, OFFSETS), bf16),
+            pltpu.VMEM((3, D, D), bf16),
             pltpu.VMEM((3, PAD, D), f32),
             pltpu.VMEM((3, PAD, D), f32),
             pltpu.VMEM((PAD, LANES), f32),
@@ -1259,7 +1358,7 @@
             pltpu.VMEM((count, piece, LANES), bf16),
             pltpu.VMEM((count, 2 * PAD, LANES), bf16),
             pltpu.VMEM((outer, piece, LANES), bf16),
-            pltpu.SemaphoreType.DMA((3,)),
+            pltpu.SemaphoreType.DMA((8,)),
         ]
         + [all_pairs] * 8
         + [pltpu.SemaphoreType.DMA((outer,))] * 2,
@@ -1268,8 +1367,8 @@
         ),
         name="last",
     )(
-        tokens, gq, gk, gv, grad_one, coeff, weights, index, rel_coeff, factors, scales,
-        small, hidden, middle_scale, rel, geq, gfk,
+        grad_one, coeff, index, rel_coeff, factors, scales, small, hidden, middle_scale,
+        tokens, gq, gk, gv, rel, geq, gfk, weights,
     )
 
 
@@ -1298,12 +1397,9 @@
         jnp.stack([rel_bucket[::-1], rel_bucket]), ((0, 0), (0, 1)), constant_values=-1
     )
     norms = (gain_one, shift_one, gain_two, shift_two)
-    q, k, v, eq, fk, ekt, eqt, weights, packed, coeff, rel_coeff, factors, scales = project(
-        tokens, qkv_weight, rel_embed, index_rows, adapt_down, adapt_up, hidden_up, hidden_down,
-        adapt_scale, out_weight, in_weight, back_weight,
-    )
-    context, p1, p2, p3, gathered = attend_forward(
-        seq_lengths, seq_counts, q, k, v, ekt, eqt, packed
+    eq, fk, coeff, rel_coeff, factors, scales, context, p1, p2, p3, q, k, v, weights, gathered = front(
+        seq_lengths, seq_counts, tokens, qkv_weight, rel_embed, index_rows, adapt_down, adapt_up,
+        hidden_up, hidden_down, adapt_scale, out_weight, in_weight, back_weight,
     )
     mixed, grad_one, context_grad, small, hidden, middle_scale = middle(
         seq_lengths, seq_counts, tokens, context, out_grad, weights, gathered, factors, scales, norms

time: 190 us -> 175 us (0.921)
  Pallas kernels: 180 us -> 164 us
    pallas_call x4 -> x3, Pallas kernels: 142 us -> 126 us  [the longest x1 50.1 us: front(): pl.pallas_call(front_kernel, grid=(TILES + H // 2,), in_specs=[pl.BlockSp...]
where the time goes in v5:
time: 175 us; the launch traced here: 174 us
  Pallas kernels  164 us (94%)
  local copies, waits for them, and re-layouts  8.5 us (5%)
    pallas_call x1, Pallas kernels, front(): pl.pallas_call(front_kernel, grid=(TILES + H // 2,), in_specs=[pl.BlockSp...  50.1 us
    pallas_call x1, Pallas kernels, middle(): pl.pallas_call(middle_kernel, grid=(ROWS // WIDE,), in_specs=[pl.BlockSpe...  45.3 us
    pallas_call x1, Pallas kernels, attend_backward(): pl.pallas_call(backward_kernel, grid=(H // 2,), in_specs=[PAIR_SPEC] * 7...  38.2 us
    pallas_call x1, Pallas kernels, last(): pl.pallas_call(last_kernel, grid=(1 + TILES,), in_specs=[tile, once(3, PA...  30.7 us
    unnamed x18, local copies, waits for them, and re-layouts  7.9 us

profile of v5, /device:TPU:0, one launch (start us, length us, event | category | flops | bytes accessed | tf_op | source)
XLA Modules:
  0.0 174.3 jit_solution(2337682145157093592)
XLA Ops:
  0.6 0.8 reverse
  1.4 0.1 slice
  1.5 0.7 pad_add_fusion
  2.2 0.6 pad.4.index_ref
  2.8 50.1 %front.1 = (bf16[1024,768]{1,0:T(8,128)(2,1)}, bf16[1024,768]{1,0:T(8,128)(2,1)}, f32[3,16,1024]{2,1,0:T(8,128)}, f32[2,16,512]{2,1,0:T(8,128)}, bf16[12,16,768]...) custom-call(s32[1,4]{1,0:T(1,128)} %lengths_ref.3, ...), custom_call_target="tpu_custom_call" | custom-call | tf_op jit(solution)/shard_map/front/pallas_call | solution.py:580
  52.9 45.3 %middle.1 = (bf16[1024,768]{1,0:T(8,128)(2,1)}, f32[1024,768]{1,0:T(8,128)}, bf16[1024,768]{1,0:T(8,128)(2,1)}, f32[4,16,768]{2,1,0:T(8,128)}, f32[8,16,768]{2,1,0:T(8,128)}, /*index=5*/f32[16,128]{1,0:T(8,128)}) custom-call(s32[1,4]{1,0:T(1,128)} %lengths_ref.3, s32[1,3]{1,0:T(1,128)} %counts_ref.3, bf16[1024,768]{1,0:T(8,128)(2,1)} %tokens_any.1, ...), custom_call_target="tpu_custom_call" | custom-call | tf_op jit(solution)/shard_map/middle/pallas_call | solution.py:952
  98.2 38.2 %attention_backward.1 = (bf16[1024,768]{1,0:T(8,128)(2,1)}, bf16[1024,768]{1,0:T(8,128)(2,1)}, bf16[1024,768]{1,0:T(8,128)(2,1)}, bf16[768,1024]{1,0:T(8,128)(2,1)}, bf16[768,1024]{1,0:T(8,128)(2,1)}) custom-call(bf16[1024,768]{1,0:T(8,128)(2,1)} %get-tuple-element.51.q_ref, bf16[1024,768]{1,0:T(8,128)(2,1)} %get-tuple-element.52.k_ref, ...), custom_call_target="tpu_custom_call" | custom-call | tf_op jit(solution)/shard_map/attention_backward/pallas_call | solution.py:781
  136.4 30.7 %last.1 = (f32[1024,768]{1,0:T(8,128)}, f32[5,12,768]{2,1,0:T(8,128)}, f32[5,12,768]{2,1,0:T(8,128)}, f32[12,768]{1,0:T(8,128)}, f32[12,768]{1,0:T(8,128)}, /*index=5*/f32[6,12]{1,0:T(8,128)}) custom-call(f32[1024,768]{1,0:T(8,128)} %get-tuple-element.45.grad_one_ref, f32[3,16,1024]{2,1,0:T(8,128)} %get-tuple-element.46.coeff_ref, s32[2,1024]{1,0:T(2,128)} %pad.4.index_ref, ...), custom_call_target="tpu_custom_call" | custom-call | tf_op jit(solution)/shard_map/last/pallas_call | solution.py:1311
  167.2 0.0 copy-start.1
  167.2 0.0 copy-start
  167.2 0.0 copy-start.3
  167.2 0.0 copy-start.2
  167.2 0.0 copy-start.4
  167.2 3.8 %copy.32 = f32[1024,768]{1,0:T(8,128)} copy(f32[1024,768]{1,0:T(8,128)} %get-tuple-element.79) | data formatting | bytes 6291456
  171.1 0.0 copy-done.1
  171.1 0.7 copy.33
  171.8 0.0 copy-done
  171.8 0.7 copy.34
  172.5 0.0 copy-done.3
  172.5 0.6 copy.35
  173.1 0.0 copy-done.2
  173.1 0.6 copy.36
  173.7 0.0 copy-done.4
  173.7 0.6 copy.37
Async XLA Ops:
  167.2 3.9 %copy-start.1 = (f32[5,12,768]{2,1,0:T(8,128)S(1)}, f32[5,12,768]{2,1,0:T(8,128)}, u32[]{:S(2)}) copy-start(f32[5,12,768]{2,1,0:T(8,128)} %get-tuple-element.80) | copy-start | bytes 552964
  167.2 4.6 %copy-start = (f32[5,12,768]{2,1,0:T(8,128)S(1)}, f32[5,12,768]{2,1,0:T(8,128)}, u32[]{:S(2)}) copy-start(f32[5,12,768]{2,1,0:T(8,128)} %get-tuple-element.81) | copy-start | bytes 552964
  167.2 5.3 %copy-start.3 = (f32[12,768]{1,0:T(8,128)S(1)}, f32[12,768]{1,0:T(8,128)}, u32[]{:S(2)}) copy-start(f32[12,768]{1,0:T(8,128)} %get-tuple-element.82) | copy-start | bytes 110596
  167.2 5.9 %copy-start.2 = (f32[12,768]{1,0:T(8,128)S(1)}, f32[12,768]{1,0:T(8,128)}, u32[]{:S(2)}) copy-start(f32[12,768]{1,0:T(8,128)} %get-tuple-element.83) | copy-start | bytes 110596
  167.2 6.5 %copy-start.4 = (f32[6,12]{1,0:T(8,128)S(1)}, f32[6,12]{1,0:T(8,128)}, u32[]{:S(2)}) copy-start(f32[6,12]{1,0:T(8,128)} %get-tuple-element.84) | copy-start | bytes 868

commit v6 on v5

--- a/solution.py
+++ b/solution.py
@@ -1027,21 +1027,21 @@
     stage_scr,
     mine_late,
     land_late,
-    mine_small,
-    land_small,
-    mine_hidden,
-    land_hidden,
+    mine_early,
+    land_early,
+    part_early,
+    land_part,
     all_sums,
     all_hidden,
     load_sem,
     late_out_sem,
     late_in_sem,
-    small_out_sem,
-    small_in_sem,
-    hidden_out_sem,
-    hidden_in_sem,
     sums_out_sem,
     sums_in_sem,
+    early_out_sem,
+    early_in_sem,
+    part_out_sem,
+    part_in_sem,
     spread_out_sem,
     spread_in_sem,
 ):
@@ -1073,41 +1073,53 @@
     def late(off):
         other, row, col = partner(off)
         return send(
-            mine_late.at[other],
-            land_late.at[off],
-            late_out_sem.at[off],
-            late_in_sem.at[off],
-            (row, col),
-        )
-
-    def small(off):
+            mine_late.at[other], land_late.at[off], late_out_sem.at[0], late_in_sem.at[0], (row, col)
+        )
+
+    def sums(off):
         other, row, col = partner(off)
         return send(
-            mine_small.at[other],
-            land_small.at[off],
-            small_out_sem.at[off],
-            small_in_sem.at[off],
-            (row, col),
-        )
-
-    def hidden(off):
-        other, row, col = partner(off)
+            all_sums.at[0], all_sums.at[off], sums_out_sem.at[0], sums_in_sem.at[0], (row, col)
+        )
+
+    def every_late():
+        others = pl.ds(1, count - 1)
         return send(
-            mine_hidden.at[col, row],
-            land_hidden.at[off],
-            hidden_out_sem.at[off],
-            hidden_in_sem.at[off],
-            (row, col),
-        )
-
-    def sums(off, origin):
-        other, row, col = partner(off)
+            mine_late.at[others],
+            land_late.at[others],
+            late_out_sem.at[0],
+            late_in_sem.at[0],
+            (my_outer, my_inner),
+        )
+
+    def every_sums():
+        others = pl.ds(1, count - 1)
         return send(
-            all_sums.at[origin],
-            all_sums.at[origin],
-            sums_out_sem.at[off],
-            sums_in_sem.at[off],
-            (row, col),
+            all_sums.at[others],
+            all_sums.at[others],
+            sums_out_sem.at[0],
+            sums_in_sem.at[0],
+            (my_outer, my_inner),
+        )
+
+    def early(off):
+        col = lax.rem(my_inner + off, inner)
+        return send(
+            mine_early.at[col],
+            land_early.at[off],
+            early_out_sem.at[off],
+            early_in_sem.at[off],
+            (my_outer, col),
+        )
+
+    def part(off):
+        row = lax.rem(my_outer + off, outer)
+        return send(
+            part_early.at[row],
+            land_part.at[off],
+            part_out_sem.at[off],
+            part_in_sem.at[off],
+            (row, my_inner),
         )
 
     def spread(off, origin):
@@ -1146,32 +1158,29 @@
             pl.semaphore_signal(barrier, inc=1, device_id=(row, col), device_id_type=MESH)
 
         scale_scr[...] = jnp.zeros_like(scale_scr)
-        if count > 4 * BLOCKS:
-            mine_small[4 * BLOCKS :] = jnp.zeros((count - 4 * BLOCKS, PAD, LANES), bf16)
+        mine_early[...] = jnp.zeros_like(mine_early)
         for number in range(4):
             for block in range(BLOCKS):
-                mine_small[number * BLOCKS + block] = small_ref[
+                piece = number * BLOCKS + block
+                mine_early[piece % inner, piece // inner, :PAD] = small_ref[
                     number, :, block * LANES : (block + 1) * LANES
                 ].astype(bf16)
-        mine_hidden[...] = jnp.zeros_like(mine_hidden)
-        tiles = mine_hidden.shape[2] // PAD
+        tiles = mine_early.shape[2] // PAD - 1
         for chunk in range(inner):
             for which in range(2):
                 for block in range(BLOCKS):
                     tile = which * BLOCKS + block
-                    at = tile % tiles * PAD
-                    mine_hidden[chunk, tile // tiles, at : at + PAD] = hidden_ref[
+                    at = (tile % tiles + 1) * PAD
+                    mine_early[chunk, tile // tiles, at : at + PAD] = hidden_ref[
                         which * inner + chunk, :, block * LANES : (block + 1) * LANES
                     ].astype(bf16)
         pl.semaphore_wait(barrier, count - 1)
 
-        @pl.loop(1, count)
+        @pl.loop(1, inner)
         def _(off):
-            small(off).start()
-            hidden(off).start()
-
-        land_small[0] = mine_small[me]
-        land_hidden[0] = mine_hidden[my_inner, my_outer]
+            early(off).start()
+
+        land_early[0] = mine_early[my_inner]
         loads[0].wait()
         tokens = tokens_scr[...]
         for member in range(3):
@@ -1183,6 +1192,18 @@
             up_scr[member] = add_parts(dot_nn(two_parts(coeff * scale), grad))
             down_scr[member] = add_parts(dot_nn(two_parts(slope * scale), tokens))
             scale_scr[:, member : member + 1] += jnp.sum(coeff * slope, axis=1, keepdims=True)
+
+        @pl.loop(1, inner)
+        def _(off):
+            early(off).wait_recv()
+
+        part_early[...] = jnp.sum(land_early[...].astype(f32), axis=0).astype(bf16)
+
+        @pl.loop(1, outer)
+        def _(off):
+            part(off).start()
+
+        land_part[0] = part_early[my_outer]
         for load in loads[4:7]:
             load.wait()
         rel = rel_scr[...]
@@ -1224,28 +1245,24 @@
 
     @pl.when(step == SUMMED)
     def _():
-        @pl.loop(1, count)
+        @pl.loop(1, outer)
         def _(off):
-            small(off).wait_recv()
-            hidden(off).wait_recv()
-
-        all_hidden[my_outer] = jnp.sum(land_hidden[...].astype(f32), axis=0).astype(bf16)
+            part(off).wait_recv()
+
+        summed = jnp.sum(land_part[...].astype(f32), axis=0).astype(bf16)
+        all_hidden[my_outer] = summed[PAD:]
+        all_sums[0, PAD:] = summed[:PAD]
 
         @pl.loop(1, outer)
         def _(off):
             spread(off, my_outer).start()
 
-        all_sums[me, PAD:] = jnp.sum(land_small[...].astype(f32), axis=0).astype(bf16)
+        every_late().wait_recv()
+        all_sums[0, :PAD] = jnp.sum(land_late[...].astype(f32), axis=0).astype(bf16)
 
         @pl.loop(1, count)
         def _(off):
-            late(off).wait_recv()
-
-        all_sums[me, :PAD] = jnp.sum(land_late[...].astype(f32), axis=0).astype(bf16)
-
-        @pl.loop(1, count)
-        def _(off):
-            sums(off, me).start()
+            sums(off).start()
 
     @pl.when(step == final)
     def _():
@@ -1263,11 +1280,13 @@
                     tile // tiles, at : at + PAD
                 ].astype(f32)[:RANK]
 
-        @pl.loop(1, count)
-        def _(off):
-            sums(off, lax.rem(me + count - off, count)).wait_recv()
-
-        stage_scr[...] = all_sums[:, :PAD].astype(f32).reshape(count * PAD, LANES)
+        every_sums().wait_recv()
+
+        def summed_by(owner):
+            return all_sums.at[lax.rem(me + count - owner, count)]
+
+        for owner in range(count):
+            stage_scr[owner * PAD : (owner + 1) * PAD, :] = summed_by(owner)[:PAD].astype(f32)
         for number in range(6):
             ref = down_out if number < 3 else up_out
             for block in range(BLOCKS):
@@ -1280,19 +1299,19 @@
             ((down_out, 3), (up_out, 3), (down_out, 4), (up_out, 4))
         ):
             for block in range(BLOCKS):
-                ref[place, :, block * LANES : (block + 1) * LANES] = all_sums[
-                    number * BLOCKS + block, PAD:
-                ].astype(f32)[:RANK]
-
-        @pl.loop(1, count)
+                ref[place, :, block * LANES : (block + 1) * LANES] = summed_by(
+                    number * BLOCKS + block
+                )[PAD:].astype(f32)[:RANK]
+        every_late().wait_send()
+        every_sums().wait_send()
+
+        @pl.loop(1, inner)
         def _(off):
-            small(off).wait_send()
-            hidden(off).wait_send()
-            late(off).wait_send()
-            sums(off, me).wait_send()
+            early(off).wait_send()
 
         @pl.loop(1, outer)
         def _(off):
+            part(off).wait_send()
             spread(off, my_outer).wait_send()
 
 
@@ -1307,7 +1326,6 @@
     tile = pl.BlockSpec((BLOCK, D), lambda i: (jnp.maximum(i - 1, 0), 0))
     factor = jax.ShapeDtypeStruct((5, RANK, D), f32)
     block = pltpu.VMEM((count, PAD, LANES), bf16)
-    all_pairs = pltpu.SemaphoreType.DMA((count,))
     return pl.pallas_call(
         last_kernel,
         grid=(1 + TILES,),
@@ -1352,16 +1370,17 @@
             pltpu.VMEM((count * PAD, LANES), f32),
             block,
             block,
-            block,
-            block,
-            pltpu.VMEM((inner, outer, piece, LANES), bf16),
-            pltpu.VMEM((count, piece, LANES), bf16),
+            pltpu.VMEM((inner, outer, PAD + piece, LANES), bf16),
+            pltpu.VMEM((inner, outer, PAD + piece, LANES), bf16),
+            pltpu.VMEM((outer, PAD + piece, LANES), bf16),
+            pltpu.VMEM((outer, PAD + piece, LANES), bf16),
             pltpu.VMEM((count, 2 * PAD, LANES), bf16),
             pltpu.VMEM((outer, piece, LANES), bf16),
             pltpu.SemaphoreType.DMA((8,)),
         ]
-        + [all_pairs] * 8
-        + [pltpu.SemaphoreType.DMA((outer,))] * 2,
+        + [pltpu.SemaphoreType.DMA((1,))] * 4
+        + [pltpu.SemaphoreType.DMA((inner,))] * 2
+        + [pltpu.SemaphoreType.DMA((outer,))] * 4,
         compiler_params=pltpu.CompilerParams(
             collective_id=0, has_side_effects=True, vmem_limit_bytes=MEMORY
         ),

time: 175 us -> 171 us (0.977)
  Pallas kernels: 164 us -> 160 us
    pallas_call x1, Pallas kernels: 30.7 us -> 26.5 us  [last(): pl.pallas_call(last_kernel, grid=(1 + TILES,), in_specs=[tile, once(3, PA...]
where the time goes in v6:
time: 171 us; the launch traced here: 170 us
  Pallas kernels  160 us (94%)
  local copies, waits for them, and re-layouts  8.5 us (5%)
    pallas_call x1, Pallas kernels, front(): pl.pallas_call(front_kernel, grid=(TILES + H // 2,), in_specs=[pl.BlockSp...  50.1 us
    pallas_call x1, Pallas kernels, middle(): pl.pallas_call(middle_kernel, grid=(ROWS // WIDE,), in_specs=[pl.BlockSpe...  45.3 us
    pallas_call x1, Pallas kernels, attend_backward(): pl.pallas_call(backward_kernel, grid=(H // 2,), in_specs=[PAIR_SPEC] * 7...  38.2 us
    pallas_call x1, Pallas kernels, last(): pl.pallas_call(last_kernel, grid=(1 + TILES,), in_specs=[tile, once(3, PA...  26.5 us
    unnamed x18, local copies, waits for them, and re-layouts  7.9 us

profile of v6, /device:TPU:0, one launch (start us, length us, event | category | flops | bytes accessed | tf_op | source)
XLA Modules:
  0.0 170.1 jit_solution(4954647878184842366)
XLA Ops:
  0.6 0.8 reverse
  1.4 0.1 slice
  1.5 0.7 pad_add_fusion
  2.2 0.6 pad.4.index_ref
  2.8 50.1 %front.1 = (bf16[1024,768]{1,0:T(8,128)(2,1)}, bf16[1024,768]{1,0:T(8,128)(2,1)}, f32[3,16,1024]{2,1,0:T(8,128)}, f32[2,16,512]{2,1,0:T(8,128)}, bf16[12,16,768]...) custom-call(s32[1,4]{1,0:T(1,128)} %lengths_ref.3, ...), custom_call_target="tpu_custom_call" | custom-call | tf_op jit(solution)/shard_map/front/pallas_call | solution.py:580
  52.9 45.3 %middle.1 = (bf16[1024,768]{1,0:T(8,128)(2,1)}, f32[1024,768]{1,0:T(8,128)}, bf16[1024,768]{1,0:T(8,128)(2,1)}, f32[4,16,768]{2,1,0:T(8,128)}, f32[8,16,768]{2,1,0:T(8,128)}, /*index=5*/f32[16,128]{1,0:T(8,128)}) custom-call(s32[1,4]{1,0:T(1,128)} %lengths_ref.3, s32[1,3]{1,0:T(1,128)} %counts_ref.3, bf16[1024,768]{1,0:T(8,128)(2,1)} %tokens_any.1, ...), custom_call_target="tpu_custom_call" | custom-call | tf_op jit(solution)/shard_map/middle/pallas_call | solution.py:952
  98.2 38.2 %attention_backward.1 = (bf16[1024,768]{1,0:T(8,128)(2,1)}, bf16[1024,768]{1,0:T(8,128)(2,1)}, bf16[1024,768]{1,0:T(8,128)(2,1)}, bf16[768,1024]{1,0:T(8,128)(2,1)}, bf16[768,1024]{1,0:T(8,128)(2,1)}) custom-call(bf16[1024,768]{1,0:T(8,128)(2,1)} %get-tuple-element.51.q_ref, bf16[1024,768]{1,0:T(8,128)(2,1)} %get-tuple-element.52.k_ref, ...), custom_call_target="tpu_custom_call" | custom-call | tf_op jit(solution)/shard_map/attention_backward/pallas_call | solution.py:781
  136.4 26.5 %last.1 = (f32[1024,768]{1,0:T(8,128)}, f32[5,12,768]{2,1,0:T(8,128)}, f32[5,12,768]{2,1,0:T(8,128)}, f32[12,768]{1,0:T(8,128)}, f32[12,768]{1,0:T(8,128)}, /*index=5*/f32[6,12]{1,0:T(8,128)}) custom-call(f32[1024,768]{1,0:T(8,128)} %get-tuple-element.45.grad_one_ref, f32[3,16,1024]{2,1,0:T(8,128)} %get-tuple-element.46.coeff_ref, s32[2,1024]{1,0:T(2,128)} %pad.4.index_ref, ...), custom_call_target="tpu_custom_call" | custom-call | tf_op jit(solution)/shard_map/last/pallas_call | solution.py:1329
  163.0 0.0 copy-start.1
  163.0 0.0 copy-start
  163.0 0.0 copy-start.3
  163.0 0.0 copy-start.2
  163.0 0.0 copy-start.4
  163.0 3.8 %copy.32 = f32[1024,768]{1,0:T(8,128)} copy(f32[1024,768]{1,0:T(8,128)} %get-tuple-element.79) | data formatting | bytes 6291456
  166.8 0.0 copy-done.1
  166.9 0.7 copy.33
  167.5 0.0 copy-done
  167.5 0.7 copy.34
  168.2 0.0 copy-done.3
  168.2 0.6 copy.35
  168.9 0.0 copy-done.2
  168.9 0.6 copy.36
  169.5 0.0 copy-done.4
  169.5 0.6 copy.37
Async XLA Ops:
  163.0 3.9 %copy-start.1 = (f32[5,12,768]{2,1,0:T(8,128)S(1)}, f32[5,12,768]{2,1,0:T(8,128)}, u32[]{:S(2)}) copy-start(f32[5,12,768]{2,1,0:T(8,128)} %get-tuple-element.80) | copy-start | bytes 552964
  163.0 4.6 %copy-start = (f32[5,12,768]{2,1,0:T(8,128)S(1)}, f32[5,12,768]{2,1,0:T(8,128)}, u32[]{:S(2)}) copy-start(f32[5,12,768]{2,1,0:T(8,128)} %get-tuple-element.81) | copy-start | bytes 552964
  163.0 5.3 %copy-start.3 = (f32[12,768]{1,0:T(8,128)S(1)}, f32[12,768]{1,0:T(8,128)}, u32[]{:S(2)}) copy-start(f32[12,768]{1,0:T(8,128)} %get-tuple-element.82) | copy-start | bytes 110596
  163.0 5.9 %copy-start.2 = (f32[12,768]{1,0:T(8,128)S(1)}, f32[12,768]{1,0:T(8,128)}, u32[]{:S(2)}) copy-start(f32[12,768]{1,0:T(8,128)} %get-tuple-element.83) | copy-start | bytes 110596
  163.0 6.5 %copy-start.4 = (f32[6,12]{1,0:T(8,128)S(1)}, f32[6,12]{1,0:T(8,128)}, u32[]{:S(2)}) copy-start(f32[6,12]{1,0:T(8,128)} %get-tuple-element.84) | copy-start | bytes 868

commit v7 on v6

--- a/solution.py
+++ b/solution.py
@@ -20,8 +20,9 @@
 BLOCK = 256
 SLOTS = ((0, 128), (128, 128), (256, 256), (512, 512))
 PACKED = 1600
-HALF = PACKED // 2
-CHUNK = HALF // 5
+QUARTER = PACKED // 4
+CHUNKS = 5
+CHUNK = QUARTER // CHUNKS
 TILES = ROWS // BLOCK
 SUMMED = 2
 WIDE = 1 * BLOCK
@@ -181,14 +182,19 @@
     near = t + 1 - 2 * lax.rem(t, 2)
     far = t + 2 - 4 * (t // 2)
     mate = d + 1 - 2 * lax.rem(d, 2)
-    half = lax.rem(d, 2)
-    chunks = HALF // CHUNK
-    near_out, near_in, far_out, far_in, mate_out, mate_in, pass_out, pass_in, late_out, late_in = sems
+    other = d + 2 - 4 * lax.rem(d // 2, 2)
+    mine = lax.rem(d, 4)
+    mates = mine + 1 - 2 * lax.rem(mine, 2)
+    others = mine + 2 - 4 * (mine // 2)
+    across = 3 - mine
+    near_out, near_in, own_sems = sems[0], sems[1], sems[2:]
+    pairs = [own_sems[2 * i : 2 * i + 2] for i in range(8)]
+    far_sems, mate_sems, other_sems, relay_sems, *pass_sems = pairs
     barrier = pltpu.get_barrier_semaphore()
-    places = ((d, near), (d, far), (mate, t))
+    places = ((d, near), (d, far), (mate, t), (other, t))
 
     def rows(which, chunk):
-        return pl.ds(pl.multiple_of(which * HALF + chunk * CHUNK, PAD), CHUNK)
+        return pl.ds(pl.multiple_of(which * QUARTER + chunk * CHUNK, PAD), CHUNK)
 
     def send(src, dst, out_sem, in_sem, place):
         return pltpu.make_async_remote_copy(
@@ -199,23 +205,33 @@
         return send(packed, gathered.at[t], near_out.at[0], near_in.at[0], places[0])
 
     def to_far(chunk):
-        here = rows(half, chunk)
+        here = rows(mine, chunk)
         return send(
-            packed.at[here], gathered.at[t, here], far_out.at[chunk], far_in.at[chunk], places[1]
-        )
-
-    def onward(which, chunk, out_sems, in_sems, place):
+            packed.at[here],
+            gathered.at[t, here],
+            far_sems[0].at[chunk],
+            far_sems[1].at[chunk],
+            places[1],
+        )
+
+    def onward(which, chunk, pair, place):
         here = gathered.at[far, rows(which, chunk)]
-        return send(here, here, out_sems.at[chunk], in_sems.at[chunk], place)
+        return send(here, here, pair[0].at[chunk], pair[1].at[chunk], place)
 
     def to_mate(chunk):
-        return onward(half, chunk, mate_out, mate_in, places[2])
-
-    def pass_near(chunk):
-        return onward(half, chunk, pass_out, pass_in, places[0])
-
-    def late_near(chunk):
-        return onward(1 - half, chunk, late_out, late_in, places[0])
+        return onward(mine, chunk, mate_sems, places[2])
+
+    def to_other(chunk):
+        return onward(mine, chunk, other_sems, places[3])
+
+    def relay(chunk):
+        if chunk % 2 == 0:
+            return onward(others, chunk, relay_sems, places[2])
+        return onward(mates, chunk, relay_sems, places[3])
+
+    def passing(number, chunk):
+        which = (mine, mates, others, across)[number]
+        return onward(which, chunk, pass_sems[number], places[0])
 
     def own():
         return pltpu.make_async_copy(packed, gathered.at[t], own_sem.at[0])
@@ -223,47 +239,61 @@
     def begin():
         for place in places:
             pl.semaphore_signal(barrier, inc=1, device_id=place, device_id_type=MESH)
+
+    def forward(chunk):
+        to_far(chunk).wait_recv()
+        to_mate(chunk).start()
+        to_other(chunk).start()
+        passing(0, chunk).start()
+
+    def cross(chunk):
+        to_mate(chunk).wait_recv()
+        to_other(chunk).wait_recv()
+        relay(chunk).start()
+        passing(1, chunk).start()
+        passing(2, chunk).start()
+
+    def close(chunk):
+        relay(chunk).wait_recv()
+        passing(3, chunk).start()
+
+    plan = {
+        3: ((forward, 0),),
+        4: ((forward, 1),),
+        5: ((forward, 2), (forward, 3)),
+        6: ((cross, 0), (forward, 4)),
+        7: ((cross, 1), (cross, 2)),
+        8: ((cross, 3), (close, 0), (close, 1)),
+        9: ((cross, 4), (close, 2), (close, 3)),
+    }
 
     def go_on():
         @pl.when(step == 0)
         def _():
             own().start()
             pl.semaphore_wait(barrier, len(places))
-            to_far(0).start()
-            to_far(1).start()
+            for chunk in range(CHUNKS):
+                to_far(chunk).start()
             to_near().start()
 
-        for chunk, when in ((2, 2), (3, 4), (4, 5)):
+        for when, moves in plan.items():
 
             @pl.when(step == when)
-            def _(chunk=chunk):
-                to_far(chunk).start()
-
-        @pl.when((step >= TILES) & (step < TILES + chunks))
-        def _():
-            chunk = step - TILES
-            to_far(chunk).wait_recv()
-            to_mate(chunk).start()
-            pass_near(chunk).start()
-
-        @pl.when((step >= TILES + 2) & (step < TILES + 1 + chunks))
-        def _():
-            chunk = step - TILES - 2
-            to_mate(chunk).wait_recv()
-            late_near(chunk).start()
+            def _(moves=moves):
+                for move, chunk in moves:
+                    move(chunk)
 
     def finish():
-        to_mate(chunks - 1).wait_recv()
-        late_near(chunks - 1).start()
+        close(CHUNKS - 1)
         own().wait()
         to_near().wait()
-        for chunk in range(chunks):
-            pass_near(chunk).wait_recv()
-            late_near(chunk).wait_recv()
+        for chunk in range(CHUNKS):
+            for number in range(4):
+                passing(number, chunk).wait()
             to_far(chunk).wait_send()
             to_mate(chunk).wait_send()
-            pass_near(chunk).wait_send()
-            late_near(chunk).wait_send()
+            to_other(chunk).wait_send()
+            relay(chunk).wait_send()
 
     return begin, go_on, finish
 
@@ -563,10 +593,9 @@
     lengths, counts, tokens, qkv_weight, rel_embed, index_rows, down, up, hidden_up, hidden_down,
     adapt_scale, out_weight, in_weight, back_weight,
 ):
-    chunks = HALF // CHUNK
-    single, several = (pltpu.SemaphoreType.DMA((n,)) for n in (1, chunks))
+    single, several = (pltpu.SemaphoreType.DMA((n,)) for n in (1, CHUNKS))
     inner = lax.axis_size("tensor")
-    assert inner == 4 and lax.axis_size("dp") % 2 == 0
+    assert inner == 4 and lax.axis_size("dp") % 4 == 0
 
     def tile_at(i):
         return jnp.minimum(i, TILES - 1)
@@ -634,7 +663,7 @@
             pltpu.SemaphoreType.DMA((1,)),
         ]
         + [single] * 2
-        + [several] * 8,
+        + [several] * 16,
         compiler_params=pltpu.CompilerParams(
             collective_id=1, has_side_effects=True, vmem_limit_bytes=MEMORY
         ),
@@ -1391,6 +1420,30 @@
     )
 
 
+def finish_kernel(*refs):
+    half = len(refs) // 2
+    refs[half][...] = refs[0][...]
+
+    @pl.when(pl.program_id(0) == 0)
+    def _():
+        for src, dst in zip(refs[1:half], refs[half + 1 :]):
+            dst[...] = src[...]
+
+
+def finish(in_grad, *small):
+    tile = pl.BlockSpec((BLOCK, D), lambda i: (i, 0))
+    specs = [tile] + [whole(*part.shape) for part in small]
+    return pl.pallas_call(
+        finish_kernel,
+        grid=(ROWS // BLOCK,),
+        in_specs=specs,
+        out_specs=specs,
+        out_shape=[jax.ShapeDtypeStruct(part.shape, part.dtype) for part in (in_grad, *small)],
+        compiler_params=pltpu.CompilerParams(vmem_limit_bytes=MEMORY),
+        name="finish",
+    )(in_grad, *small)
+
+
 def on_device(
     tokens,
     qkv_weight,
@@ -1426,11 +1479,11 @@
     gq, gk, gv, geq, gfk = attend_backward(
         q, k, v, context_grad, context, eq, fk, p1, p2, p3
     )
-    in_grad, down_grad, up_grad, hidden_up_grad, hidden_down_grad, scale_grad = last(
+    sums = last(
         tokens, gq, gk, gv, grad_one, coeff, weights, index_rows, rel_coeff, factors, scales,
         small, hidden, middle_scale, rel_embed, geq, gfk,
     )
-    return (mixed, in_grad, down_grad, up_grad, hidden_up_grad, hidden_down_grad, scale_grad)
+    return (mixed, *finish(*sums))
 
 
 def solution(mesh):

time: 171 us -> 166 us (0.971)
  local copies, waits for them, and re-layouts: 8.5 us -> 1.44 us
  Pallas kernels: 160 us -> 162 us
    unnamed x18 -> x2, local copies, waits for them, and re-layouts: 7.9 us -> 0.83 us
    pallas_call x0 -> x1, Pallas kernels: none -> 4.58 us  [finish(): pl.pallas_call(finish_kernel, grid=(ROWS // BLOCK,), in_specs=specs, out_...]
    pallas_call x1, Pallas kernels: 50.1 us -> 47.7 us  [front(): pl.pallas_call(front_kernel, grid=(TILES + H // 2,), in_specs=[pl.BlockSp...]
where the time goes in v7:
time: 166 us; the launch traced here: 165 us
  Pallas kernels  162 us (98%)
    pallas_call x1, Pallas kernels, front(): pl.pallas_call(front_kernel, grid=(TILES + H // 2,), in_specs=[pl.BlockSp...  47.7 us
    pallas_call x1, Pallas kernels, middle(): pl.pallas_call(middle_kernel, grid=(ROWS // WIDE,), in_specs=[pl.BlockSpe...  45.3 us
    pallas_call x1, Pallas kernels, attend_backward(): pl.pallas_call(backward_kernel, grid=(H // 2,), in_specs=[PAIR_SPEC] * 7...  38.2 us
    pallas_call x1, Pallas kernels, last(): pl.pallas_call(last_kernel, grid=(1 + TILES,), in_specs=[tile, once(3, PA...  25.7 us
    pallas_call x1, Pallas kernels, finish(): pl.pallas_call(finish_kernel, grid=(ROWS // BLOCK,), in_specs=specs, out_...  4.58 us

profile of v7, /device:TPU:0, one launch (start us, length us, event | category | flops | bytes accessed | tf_op | source)
XLA Modules:
  0.0 164.6 jit_solution(194012489959942750)
XLA Ops:
  0.6 0.8 reverse
  1.4 0.1 slice
  1.5 0.7 pad_add_fusion
  2.2 0.6 pad.4.index_ref
  2.8 47.7 %front.1 = (bf16[1024,768]{1,0:T(8,128)(2,1)}, bf16[1024,768]{1,0:T(8,128)(2,1)}, f32[3,16,1024]{2,1,0:T(8,128)}, f32[2,16,512]{2,1,0:T(8,128)}, bf16[12,16,768]...) custom-call(s32[1,4]{1,0:T(1,128)} %lengths_ref.3, ...), custom_call_target="tpu_custom_call" | custom-call | tf_op jit(solution)/shard_map/front/pallas_call | solution.py:609
  50.5 45.3 %middle.1 = (bf16[1024,768]{1,0:T(8,128)(2,1)}, f32[1024,768]{1,0:T(8,128)}, bf16[1024,768]{1,0:T(8,128)(2,1)}, f32[4,16,768]{2,1,0:T(8,128)}, f32[8,16,768]{2,1,0:T(8,128)}, /*index=5*/f32[16,128]{1,0:T(8,128)}) custom-call(s32[1,4]{1,0:T(1,128)} %lengths_ref.3, s32[1,3]{1,0:T(1,128)} %counts_ref.3, bf16[1024,768]{1,0:T(8,128)(2,1)} %tokens_any.1, ...), custom_call_target="tpu_custom_call" | custom-call | tf_op jit(solution)/shard_map/middle/pallas_call | solution.py:981
  95.8 38.2 %attention_backward.1 = (bf16[1024,768]{1,0:T(8,128)(2,1)}, bf16[1024,768]{1,0:T(8,128)(2,1)}, bf16[1024,768]{1,0:T(8,128)(2,1)}, bf16[768,1024]{1,0:T(8,128)(2,1)}, bf16[768,1024]{1,0:T(8,128)(2,1)}) custom-call(bf16[1024,768]{1,0:T(8,128)(2,1)} %get-tuple-element.57.q_ref, bf16[1024,768]{1,0:T(8,128)(2,1)} %get-tuple-element.58.k_ref, ...), custom_call_target="tpu_custom_call" | custom-call | tf_op jit(solution)/shard_map/attention_backward/pallas_call | solution.py:810
  134.1 25.7 %last.1 = (f32[1024,768]{1,0:T(8,128)}, f32[5,12,768]{2,1,0:T(8,128)}, f32[5,12,768]{2,1,0:T(8,128)}, f32[12,768]{1,0:T(8,128)}, f32[12,768]{1,0:T(8,128)}, /*index=5*/f32[6,12]{1,0:T(8,128)}) custom-call(f32[1024,768]{1,0:T(8,128)} %get-tuple-element.51.grad_one_ref, f32[3,16,1024]{2,1,0:T(8,128)} %get-tuple-element.52.coeff_ref, s32[2,1024]{1,0:T(2,128)} %pad.4.index_ref, ...), custom_call_target="tpu_custom_call" | custom-call | tf_op jit(solution)/shard_map/last/pallas_call | solution.py:1358
  159.8 4.6 %finish.1 = (f32[1024,768]{1,0:T(8,128)}, f32[5,12,768]{2,1,0:T(8,128)}, f32[5,12,768]{2,1,0:T(8,128)}, f32[12,768]{1,0:T(8,128)}, f32[12,768]{1,0:T(8,128)}, /*index=5*/f32[6,12]{1,0:T(8,128)}) custom-call(f32[1024,768]{1,0:T(8,128)} %get-tuple-element.71.refs_0_, f32[5,12,768]{2,1,0:T(8,128)} %get-tuple-element.72.refs_1_, ...), custom_call_target="tpu_custom_call" | custom-call | tf_op jit(solution)/shard_map/finish/pallas_call | solution.py:1436

commit v8 on v7

--- a/solution.py
+++ b/solution.py
@@ -414,11 +414,26 @@
         context_unit(slot)
 
 
+def reversed_buckets(row):
+    wide = row.astype(f32) + 1.0
+    blocks = jnp.concatenate(
+        [wide[:, at : at + LANES] for at in range(OFFSETS - LANES, -1, -LANES)], axis=0
+    )
+    high = jnp.floor(blocks * 0.5)
+    both = jnp.concatenate([high, blocks - 2.0 * high], axis=0).astype(bf16)
+    turned = dot_nn(both, unit_matrix(True))
+    count = OFFSETS // LANES
+    value = 2.0 * turned[:count] + turned[count:]
+    line = jnp.concatenate([value[at : at + 1, :] for at in range(count)], axis=1)
+    line = pltpu.roll(jnp.broadcast_to(line, (8, OFFSETS)), OFFSETS - 1, 1)[:1]
+    return (line - 1.0).astype(jnp.int32)
+
+
 def front_kernel(
     lengths_ref,
     counts_ref,
     tokens_ref,
-    index_ref,
+    bucket_ref,
     down_ref,
     up_ref,
     hidden_up_ref,
@@ -435,6 +450,7 @@
     rel_coeff_ref,
     factor_ref,
     scale_ref,
+    index_ref,
     context_ref,
     p1_ref,
     p2_ref,
@@ -513,6 +529,8 @@
 
     @pl.when(step == 0)
     def _():
+        index_ref[0:1, :] = reversed_buckets(bucket_ref[...].reshape(1, OFFSETS))
+        index_ref[1:2, :] = bucket_ref[...].reshape(1, OFFSETS)
         loads[2].wait()
         for member in range(3):
             merged_scr[member] = merged(
@@ -543,7 +561,7 @@
         coeff_ref[...] = coeff.reshape(3, PAD, BLOCK)
         bucket = lax.broadcasted_iota(jnp.int32, (2 * SPAN, BLOCK), 0)
         back, forth = (
-            jnp.where(bucket == index_ref[row : row + 1, :], 1.0, 0.0).astype(bf16)
+            jnp.where(bucket == index_ref[row : row + 1, rows], 1.0, 0.0).astype(bf16)
             for row in range(2)
         )
         eq_ref[...] = dot_tn(back, pos_scr[0]).astype(bf16)
@@ -590,7 +608,7 @@
 
 
 def front(
-    lengths, counts, tokens, qkv_weight, rel_embed, index_rows, down, up, hidden_up, hidden_down,
+    lengths, counts, tokens, qkv_weight, rel_embed, buckets, down, up, hidden_up, hidden_down,
     adapt_scale, out_weight, in_weight, back_weight,
 ):
     single, several = (pltpu.SemaphoreType.DMA((n,)) for n in (1, CHUNKS))
@@ -612,7 +630,7 @@
         in_specs=[pl.BlockSpec(memory_space=pltpu.SMEM)] * 2
         + [
             tile,
-            pl.BlockSpec((2, BLOCK), lambda i: (0, tile_at(i))),
+            once(OFFSETS),
             once(5, RANK, D),
             once(5, RANK, D),
             once(RANK, D),
@@ -626,6 +644,7 @@
             whole(2, PAD, 2 * SPAN),
             whole(12, PAD, D),
             whole(PAD, LANES),
+            whole(2, OFFSETS),
             pl.BlockSpec((ROWS, PAIR), lambda i: (0, pair_at(i))),
         ]
         + [pl.BlockSpec((2, *size), lambda i: (pair_at(i), 0, 0)) for size in PROB_SIZES]
@@ -636,6 +655,7 @@
             jax.ShapeDtypeStruct((2, PAD, 2 * SPAN), f32),
             jax.ShapeDtypeStruct((12, PAD, D), bf16),
             jax.ShapeDtypeStruct((PAD, LANES), f32),
+            jax.ShapeDtypeStruct((2, OFFSETS), jnp.int32),
             rows,
         ]
         + [jax.ShapeDtypeStruct((H, *size), bf16) for size in PROB_SIZES]
@@ -669,7 +689,7 @@
         ),
         name="front",
     )(
-        lengths, counts, tokens, index_rows, down, up, hidden_up, hidden_down, adapt_scale,
+        lengths, counts, tokens, buckets, down, up, hidden_up, hidden_down, adapt_scale,
         in_weight, back_weight, qkv_weight, rel_embed, out_weight,
     )
 
@@ -781,10 +801,10 @@
         gfk_scr[:, window] += dot_tn(each_head(q_ref[rows, :]), spread)
 
     first, second = slot_tiles(3), slot_tiles(2) + slot_tiles(1) + slot_tiles(0)
-    jobs = [("key", unit) for unit in first]
-    for one, other in zip(second, first):
+    jobs = [("key", unit) for unit in second]
+    for one, other in zip(first, second):
         jobs += [("key", one), ("query", other)]
-    jobs += [("query", unit) for unit in second]
+    jobs += [("query", unit) for unit in first]
     held = {}
     for at in range(len(jobs) + 2):
         if at < len(jobs):
@@ -1465,12 +1485,13 @@
     rel_bucket,
     out_grad,
 ):
-    index_rows = jnp.pad(
-        jnp.stack([rel_bucket[::-1], rel_bucket]), ((0, 0), (0, 1)), constant_values=-1
-    )
+    buckets = jnp.pad(rel_bucket, (0, 1), constant_values=-1)
     norms = (gain_one, shift_one, gain_two, shift_two)
-    eq, fk, coeff, rel_coeff, factors, scales, context, p1, p2, p3, q, k, v, weights, gathered = front(
-        seq_lengths, seq_counts, tokens, qkv_weight, rel_embed, index_rows, adapt_down, adapt_up,
+    (
+        eq, fk, coeff, rel_coeff, factors, scales, index_rows, context, p1, p2, p3, q, k, v, weights,
+        gathered,
+    ) = front(
+        seq_lengths, seq_counts, tokens, qkv_weight, rel_embed, buckets, adapt_down, adapt_up,
         hidden_up, hidden_down, adapt_scale, out_weight, in_weight, back_weight,
     )
     mixed, grad_one, context_grad, small, hidden, middle_scale = middle(

time: 166 us -> 163 us (0.982)
  Pallas kernels: 162 us -> 160 us
    pallas_call x1, Pallas kernels: 38.2 us -> 36.1 us  [attend_backward(): pl.pallas_call(backward_kernel, grid=(H // 2,), in_specs=[PAIR_SPEC] * 7...]
where the time goes in v8:
time: 163 us; the launch traced here: 162 us
  Pallas kernels  160 us (98%)
    pallas_call x1, Pallas kernels, front(): pl.pallas_call(front_kernel, grid=(TILES + H // 2,), in_specs=[pl.BlockSp...  48 us
    pallas_call x1, Pallas kernels, middle(): pl.pallas_call(middle_kernel, grid=(ROWS // WIDE,), in_specs=[pl.BlockSpe...  45.4 us
    pallas_call x1, Pallas kernels, attend_backward(): pl.pallas_call(backward_kernel, grid=(H // 2,), in_specs=[PAIR_SPEC] * 7...  36.1 us
    pallas_call x1, Pallas kernels, last(): pl.pallas_call(last_kernel, grid=(1 + TILES,), in_specs=[tile, once(3, PA...  25.7 us
    pallas_call x1, Pallas kernels, finish(): pl.pallas_call(finish_kernel, grid=(ROWS // BLOCK,), in_specs=specs, out_...  4.58 us

profile of v8, /device:TPU:0, one launch (start us, length us, event | category | flops | bytes accessed | tf_op | source)
XLA Modules:
  0.0 161.9 jit_solution(6663300744500835435)
XLA Ops:
  0.6 1.3 pad.4.bucket_ref
  1.9 48.0 %front.1 = (bf16[1024,768]{1,0:T(8,128)(2,1)}, bf16[1024,768]{1,0:T(8,128)(2,1)}, f32[3,16,1024]{2,1,0:T(8,128)}, f32[2,16,512]{2,1,0:T(8,128)}, bf16[12,16,768]...) custom-call(s32[1,4]{1,0:T(1,128)} %lengths_ref.3, ...), custom_call_target="tpu_custom_call" | custom-call | tf_op jit(solution)/shard_map/front/pallas_call | solution.py:627
  49.9 45.4 %middle.1 = (bf16[1024,768]{1,0:T(8,128)(2,1)}, f32[1024,768]{1,0:T(8,128)}, bf16[1024,768]{1,0:T(8,128)(2,1)}, f32[4,16,768]{2,1,0:T(8,128)}, f32[8,16,768]{2,1,0:T(8,128)}, /*index=5*/f32[16,128]{1,0:T(8,128)}) custom-call(s32[1,4]{1,0:T(1,128)} %lengths_ref.3, s32[1,3]{1,0:T(1,128)} %counts_ref.3, bf16[1024,768]{1,0:T(8,128)(2,1)} %tokens_any.1, ...), custom_call_target="tpu_custom_call" | custom-call | tf_op jit(solution)/shard_map/middle/pallas_call | solution.py:1001
  95.2 36.1 %attention_backward.1 = (bf16[1024,768]{1,0:T(8,128)(2,1)}, bf16[1024,768]{1,0:T(8,128)(2,1)}, bf16[1024,768]{1,0:T(8,128)(2,1)}, bf16[768,1024]{1,0:T(8,128)(2,1)}, bf16[768,1024]{1,0:T(8,128)(2,1)}) custom-call(bf16[1024,768]{1,0:T(8,128)(2,1)} %get-tuple-element.59.q_ref, bf16[1024,768]{1,0:T(8,128)(2,1)} %get-tuple-element.60.k_ref, ...), custom_call_target="tpu_custom_call" | custom-call | tf_op jit(solution)/shard_map/attention_backward/pallas_call | solution.py:830
  131.4 25.7 %last.1 = (f32[1024,768]{1,0:T(8,128)}, f32[5,12,768]{2,1,0:T(8,128)}, f32[5,12,768]{2,1,0:T(8,128)}, f32[12,768]{1,0:T(8,128)}, f32[12,768]{1,0:T(8,128)}, /*index=5*/f32[6,12]{1,0:T(8,128)}) custom-call(f32[1024,768]{1,0:T(8,128)} %get-tuple-element.52.grad_one_ref, f32[3,16,1024]{2,1,0:T(8,128)} %get-tuple-element.53.coeff_ref, ...), custom_call_target="tpu_custom_call" | custom-call | tf_op jit(solution)/shard_map/last/pallas_call | solution.py:1378
  157.1 4.6 %finish.1 = (f32[1024,768]{1,0:T(8,128)}, f32[5,12,768]{2,1,0:T(8,128)}, f32[5,12,768]{2,1,0:T(8,128)}, f32[12,768]{1,0:T(8,128)}, f32[12,768]{1,0:T(8,128)}, /*index=5*/f32[6,12]{1,0:T(8,128)}) custom-call(f32[1024,768]{1,0:T(8,128)} %get-tuple-element.73.refs_0_, f32[5,12,768]{2,1,0:T(8,128)} %get-tuple-element.74.refs_1_, ...), custom_call_target="tpu_custom_call" | custom-call | tf_op jit(solution)/shard_map/finish/pallas_call | solution.py:1456

commit v9 on v8

--- a/solution.py
+++ b/solution.py
@@ -24,7 +24,7 @@
 CHUNKS = 5
 CHUNK = QUARTER // CHUNKS
 TILES = ROWS // BLOCK
-SUMMED = 2
+SUMMED = 1
 WIDE = 1 * BLOCK
 LAG = 1
 LANES = 128

time: 163 us -> 163 us (level)
  no operation moved by 1% of the time
where the time goes in v9:
time: 163 us
  Pallas kernels  161 us (99%)
    pallas_call x1, Pallas kernels, front(): pl.pallas_call(front_kernel, grid=(TILES + H // 2,), in_specs=[pl.BlockSp...  48 us
    pallas_call x1, Pallas kernels, middle(): pl.pallas_call(middle_kernel, grid=(ROWS // WIDE,), in_specs=[pl.BlockSpe...  45.4 us
    pallas_call x1, Pallas kernels, attend_backward(): pl.pallas_call(backward_kernel, grid=(H // 2,), in_specs=[PAIR_SPEC] * 7...  36.1 us
    pallas_call x1, Pallas kernels, last(): pl.pallas_call(last_kernel, grid=(1 + TILES,), in_specs=[tile, once(3, PA...  26.5 us
    pallas_call x1, Pallas kernels, finish(): pl.pallas_call(finish_kernel, grid=(ROWS // BLOCK,), in_specs=specs, out_...  4.58 us

profile of v9, /device:TPU:0, one launch (start us, length us, event | category | flops | bytes accessed | tf_op | source)
XLA Modules:
  0.0 162.7 jit_solution(17774317596072957600)
XLA Ops:
  0.6 1.3 pad.4.bucket_ref
  1.9 48.0 %front.1 = (bf16[1024,768]{1,0:T(8,128)(2,1)}, bf16[1024,768]{1,0:T(8,128)(2,1)}, f32[3,16,1024]{2,1,0:T(8,128)}, f32[2,16,512]{2,1,0:T(8,128)}, bf16[12,16,768]...) custom-call(s32[1,4]{1,0:T(1,128)} %lengths_ref.3, ...), custom_call_target="tpu_custom_call" | custom-call | tf_op jit(solution)/shard_map/front/pallas_call | solution.py:627
  49.9 45.4 %middle.1 = (bf16[1024,768]{1,0:T(8,128)(2,1)}, f32[1024,768]{1,0:T(8,128)}, bf16[1024,768]{1,0:T(8,128)(2,1)}, f32[4,16,768]{2,1,0:T(8,128)}, f32[8,16,768]{2,1,0:T(8,128)}, /*index=5*/f32[16,128]{1,0:T(8,128)}) custom-call(s32[1,4]{1,0:T(1,128)} %lengths_ref.3, s32[1,3]{1,0:T(1,128)} %counts_ref.3, bf16[1024,768]{1,0:T(8,128)(2,1)} %tokens_any.1, ...), custom_call_target="tpu_custom_call" | custom-call | tf_op jit(solution)/shard_map/middle/pallas_call | solution.py:1001
  95.2 36.1 %attention_backward.1 = (bf16[1024,768]{1,0:T(8,128)(2,1)}, bf16[1024,768]{1,0:T(8,128)(2,1)}, bf16[1024,768]{1,0:T(8,128)(2,1)}, bf16[768,1024]{1,0:T(8,128)(2,1)}, bf16[768,1024]{1,0:T(8,128)(2,1)}) custom-call(bf16[1024,768]{1,0:T(8,128)(2,1)} %get-tuple-element.59.q_ref, bf16[1024,768]{1,0:T(8,128)(2,1)} %get-tuple-element.60.k_ref, ...), custom_call_target="tpu_custom_call" | custom-call | tf_op jit(solution)/shard_map/attention_backward/pallas_call | solution.py:830
  131.4 26.5 %last.1 = (f32[1024,768]{1,0:T(8,128)}, f32[5,12,768]{2,1,0:T(8,128)}, f32[5,12,768]{2,1,0:T(8,128)}, f32[12,768]{1,0:T(8,128)}, f32[12,768]{1,0:T(8,128)}, /*index=5*/f32[6,12]{1,0:T(8,128)}) custom-call(f32[1024,768]{1,0:T(8,128)} %get-tuple-element.52.grad_one_ref, f32[3,16,1024]{2,1,0:T(8,128)} %get-tuple-element.53.coeff_ref, ...), custom_call_target="tpu_custom_call" | custom-call | tf_op jit(solution)/shard_map/last/pallas_call | solution.py:1378
  157.9 4.6 %finish.1 = (f32[1024,768]{1,0:T(8,128)}, f32[5,12,768]{2,1,0:T(8,128)}, f32[5,12,768]{2,1,0:T(8,128)}, f32[12,768]{1,0:T(8,128)}, f32[12,768]{1,0:T(8,128)}, /*index=5*/f32[6,12]{1,0:T(8,128)}) custom-call(f32[1024,768]{1,0:T(8,128)} %get-tuple-element.73.refs_0_, f32[5,12,768]{2,1,0:T(8,128)} %get-tuple-element.74.refs_1_, ...), custom_call_target="tpu_custom_call" | custom-call | tf_op jit(solution)/shard_map/finish/pallas_call | solution.py:1456
